TPU v7x, 512 devices: a whole 4x8x8 slice. The times are simulated.
512 devices in a mesh: gx: 64 (over z_hi, y, core), gy: 8 (over x, z_lo).
Axes of the slice: x: 4, y: 8, z: 8 (z_hi: 4, z_lo: 2; z = z_hi * 2 + z_lo), core: 2. Of those that a mesh axis runs over, the one named last changes fastest.
Arguments:
- velocity: float32 [3, 1024, 128, 128], P(None, 'gx', 'gy'), may hold values from -6 to 6
- pressure: float32 [1024, 128, 128], P('gx', 'gy'), may hold values from -6 to 6
- land_type: int32 [1024, 128], P('gx', 'gy'), may hold values from 0 to 15
- turbine_cells: int32 [1024, 128, 128], P('gx', 'gy'), may hold values 0 or 1
- surface_drag: float32 [16], replicated, may hold values from 0.2 to 2
Outputs:
- velocity_new: float32 [3, 1024, 128, 128], P(None, 'gx', 'gy')
- pressure_new: float32 [1024, 128, 128], P('gx', 'gy')
All inputs are finite; a program needn't handle non-finite values. No bound on the sum of `turbine_cells` on one device may be relied on, other than what follows from the above.
Results may differ from a plain program's by a relative error of at most 0.00002.
Values sent between devices are 32-bit elements; how exact they have to be, the bound alone decides.
No kernel may reach another device: no remote copies, remote signals or barrier semaphores. Data moves between devices by JAX's collectives and lax.ppermute only.
A program may use at most 64 MiB of HBM per device.

v0:
```python
import jax
import jax.numpy as jnp
from jax import lax
from jax.sharding import PartitionSpec as P

SWEEPS = 2
COARSE_SWEEPS = 4


time_step = 0.1
vertical_step = 0.5
eddy_coeff = 0.03
thrust_factor = 2.0
relax_weight = 0.8
driving_force = 1.0


def padded_2(shard, sides, width):
    edges = {}
    for axis, dim in sides:
        peers, length = (lax.axis_size(axis), shard.shape[dim])
        up = [(i, (i + 1) % peers) for i in range(peers)]
        last = lax.slice_in_dim(shard, length - width, length, axis=dim)
        initial = lax.slice_in_dim(shard, 0, width, axis=dim)
        edges[dim] = (
            lax.ppermute(last, axis, up),
            lax.ppermute(initial, axis, [(b, a) for a, b in up]),
        )
    done = []
    for _, dim in sides:
        low, high = edges[dim]
        around = [(width, width) if d in done else (0, 0) for d in range(shard.ndim)]
        shard = jnp.concatenate([jnp.pad(low, around), shard, jnp.pad(high, around)], axis=dim)
        done.append(dim)
    return shard


def with_halo(block, sides, width):
    for axis, dim in sides:
        count = lax.axis_size(axis)
        forward = [(i, i + 1) for i in range(count - 1)]
        forward.append((count - 1, 0))
        backward = [(target, source) for source, target in forward]
        low = lax.ppermute(
            lax.slice_in_dim(block, block.shape[dim] - width, None, axis=dim), axis, forward
        )
        high = lax.ppermute(lax.slice_in_dim(block, 0, width, axis=dim), axis, backward)
        block = jnp.concatenate([low, block, high], axis=dim)
    return block


def sent_to_all(shard, axis):
    peers = lax.axis_size(axis)
    return lax.all_to_all(
        jnp.broadcast_to(shard[None], (peers, *shard.shape)), axis, 0, 0, tiled=True
    )


def in_order(pieces, dim):
    pieces = jnp.moveaxis(pieces, 0, dim)
    shape = pieces.shape
    return pieces.reshape(*shape[:dim], shape[dim] * shape[dim + 1], *shape[dim + 2 :])


def collect(shard, axis, dim):
    pieces = sent_to_all(shard, axis)
    return in_order(pieces, dim)


def shifted(values, axis_pos, offset):
    starts = [1, 1, 1]
    starts[axis_pos] = 1 + offset
    length = [values.shape[-3] - 2, values.shape[-2] - 2, values.shape[-1] - 2]
    return values[
        ...,
        starts[0] : starts[0] + length[0],
        starts[1] : starts[1] + length[1],
        starts[2] : starts[2] + length[2],
    ]


def central(values, axis_pos):
    spacing = vertical_step if axis_pos == 2 else 1.0
    return (shifted(values, axis_pos, 1) - shifted(values, axis_pos, -1)) * (0.5 / spacing)


def surface_field(land_type, turbine_cells, surface_drag):
    kind_ids = jnp.arange(surface_drag.shape[0], dtype=jnp.int32)
    ground = jnp.sum(jnp.where(land_type[:, :, None] == kind_ids, surface_drag, 0.0), axis=-1)
    ground_layer = jnp.arange(turbine_cells.shape[2], dtype=jnp.int32) == 0
    return thrust_factor * turbine_cells.astype(jnp.float32) + jnp.where(
        ground_layer, ground[:, :, None], 0.0
    )


def advance(padded, drag_field):
    gradient = [central(padded, axis_pos) for axis_pos in range(3)]
    strain = [
        [0.5 * (gradient[col_idx][row_idx] + gradient[row_idx][col_idx]) for col_idx in range(3)]
        for row_idx in range(3)
    ]
    square_sum = strain[0][0] * strain[0][0]
    for row_idx in range(3):
        for col_idx in range(3):
            if row_idx + col_idx > 0:
                square_sum = square_sum + strain[row_idx][col_idx] * strain[row_idx][col_idx]
    viscosity = eddy_coeff * jnp.sqrt(2.0 * square_sum)
    centre = padded[:, 2:-2, 2:-2, 2:-2]
    wind_speed = jnp.sqrt(centre[0] * centre[0] + centre[1] * centre[1])
    updated = []
    for row_idx in range(3):
        change = jnp.zeros_like(centre[0])
        for col_idx in range(3):
            stress = 2.0 * viscosity * strain[row_idx][col_idx]
            change = (
                change
                + central(stress, col_idx)
                - centre[col_idx] * gradient[col_idx][row_idx][1:-1, 1:-1, 1:-1]
            )
        if row_idx < 2:
            change = change - drag_field * wind_speed * centre[row_idx]
        if row_idx == 0:
            change = change + driving_force
        updated.append(centre[row_idx] + time_step * change)
    return jnp.stack(updated)


def divergence(padded):
    return central(padded[0], 0) + central(padded[1], 1) + central(padded[2], 2)


def laplace(padded, spacing):
    centre = padded[1:-1, 1:-1, 1:-1]
    upright = vertical_step * spacing
    horizontal = (
        shifted(padded, 0, 1)
        + shifted(padded, 0, -1)
        + shifted(padded, 1, 1)
        + shifted(padded, 1, -1)
        - 4.0 * centre
    ) / (spacing * spacing)
    vertical = (shifted(padded, 2, 1) + shifted(padded, 2, -1) - 2.0 * centre) / (upright * upright)
    return horizontal + vertical


def diagonal_of(spacing):
    upright = vertical_step * spacing
    return -(4.0 / (spacing * spacing) + 2.0 / (upright * upright))


def relax(pressure, padded, source, spacing):
    return pressure + relax_weight * (source - laplace(padded, spacing)) / diagonal_of(spacing)


def line_correct(pressure, residual, spacing):
    return pressure + relax_weight * jnp.mean(residual, axis=1, keepdims=True) / diagonal_of(
        spacing
    )


def coarsen(values):
    return values.reshape(
        values.shape[0] // 2, 2, values.shape[1] // 2, 2, values.shape[2] // 2, 2
    ).mean(axis=(1, 3, 5))


def refine(values):
    return jnp.repeat(jnp.repeat(jnp.repeat(values, 2, axis=0), 2, axis=1), 2, axis=2)


def faces(values):
    padded = padded_2(values, (("gx", 0), ("gy", 1)), 1)
    return jnp.pad(padded, ((0, 0), (0, 0), (1, 1)), mode="edge")


def strip(values):
    padded = with_halo(values, (("gx", 0),), 1)
    padded = jnp.pad(padded, ((0, 0), (1, 1), (0, 0)), mode="wrap")
    return jnp.pad(padded, ((0, 0), (0, 0), (1, 1)), mode="edge")


def smooth(pressure, source, spacing, padder, count):
    for sweep_idx in range(count):
        pressure = relax(pressure, padder(pressure), source, spacing)
    return pressure


def residual_of(pressure, source, spacing, padder):
    return source - laplace(padder(pressure), spacing)


def per_device(velocity, pressure, land_type, turbine_cells, surface_drag):
    drag_field = surface_field(land_type, turbine_cells, surface_drag)
    stacked = jnp.concatenate([velocity, drag_field[None]], 0)
    widened = with_halo(stacked, (("gx", 1), ("gy", 2)), 3)
    moving = jnp.pad(widened[:3], ((0, 0), (0, 0), (0, 0), (2, 2)))
    star_rim = advance(moving, widened[3, 2:-2, 2:-2])
    star_velocity = star_rim[:, 1:-1, 1:-1]
    source = divergence(jnp.pad(star_rim, ((0, 0), (0, 0), (0, 0), (1, 1)))) / time_step
    finest = smooth(pressure, source, 1.0, faces, SWEEPS)
    source_one = coarsen(residual_of(finest, source, 1.0, faces))
    second = smooth(jnp.zeros_like(source_one), source_one, 2.0, faces, SWEEPS)
    local_two = coarsen(residual_of(second, source_one, 2.0, faces))
    source_two = collect(local_two, "gy", 1)
    third = smooth(jnp.zeros_like(source_two), source_two, 4.0, strip, SWEEPS)
    source_three = coarsen(residual_of(third, source_two, 4.0, strip))
    coarsest = smooth(jnp.zeros_like(source_three), source_three, 8.0, strip, COARSE_SWEEPS)
    coarsest = line_correct(coarsest, residual_of(coarsest, source_three, 8.0, strip), 8.0)
    third = smooth(third + refine(coarsest), source_two, 4.0, strip, SWEEPS)
    own_third = lax.dynamic_slice_in_dim(
        third, lax.axis_index("gy") * local_two.shape[1], local_two.shape[1], 1
    )
    second = smooth(second + refine(own_third), source_one, 2.0, faces, SWEEPS)
    pressure_new = smooth(finest + refine(second), source, 1.0, faces, SWEEPS)
    padded = faces(pressure_new)
    gradient = jnp.stack([central(padded, 0), central(padded, 1), central(padded, 2)])
    return (star_velocity - time_step * gradient, pressure_new)


def solution(mesh):
    in_specs = (
        P(None, "gx", "gy", None),
        P("gx", "gy", None),
        P("gx", "gy"),
        P("gx", "gy", None),
        P(),
    )
    out_specs = (P(None, "gx", "gy", None), P("gx", "gy", None))
    return jax.shard_map(
        per_device, mesh=mesh, in_specs=in_specs, out_specs=out_specs, check_vma=False
    )
```

profile of v0, /device:TPU:1, one launch (start us, length us, event | category | flops | bytes accessed | tf_op | source)
XLA Modules:
  0.0 381.8 jit_solution(9404161530856094721)
XLA Ops:
  0.7 7.2 %collective-permute-start.18 = (f32[8,1,64]{2,1,0:T(1,128)S(1)}, f32[8,1,64]{2,1,0:T(1,128)S(1)}, u32[]{:S(2)}, u32[]{:S(2)}) collective-permute-start(f32[8,1,64]{2,1,0:T(1,128)S(1)} %broadcast.255), channel_id=1, source_target_pairs={{1,0},{2,1},{3,2},{4,3},{5,4},{6,5},{7,6},{0,7},{9,8},{10,9},{11,1... | collective-permute-start | bytes 6152 | tf_op jit(solution)/shard_map/ppermute | solution.py:27
  9.8 5.7 %collective-permute-start.34 = (f32[1,16,16]{2,1,0:T(8,128)S(1)}, f32[1,16,16]{2,1,0:T(8,128)S(1)}, u32[]{:S(2)}, u32[]{:S(2)}) collective-permute-start(f32[1,16,16]{2,1,0:T(8,128)S(1)} %broadcast.264), channel_id=1, source_target_pairs={{8,0},{16,8},{24,16},{32,24},{40,32},{48,40},{56,48},{64,56},{72,6... | collective-permute-start | bytes 3080 | tf_op jit(solution)/shard_map/ppermute | solution.py:47
  17.4 9.3 %collective-permute-start.16 = (f32[1,8,64]{2,1,0:T(8,128)S(1)}, f32[1,8,64]{2,1,0:T(8,128)S(1)}, u32[]{:S(2)}, u32[]{:S(2)}) collective-permute-start(f32[1,8,64]{2,1,0:T(8,128)S(1)} %broadcast.254), channel_id=1, source_target_pairs={{8,0},{16,8},{24,16},{32,24},{40,32},{48,40},{56,48},{64,56},{72,6... | collective-permute-start | bytes 6152 | tf_op jit(solution)/shard_map/ppermute | solution.py:27
  33.1 1.9 collective-permute-start.5
  35.1 7.9 %collective-permute-start.4 = (f32[1,16,128]{2,1,0:T(8,128)S(1)}, f32[1,16,128]{2,1,0:T(8,128)S(1)}, u32[]{:S(2)}, u32[]{:S(2)}) collective-permute-start(f32[1,16,128]{2,1,0:T(8,128)S(1)} %get-tuple-element.82), channel_id=1, source_target_pairs={{8,0},{16,8},{24,16},{32,24},{40,32},{48,40},{56,48},{64,56},{72,6... | collective-permute-start | bytes 24584 | tf_op jit(solution)/shard_map/ppermute | solution.py:27
  43.0 5.5 %collective-permute-start.6 = (f32[16,1,128]{2,0,1:T(8,128)S(1)}, f32[16,1,128]{2,0,1:T(8,128)S(1)}, u32[]{:S(2)}, u32[]{:S(2)}) collective-permute-start(f32[16,1,128]{2,0,1:T(8,128)S(1)} %bitcast.178), channel_id=1, source_target_pairs={{1,0},{2,1},{3,2},{4,3},{5,4},{6,5},{7,6},{0,7},{9,8},{10,9},{11,1... | collective-permute-start | bytes 24584 | tf_op jit(solution)/shard_map/ppermute | solution.py:27
  48.5 1.9 collective-permute-start.7
  55.0 9.3 %collective-permute-start.1 = (f32[4,3,16,128]{3,2,1,0:T(8,128)S(1)}, f32[4,3,16,128]{3,2,1,0:T(8,128)S(1)}, u32[]{:S(2)}, u32[]{:S(2)}) collective-permute-start(f32[4,3,16,128]{3,2,1,0:T(8,128)S(1)} %get-tuple-element.45), channel_id=1, source_target_pairs={{8,0},{16,8},{24,16},{32,24},{40,32},{48,40},{56,48},{64,56},{72,6... | collective-permute-start | bytes 294920 | tf_op jit(solution)/shard_map/ppermute | solution.py:47
  64.3 5.0 %collective-permute-start.28 = (f32[1,32,32]{2,1,0:T(8,128)S(1)}, f32[1,32,32]{2,1,0:T(8,128)S(1)}, u32[]{:S(2)}, u32[]{:S(2)}) collective-permute-start(f32[1,32,32]{2,1,0:T(8,128)S(1)} %broadcast.259), channel_id=1, source_target_pairs={{8,0},{16,8},{24,16},{32,24},{40,32},{48,40},{56,48},{64,56},{72,6... | collective-permute-start | bytes 12296 | tf_op jit(solution)/shard_map/ppermute | solution.py:47
  69.6 1.9 collective-permute-start.2
  71.5 5.8 %collective-permute-start.3 = (f32[4,22,3,128]{3,0,2,1:T(4,128)S(1)}, f32[4,22,3,128]{3,0,2,1:T(4,128)S(1)}, u32[]{:S(2)}, u32[]{:S(2)}) collective-permute-start(f32[4,22,3,128]{3,0,2,1:T(4,128)S(1)} %copy.435), channel_id=1, source_target_pairs={{1,0},{2,1},{3,2},{4,3},{5,4},{6,5},{7,6},{0,7},{9,8},{10,9},{11,1... | collective-permute-start | bytes 405512 | tf_op jit(solution)/shard_map/ppermute | solution.py:47
  80.4 2.0 fusion.3
  86.8 6.2 %collective-permute-start.10 = (f32[16,1,128]{2,0,1:T(8,128)S(1)}, f32[16,1,128]{2,0,1:T(8,128)S(1)}, u32[]{:S(2)}, u32[]{:S(2)}) collective-permute-start(f32[16,1,128]{2,0,1:T(8,128)S(1)} %bitcast.181), channel_id=1, source_target_pairs={{1,0},{2,1},{3,2},{4,3},{5,4},{6,5},{7,6},{0,7},{9,8},{10,9},{11,1... | collective-permute-start | bytes 24584 | tf_op jit(solution)/shard_map/ppermute | solution.py:27
  95.0 3.2 collective-permute-start.8
  98.2 2.4 collective-permute-start.9
  100.7 3.8 collective-permute-done.9
  104.9 5.5 %collective-permute-start.14 = (f32[16,1,128]{2,0,1:T(8,128)S(1)}, f32[16,1,128]{2,0,1:T(8,128)S(1)}, u32[]{:S(2)}, u32[]{:S(2)}) collective-permute-start(f32[16,1,128]{2,0,1:T(8,128)S(1)} %bitcast.185), channel_id=1, source_target_pairs={{1,0},{2,1},{3,2},{4,3},{5,4},{6,5},{7,6},{0,7},{9,8},{10,9},{11,1... | collective-permute-start | bytes 24584 | tf_op jit(solution)/shard_map/ppermute | solution.py:27
  112.3 8.8 %collective-permute-start.12 = (f32[1,16,128]{2,1,0:T(8,128)S(1)}, f32[1,16,128]{2,1,0:T(8,128)S(1)}, u32[]{:S(2)}, u32[]{:S(2)}) collective-permute-start(f32[1,16,128]{2,1,0:T(8,128)S(1)} %get-tuple-element.75), channel_id=1, source_target_pairs={{8,0},{16,8},{24,16},{32,24},{40,32},{48,40},{56,48},{64,56},{72,6... | collective-permute-start | bytes 24584 | tf_op jit(solution)/shard_map/ppermute | solution.py:27
  125.6 9.8 %reshape.53 = f32[8,2,8,2,64,2]{5,4,3,2,1,0:T(8,128)} reshape(f32[16,16,128]{2,1,0:T(8,128)S(1)} %fusion.82) | data formatting | bytes 262144 | tf_op jit(solution)/shard_map/reshape | solution.py:162
  135.3 4.0 %reduce_sum.46 = f32[8,8,64]{2,1,0:T(8,128)S(1)} reduce(f32[8,2,8,2,64,2]{5,4,3,2,1,0:T(8,128)} %reshape.53, f32[]{:T(128)} %constant.139.clone.1), dimensions={1,3,5}, to_apply=%region_1.2 | reduce | flops 28672 | bytes 147460 | tf_op jit(solution)/shard_map/reduce_sum | solution.py:164
  139.5 5.8 %collective-permute-start.22 = (f32[8,1,64]{2,1,0:T(1,128)S(1)}, f32[8,1,64]{2,1,0:T(1,128)S(1)}, u32[]{:S(2)}, u32[]{:S(2)}) collective-permute-start(f32[8,1,64]{2,1,0:T(1,128)S(1)} %get-tuple-element.157), channel_id=1, source_target_pairs={{1,0},{2,1},{3,2},{4,3},{5,4},{6,5},{7,6},{0,7},{9,8},{10,9},{11,1... | collective-permute-start | bytes 6152 | tf_op jit(solution)/shard_map/ppermute | solution.py:27
  147.2 7.4 %collective-permute-start.20 = (f32[1,8,64]{2,1,0:T(8,128)S(1)}, f32[1,8,64]{2,1,0:T(8,128)S(1)}, u32[]{:S(2)}, u32[]{:S(2)}) collective-permute-start(f32[1,8,64]{2,1,0:T(8,128)S(1)} %get-tuple-element.159), channel_id=1, source_target_pairs={{8,0},{16,8},{24,16},{32,24},{40,32},{48,40},{56,48},{64,56},{72,6... | collective-permute-start | bytes 6152 | tf_op jit(solution)/shard_map/ppermute | solution.py:27
  158.4 5.5 %collective-permute-start.26 = (f32[8,1,64]{2,1,0:T(1,128)S(1)}, f32[8,1,64]{2,1,0:T(1,128)S(1)}, u32[]{:S(2)}, u32[]{:S(2)}) collective-permute-start(f32[8,1,64]{2,1,0:T(1,128)S(1)} %get-tuple-element.153), channel_id=1, source_target_pairs={{1,0},{2,1},{3,2},{4,3},{5,4},{6,5},{7,6},{0,7},{9,8},{10,9},{11,1... | collective-permute-start | bytes 6152 | tf_op jit(solution)/shard_map/ppermute | solution.py:27
  165.8 8.8 %collective-permute-start.24 = (f32[1,8,64]{2,1,0:T(8,128)S(1)}, f32[1,8,64]{2,1,0:T(8,128)S(1)}, u32[]{:S(2)}, u32[]{:S(2)}) collective-permute-start(f32[1,8,64]{2,1,0:T(8,128)S(1)} %get-tuple-element.155), channel_id=1, source_target_pairs={{8,0},{16,8},{24,16},{32,24},{40,32},{48,40},{56,48},{64,56},{72,6... | collective-permute-start | bytes 6152 | tf_op jit(solution)/shard_map/ppermute | solution.py:27
  174.6 2.1 collective-permute-start.25
  179.9 5.1 %all-to-all-start = ((f32[8,1,512]{2,1,0:T(1,128)}), f32[8,1,512]{2,1,0:T(1,128)S(1)}, u32[]{:S(2)}, u32[]{:S(2)}) async-start(f32[8,1,512]{2,1,0:T(1,128)} %reshape.66), calls=%async_computation | async-start | bytes 32768 | tf_op jit(solution)/shard_map/all_to_all | solution.py:54
  185.1 5.0 %all-to-all-done = f32[8,1,512]{2,1,0:T(1,128)S(1)} async-done(((f32[8,1,512]{2,1,0:T(1,128)}), f32[8,1,512]{2,1,0:T(1,128)S(1)}, u32[]{:S(2)}, u32[]{:S(2)}) %all-to-all-start) | async-done | bytes 16416 | tf_op jit(solution)/shard_map/all_to_all | solution.py:54
  191.5 9.4 %collective-permute-start.30 = (f32[1,32,32]{2,1,0:T(8,128)S(1)}, f32[1,32,32]{2,1,0:T(8,128)S(1)}, u32[]{:S(2)}, u32[]{:S(2)}) collective-permute-start(f32[1,32,32]{2,1,0:T(8,128)S(1)} %get-tuple-element.123), channel_id=1, source_target_pairs={{8,0},{16,8},{24,16},{32,24},{40,32},{48,40},{56,48},{64,56},{72,6... | collective-permute-start | bytes 12296 | tf_op jit(solution)/shard_map/ppermute | solution.py:47
  204.4 8.1 %collective-permute-start.32 = (f32[1,32,32]{2,1,0:T(8,128)S(1)}, f32[1,32,32]{2,1,0:T(8,128)S(1)}, u32[]{:S(2)}, u32[]{:S(2)}) collective-permute-start(f32[1,32,32]{2,1,0:T(8,128)S(1)} %get-tuple-element.121), channel_id=1, source_target_pairs={{8,0},{16,8},{24,16},{32,24},{40,32},{48,40},{56,48},{64,56},{72,6... | collective-permute-start | bytes 12296 | tf_op jit(solution)/shard_map/ppermute | solution.py:47
  212.5 1.9 collective-permute-start.33
  216.7 8.1 %collective-permute-start.36 = (f32[1,16,16]{2,1,0:T(8,128)S(1)}, f32[1,16,16]{2,1,0:T(8,128)S(1)}, u32[]{:S(2)}, u32[]{:S(2)}) collective-permute-start(f32[1,16,16]{2,1,0:T(8,128)S(1)} %get-tuple-element.167), channel_id=1, source_target_pairs={{8,0},{16,8},{24,16},{32,24},{40,32},{48,40},{56,48},{64,56},{72,6... | collective-permute-start | bytes 3080 | tf_op jit(solution)/shard_map/ppermute | solution.py:47
  228.1 8.0 %collective-permute-start.38 = (f32[1,16,16]{2,1,0:T(8,128)S(1)}, f32[1,16,16]{2,1,0:T(8,128)S(1)}, u32[]{:S(2)}, u32[]{:S(2)}) collective-permute-start(f32[1,16,16]{2,1,0:T(8,128)S(1)} %get-tuple-element.165), channel_id=1, source_target_pairs={{8,0},{16,8},{24,16},{32,24},{40,32},{48,40},{56,48},{64,56},{72,6... | collective-permute-start | bytes 3080 | tf_op jit(solution)/shard_map/ppermute | solution.py:47
  239.4 8.0 %collective-permute-start.40 = (f32[1,16,16]{2,1,0:T(8,128)S(1)}, f32[1,16,16]{2,1,0:T(8,128)S(1)}, u32[]{:S(2)}, u32[]{:S(2)}) collective-permute-start(f32[1,16,16]{2,1,0:T(8,128)S(1)} %get-tuple-element.163), channel_id=1, source_target_pairs={{8,0},{16,8},{24,16},{32,24},{40,32},{48,40},{56,48},{64,56},{72,6... | collective-permute-start | bytes 3080 | tf_op jit(solution)/shard_map/ppermute | solution.py:47
  247.5 1.9 collective-permute-start.41
  250.8 8.0 %collective-permute-start.42 = (f32[1,16,16]{2,1,0:T(8,128)S(1)}, f32[1,16,16]{2,1,0:T(8,128)S(1)}, u32[]{:S(2)}, u32[]{:S(2)}) collective-permute-start(f32[1,16,16]{2,1,0:T(8,128)S(1)} %get-tuple-element.161), channel_id=1, source_target_pairs={{8,0},{16,8},{24,16},{32,24},{40,32},{48,40},{56,48},{64,56},{72,6... | collective-permute-start | bytes 3080 | tf_op jit(solution)/shard_map/ppermute | solution.py:47
  262.4 8.0 %collective-permute-start.44 = (f32[1,32,32]{2,1,0:T(8,128)S(1)}, f32[1,32,32]{2,1,0:T(8,128)S(1)}, u32[]{:S(2)}, u32[]{:S(2)}) collective-permute-start(f32[1,32,32]{2,1,0:T(8,128)S(1)} %get-tuple-element.119), channel_id=1, source_target_pairs={{8,0},{16,8},{24,16},{32,24},{40,32},{48,40},{56,48},{64,56},{72,6... | collective-permute-start | bytes 12296 | tf_op jit(solution)/shard_map/ppermute | solution.py:47
  273.9 8.1 %collective-permute-start.46 = (f32[1,32,32]{2,1,0:T(8,128)S(1)}, f32[1,32,32]{2,1,0:T(8,128)S(1)}, u32[]{:S(2)}, u32[]{:S(2)}) collective-permute-start(f32[1,32,32]{2,1,0:T(8,128)S(1)} %get-tuple-element.117), channel_id=1, source_target_pairs={{8,0},{16,8},{24,16},{32,24},{40,32},{48,40},{56,48},{64,56},{72,6... | collective-permute-start | bytes 12296 | tf_op jit(solution)/shard_map/ppermute | solution.py:47
  285.8 2.8 collective-permute-start.50
  288.6 2.4 collective-permute-start.51
  291.1 8.7 %collective-permute-start.48 = (f32[1,8,64]{2,1,0:T(8,128)S(1)}, f32[1,8,64]{2,1,0:T(8,128)S(1)}, u32[]{:S(2)}, u32[]{:S(2)}) collective-permute-start(f32[1,8,64]{2,1,0:T(8,128)S(1)} %get-tuple-element.141), channel_id=1, source_target_pairs={{8,0},{16,8},{24,16},{32,24},{40,32},{48,40},{56,48},{64,56},{72,6... | collective-permute-start | bytes 6152 | tf_op jit(solution)/shard_map/ppermute | solution.py:27
  303.1 4.9 %collective-permute-start.54 = (f32[8,1,64]{2,1,0:T(1,128)S(1)}, f32[8,1,64]{2,1,0:T(1,128)S(1)}, u32[]{:S(2)}, u32[]{:S(2)}) collective-permute-start(f32[8,1,64]{2,1,0:T(1,128)S(1)} %get-tuple-element.135), channel_id=1, source_target_pairs={{1,0},{2,1},{3,2},{4,3},{5,4},{6,5},{7,6},{0,7},{9,8},{10,9},{11,1... | collective-permute-start | bytes 6152 | tf_op jit(solution)/shard_map/ppermute | solution.py:27
  310.0 8.3 %collective-permute-start.52 = (f32[1,8,64]{2,1,0:T(8,128)S(1)}, f32[1,8,64]{2,1,0:T(8,128)S(1)}, u32[]{:S(2)}, u32[]{:S(2)}) collective-permute-start(f32[1,8,64]{2,1,0:T(8,128)S(1)} %get-tuple-element.137), channel_id=1, source_target_pairs={{8,0},{16,8},{24,16},{32,24},{40,32},{48,40},{56,48},{64,56},{72,6... | collective-permute-start | bytes 6152 | tf_op jit(solution)/shard_map/ppermute | solution.py:27
  322.5 5.8 %collective-permute-start.58 = (f32[16,1,128]{2,0,1:T(8,128)S(1)}, f32[16,1,128]{2,0,1:T(8,128)S(1)}, u32[]{:S(2)}, u32[]{:S(2)}) collective-permute-start(f32[16,1,128]{2,0,1:T(8,128)S(1)} %bitcast.186), channel_id=1, source_target_pairs={{1,0},{2,1},{3,2},{4,3},{5,4},{6,5},{7,6},{0,7},{9,8},{10,9},{11,1... | collective-permute-start | bytes 24584 | tf_op jit(solution)/shard_map/ppermute | solution.py:27
  330.2 8.3 %collective-permute-start.56 = (f32[1,16,128]{2,1,0:T(8,128)S(1)}, f32[1,16,128]{2,1,0:T(8,128)S(1)}, u32[]{:S(2)}, u32[]{:S(2)}) collective-permute-start(f32[1,16,128]{2,1,0:T(8,128)S(1)} %get-tuple-element.71), channel_id=1, source_target_pairs={{8,0},{16,8},{24,16},{32,24},{40,32},{48,40},{56,48},{64,56},{72,6... | collective-permute-start | bytes 24584 | tf_op jit(solution)/shard_map/ppermute | solution.py:27
  342.0 5.8 %collective-permute-start.62 = (f32[16,1,128]{2,0,1:T(8,128)S(1)}, f32[16,1,128]{2,0,1:T(8,128)S(1)}, u32[]{:S(2)}, u32[]{:S(2)}) collective-permute-start(f32[16,1,128]{2,0,1:T(8,128)S(1)} %bitcast.187), channel_id=1, source_target_pairs={{1,0},{2,1},{3,2},{4,3},{5,4},{6,5},{7,6},{0,7},{9,8},{10,9},{11,1... | collective-permute-start | bytes 24584 | tf_op jit(solution)/shard_map/ppermute | solution.py:27
  349.7 8.3 %collective-permute-start.60 = (f32[1,16,128]{2,1,0:T(8,128)S(1)}, f32[1,16,128]{2,1,0:T(8,128)S(1)}, u32[]{:S(2)}, u32[]{:S(2)}) collective-permute-start(f32[1,16,128]{2,1,0:T(8,128)S(1)} %get-tuple-element.67), channel_id=1, source_target_pairs={{8,0},{16,8},{24,16},{32,24},{40,32},{48,40},{56,48},{64,56},{72,6... | collective-permute-start | bytes 24584 | tf_op jit(solution)/shard_map/ppermute | solution.py:27
  361.5 5.8 %collective-permute-start.66 = (f32[16,1,128]{2,0,1:T(8,128)S(1)}, f32[16,1,128]{2,0,1:T(8,128)S(1)}, u32[]{:S(2)}, u32[]{:S(2)}) collective-permute-start(f32[16,1,128]{2,0,1:T(8,128)S(1)} %bitcast.188), channel_id=1, source_target_pairs={{1,0},{2,1},{3,2},{4,3},{5,4},{6,5},{7,6},{0,7},{9,8},{10,9},{11,1... | collective-permute-start | bytes 24584 | tf_op jit(solution)/shard_map/ppermute | solution.py:27
  369.2 8.3 %collective-permute-start.64 = (f32[1,16,128]{2,1,0:T(8,128)S(1)}, f32[1,16,128]{2,1,0:T(8,128)S(1)}, u32[]{:S(2)}, u32[]{:S(2)}) collective-permute-start(f32[1,16,128]{2,1,0:T(8,128)S(1)} %get-tuple-element.63), channel_id=1, source_target_pairs={{8,0},{16,8},{24,16},{32,24},{40,32},{48,40},{56,48},{64,56},{72,6... | collective-permute-start | bytes 24584 | tf_op jit(solution)/shard_map/ppermute | solution.py:27
  (289 shorter events, 93.4 us)
Async XLA Ops:
  0.7 34.4 %collective-permute-start.18 = (f32[8,1,64]{2,1,0:T(1,128)S(1)}, f32[8,1,64]{2,1,0:T(1,128)S(1)}, u32[]{:S(2)}, u32[]{:S(2)}) collective-permute-start(f32[8,1,64]{2,1,0:T(1,128)S(1)} %broadcast.255), channel_id=1, source_target_pairs={{1,0},{2,1},{3,2},{4,3},{5,4},{6,5},{7,6},{0,7},{9,8},{10,9},{11,1... | collective-permute-start | bytes 6152 | tf_op jit(solution)/shard_map/ppermute | solution.py:27
  7.8 35.1 %collective-permute-start.19 = (f32[8,1,64]{2,1,0:T(1,128)S(1)}, f32[8,1,64]{2,1,0:T(1,128)S(1)}, u32[]{:S(2)}, u32[]{:S(2)}) collective-permute-start(f32[8,1,64]{2,1,0:T(1,128)S(1)} %broadcast.255), channel_id=1, source_target_pairs={{0,1},{1,2},{2,3},{3,4},{4,5},{5,6},{6,7},{7,0},{8,9},{9,10},{10,1... | collective-permute-start | bytes 6152 | tf_op jit(solution)/shard_map/ppermute | solution.py:26
  9.8 21.4 %collective-permute-start.34 = (f32[1,16,16]{2,1,0:T(8,128)S(1)}, f32[1,16,16]{2,1,0:T(8,128)S(1)}, u32[]{:S(2)}, u32[]{:S(2)}) collective-permute-start(f32[1,16,16]{2,1,0:T(8,128)S(1)} %broadcast.264), channel_id=1, source_target_pairs={{8,0},{16,8},{24,16},{32,24},{40,32},{48,40},{56,48},{64,56},{72,6... | collective-permute-start | bytes 3080 | tf_op jit(solution)/shard_map/ppermute | solution.py:47
  15.4 17.7 %collective-permute-start.35 = (f32[1,16,16]{2,1,0:T(8,128)S(1)}, f32[1,16,16]{2,1,0:T(8,128)S(1)}, u32[]{:S(2)}, u32[]{:S(2)}) collective-permute-start(f32[1,16,16]{2,1,0:T(8,128)S(1)} %broadcast.264), channel_id=1, source_target_pairs={{0,8},{8,16},{16,24},{24,32},{32,40},{40,48},{48,56},{56,64},{64,7... | collective-permute-start | bytes 3080 | tf_op jit(solution)/shard_map/ppermute | solution.py:44
  17.4 77.6 %collective-permute-start.16 = (f32[1,8,64]{2,1,0:T(8,128)S(1)}, f32[1,8,64]{2,1,0:T(8,128)S(1)}, u32[]{:S(2)}, u32[]{:S(2)}) collective-permute-start(f32[1,8,64]{2,1,0:T(8,128)S(1)} %broadcast.254), channel_id=1, source_target_pairs={{8,0},{16,8},{24,16},{32,24},{40,32},{48,40},{56,48},{64,56},{72,6... | collective-permute-start | bytes 6152 | tf_op jit(solution)/shard_map/ppermute | solution.py:27
  31.2 67.0 %collective-permute-start.17 = (f32[1,8,64]{2,1,0:T(8,128)S(1)}, f32[1,8,64]{2,1,0:T(8,128)S(1)}, u32[]{:S(2)}, u32[]{:S(2)}) collective-permute-start(f32[1,8,64]{2,1,0:T(8,128)S(1)} %broadcast.254), channel_id=1, source_target_pairs={{0,8},{8,16},{16,24},{24,32},{32,40},{40,48},{48,56},{56,64},{64,7... | collective-permute-start | bytes 6152 | tf_op jit(solution)/shard_map/ppermute | solution.py:26
  33.1 15.4 %collective-permute-start.5 = (f32[1,16,128]{2,1,0:T(8,128)S(1)}, f32[1,16,128]{2,1,0:T(8,128)S(1)}, u32[]{:S(2)}, u32[]{:S(2)}) collective-permute-start(f32[1,16,128]{2,1,0:T(8,128)S(1)} %get-tuple-element.83), channel_id=1, source_target_pairs={{0,8},{8,16},{16,24},{24,32},{32,40},{40,48},{48,56},{56,64},{64,7... | collective-permute-start | bytes 24584 | tf_op jit(solution)/shard_map/ppermute | solution.py:26
  35.1 29.2 %collective-permute-start.4 = (f32[1,16,128]{2,1,0:T(8,128)S(1)}, f32[1,16,128]{2,1,0:T(8,128)S(1)}, u32[]{:S(2)}, u32[]{:S(2)}) collective-permute-start(f32[1,16,128]{2,1,0:T(8,128)S(1)} %get-tuple-element.82), channel_id=1, source_target_pairs={{8,0},{16,8},{24,16},{32,24},{40,32},{48,40},{56,48},{64,56},{72,6... | collective-permute-start | bytes 24584 | tf_op jit(solution)/shard_map/ppermute | solution.py:27
  51.3 18.1 %collective-permute-start = (f32[4,3,16,128]{3,2,1,0:T(8,128)S(1)}, f32[4,3,16,128]{3,2,1,0:T(8,128)S(1)}, u32[]{:S(2)}, u32[]{:S(2)}) collective-permute-start(f32[4,3,16,128]{3,2,1,0:T(8,128)S(1)} %get-tuple-element.44), channel_id=1, source_target_pairs={{0,8},{8,16},{16,24},{24,32},{32,40},{40,48},{48,56},{56,64},{64,7... | collective-permute-start | bytes 294920 | tf_op jit(solution)/shard_map/ppermute | solution.py:44
  55.0 14.4 %collective-permute-start.1 = (f32[4,3,16,128]{3,2,1,0:T(8,128)S(1)}, f32[4,3,16,128]{3,2,1,0:T(8,128)S(1)}, u32[]{:S(2)}, u32[]{:S(2)}) collective-permute-start(f32[4,3,16,128]{3,2,1,0:T(8,128)S(1)} %get-tuple-element.45), channel_id=1, source_target_pairs={{8,0},{16,8},{24,16},{32,24},{40,32},{48,40},{56,48},{64,56},{72,6... | collective-permute-start | bytes 294920 | tf_op jit(solution)/shard_map/ppermute | solution.py:47
  64.3 90.3 %collective-permute-start.28 = (f32[1,32,32]{2,1,0:T(8,128)S(1)}, f32[1,32,32]{2,1,0:T(8,128)S(1)}, u32[]{:S(2)}, u32[]{:S(2)}) collective-permute-start(f32[1,32,32]{2,1,0:T(8,128)S(1)} %broadcast.259), channel_id=1, source_target_pairs={{8,0},{16,8},{24,16},{32,24},{40,32},{48,40},{56,48},{64,56},{72,6... | collective-permute-start | bytes 12296 | tf_op jit(solution)/shard_map/ppermute | solution.py:47
  69.6 9.5 %collective-permute-start.2 = (f32[4,22,3,128]{3,0,2,1:T(4,128)S(1)}, f32[4,22,3,128]{3,0,2,1:T(4,128)S(1)}, u32[]{:S(2)}, u32[]{:S(2)}) collective-permute-start(f32[4,22,3,128]{3,0,2,1:T(4,128)S(1)} %copy.434), channel_id=1, source_target_pairs={{0,1},{1,2},{2,3},{3,4},{4,5},{5,6},{6,7},{7,0},{8,9},{9,10},{10,1... | collective-permute-start | bytes 405512 | tf_op jit(solution)/shard_map/ppermute | solution.py:44
  71.5 8.6 %collective-permute-start.3 = (f32[4,22,3,128]{3,0,2,1:T(4,128)S(1)}, f32[4,22,3,128]{3,0,2,1:T(4,128)S(1)}, u32[]{:S(2)}, u32[]{:S(2)}) collective-permute-start(f32[4,22,3,128]{3,0,2,1:T(4,128)S(1)} %copy.435), channel_id=1, source_target_pairs={{1,0},{2,1},{3,2},{4,3},{5,4},{6,5},{7,6},{0,7},{9,8},{10,9},{11,1... | collective-permute-start | bytes 405512 | tf_op jit(solution)/shard_map/ppermute | solution.py:47
  86.8 13.8 %collective-permute-start.10 = (f32[16,1,128]{2,0,1:T(8,128)S(1)}, f32[16,1,128]{2,0,1:T(8,128)S(1)}, u32[]{:S(2)}, u32[]{:S(2)}) collective-permute-start(f32[16,1,128]{2,0,1:T(8,128)S(1)} %bitcast.181), channel_id=1, source_target_pairs={{1,0},{2,1},{3,2},{4,3},{5,4},{6,5},{7,6},{0,7},{9,8},{10,9},{11,1... | collective-permute-start | bytes 24584 | tf_op jit(solution)/shard_map/ppermute | solution.py:27
  104.9 18.2 %collective-permute-start.14 = (f32[16,1,128]{2,0,1:T(8,128)S(1)}, f32[16,1,128]{2,0,1:T(8,128)S(1)}, u32[]{:S(2)}, u32[]{:S(2)}) collective-permute-start(f32[16,1,128]{2,0,1:T(8,128)S(1)} %bitcast.185), channel_id=1, source_target_pairs={{1,0},{2,1},{3,2},{4,3},{5,4},{6,5},{7,6},{0,7},{9,8},{10,9},{11,1... | collective-permute-start | bytes 24584 | tf_op jit(solution)/shard_map/ppermute | solution.py:27
  110.4 14.7 %collective-permute-start.15 = (f32[16,1,128]{2,0,1:T(8,128)S(1)}, f32[16,1,128]{2,0,1:T(8,128)S(1)}, u32[]{:S(2)}, u32[]{:S(2)}) collective-permute-start(f32[16,1,128]{2,0,1:T(8,128)S(1)} %bitcast.180), channel_id=1, source_target_pairs={{0,1},{1,2},{2,3},{3,4},{4,5},{5,6},{6,7},{7,0},{8,9},{9,10},{10,1... | collective-permute-start | bytes 24584 | tf_op jit(solution)/shard_map/ppermute | solution.py:26
  112.3 12.8 %collective-permute-start.12 = (f32[1,16,128]{2,1,0:T(8,128)S(1)}, f32[1,16,128]{2,1,0:T(8,128)S(1)}, u32[]{:S(2)}, u32[]{:S(2)}) collective-permute-start(f32[1,16,128]{2,1,0:T(8,128)S(1)} %get-tuple-element.75), channel_id=1, source_target_pairs={{8,0},{16,8},{24,16},{32,24},{40,32},{48,40},{56,48},{64,56},{72,6... | collective-permute-start | bytes 24584 | tf_op jit(solution)/shard_map/ppermute | solution.py:27
  123.2 33.4 %collective-permute-start.29 = (f32[1,32,32]{2,1,0:T(8,128)S(1)}, f32[1,32,32]{2,1,0:T(8,128)S(1)}, u32[]{:S(2)}, u32[]{:S(2)}) collective-permute-start(f32[1,32,32]{2,1,0:T(8,128)S(1)} %broadcast.259), channel_id=1, source_target_pairs={{0,8},{8,16},{16,24},{24,32},{32,40},{40,48},{48,56},{56,64},{64,7... | collective-permute-start | bytes 12296 | tf_op jit(solution)/shard_map/ppermute | solution.py:44
  139.5 17.1 %collective-permute-start.22 = (f32[8,1,64]{2,1,0:T(1,128)S(1)}, f32[8,1,64]{2,1,0:T(1,128)S(1)}, u32[]{:S(2)}, u32[]{:S(2)}) collective-permute-start(f32[8,1,64]{2,1,0:T(1,128)S(1)} %get-tuple-element.157), channel_id=1, source_target_pairs={{1,0},{2,1},{3,2},{4,3},{5,4},{6,5},{7,6},{0,7},{9,8},{10,9},{11,1... | collective-permute-start | bytes 6152 | tf_op jit(solution)/shard_map/ppermute | solution.py:27
  145.3 11.3 %collective-permute-start.23 = (f32[8,1,64]{2,1,0:T(1,128)S(1)}, f32[8,1,64]{2,1,0:T(1,128)S(1)}, u32[]{:S(2)}, u32[]{:S(2)}) collective-permute-start(f32[8,1,64]{2,1,0:T(1,128)S(1)} %get-tuple-element.156), channel_id=1, source_target_pairs={{0,1},{1,2},{2,3},{3,4},{4,5},{5,6},{6,7},{7,0},{8,9},{9,10},{10,1... | collective-permute-start | bytes 6152 | tf_op jit(solution)/shard_map/ppermute | solution.py:26
  147.2 9.4 %collective-permute-start.20 = (f32[1,8,64]{2,1,0:T(8,128)S(1)}, f32[1,8,64]{2,1,0:T(8,128)S(1)}, u32[]{:S(2)}, u32[]{:S(2)}) collective-permute-start(f32[1,8,64]{2,1,0:T(8,128)S(1)} %get-tuple-element.159), channel_id=1, source_target_pairs={{8,0},{16,8},{24,16},{32,24},{40,32},{48,40},{56,48},{64,56},{72,6... | collective-permute-start | bytes 6152 | tf_op jit(solution)/shard_map/ppermute | solution.py:27
  158.4 18.3 %collective-permute-start.26 = (f32[8,1,64]{2,1,0:T(1,128)S(1)}, f32[8,1,64]{2,1,0:T(1,128)S(1)}, u32[]{:S(2)}, u32[]{:S(2)}) collective-permute-start(f32[8,1,64]{2,1,0:T(1,128)S(1)} %get-tuple-element.153), channel_id=1, source_target_pairs={{1,0},{2,1},{3,2},{4,3},{5,4},{6,5},{7,6},{0,7},{9,8},{10,9},{11,1... | collective-permute-start | bytes 6152 | tf_op jit(solution)/shard_map/ppermute | solution.py:27
  163.9 12.9 %collective-permute-start.27 = (f32[8,1,64]{2,1,0:T(1,128)S(1)}, f32[8,1,64]{2,1,0:T(1,128)S(1)}, u32[]{:S(2)}, u32[]{:S(2)}) collective-permute-start(f32[8,1,64]{2,1,0:T(1,128)S(1)} %get-tuple-element.152), channel_id=1, source_target_pairs={{0,1},{1,2},{2,3},{3,4},{4,5},{5,6},{6,7},{7,0},{8,9},{9,10},{10,1... | collective-permute-start | bytes 6152 | tf_op jit(solution)/shard_map/ppermute | solution.py:26
  165.8 11.0 %collective-permute-start.24 = (f32[1,8,64]{2,1,0:T(8,128)S(1)}, f32[1,8,64]{2,1,0:T(8,128)S(1)}, u32[]{:S(2)}, u32[]{:S(2)}) collective-permute-start(f32[1,8,64]{2,1,0:T(8,128)S(1)} %get-tuple-element.155), channel_id=1, source_target_pairs={{8,0},{16,8},{24,16},{32,24},{40,32},{48,40},{56,48},{64,56},{72,6... | collective-permute-start | bytes 6152 | tf_op jit(solution)/shard_map/ppermute | solution.py:27
  179.9 10.2 %all-to-all-start = ((f32[8,1,512]{2,1,0:T(1,128)}), f32[8,1,512]{2,1,0:T(1,128)S(1)}, u32[]{:S(2)}, u32[]{:S(2)}) async-start(f32[8,1,512]{2,1,0:T(1,128)} %reshape.66), calls=%async_computation | async-start | bytes 32768 | tf_op jit(solution)/shard_map/all_to_all | solution.py:54
  191.5 11.4 %collective-permute-start.30 = (f32[1,32,32]{2,1,0:T(8,128)S(1)}, f32[1,32,32]{2,1,0:T(8,128)S(1)}, u32[]{:S(2)}, u32[]{:S(2)}) collective-permute-start(f32[1,32,32]{2,1,0:T(8,128)S(1)} %get-tuple-element.123), channel_id=1, source_target_pairs={{8,0},{16,8},{24,16},{32,24},{40,32},{48,40},{56,48},{64,56},{72,6... | collective-permute-start | bytes 12296 | tf_op jit(solution)/shard_map/ppermute | solution.py:47
  204.4 10.1 %collective-permute-start.32 = (f32[1,32,32]{2,1,0:T(8,128)S(1)}, f32[1,32,32]{2,1,0:T(8,128)S(1)}, u32[]{:S(2)}, u32[]{:S(2)}) collective-permute-start(f32[1,32,32]{2,1,0:T(8,128)S(1)} %get-tuple-element.121), channel_id=1, source_target_pairs={{8,0},{16,8},{24,16},{32,24},{40,32},{48,40},{56,48},{64,56},{72,6... | collective-permute-start | bytes 12296 | tf_op jit(solution)/shard_map/ppermute | solution.py:47
  216.7 10.1 %collective-permute-start.36 = (f32[1,16,16]{2,1,0:T(8,128)S(1)}, f32[1,16,16]{2,1,0:T(8,128)S(1)}, u32[]{:S(2)}, u32[]{:S(2)}) collective-permute-start(f32[1,16,16]{2,1,0:T(8,128)S(1)} %get-tuple-element.167), channel_id=1, source_target_pairs={{8,0},{16,8},{24,16},{32,24},{40,32},{48,40},{56,48},{64,56},{72,6... | collective-permute-start | bytes 3080 | tf_op jit(solution)/shard_map/ppermute | solution.py:47
  228.1 10.0 %collective-permute-start.38 = (f32[1,16,16]{2,1,0:T(8,128)S(1)}, f32[1,16,16]{2,1,0:T(8,128)S(1)}, u32[]{:S(2)}, u32[]{:S(2)}) collective-permute-start(f32[1,16,16]{2,1,0:T(8,128)S(1)} %get-tuple-element.165), channel_id=1, source_target_pairs={{8,0},{16,8},{24,16},{32,24},{40,32},{48,40},{56,48},{64,56},{72,6... | collective-permute-start | bytes 3080 | tf_op jit(solution)/shard_map/ppermute | solution.py:47
  239.4 10.0 %collective-permute-start.40 = (f32[1,16,16]{2,1,0:T(8,128)S(1)}, f32[1,16,16]{2,1,0:T(8,128)S(1)}, u32[]{:S(2)}, u32[]{:S(2)}) collective-permute-start(f32[1,16,16]{2,1,0:T(8,128)S(1)} %get-tuple-element.163), channel_id=1, source_target_pairs={{8,0},{16,8},{24,16},{32,24},{40,32},{48,40},{56,48},{64,56},{72,6... | collective-permute-start | bytes 3080 | tf_op jit(solution)/shard_map/ppermute | solution.py:47
  250.8 10.0 %collective-permute-start.42 = (f32[1,16,16]{2,1,0:T(8,128)S(1)}, f32[1,16,16]{2,1,0:T(8,128)S(1)}, u32[]{:S(2)}, u32[]{:S(2)}) collective-permute-start(f32[1,16,16]{2,1,0:T(8,128)S(1)} %get-tuple-element.161), channel_id=1, source_target_pairs={{8,0},{16,8},{24,16},{32,24},{40,32},{48,40},{56,48},{64,56},{72,6... | collective-permute-start | bytes 3080 | tf_op jit(solution)/shard_map/ppermute | solution.py:47
  262.4 10.0 %collective-permute-start.44 = (f32[1,32,32]{2,1,0:T(8,128)S(1)}, f32[1,32,32]{2,1,0:T(8,128)S(1)}, u32[]{:S(2)}, u32[]{:S(2)}) collective-permute-start(f32[1,32,32]{2,1,0:T(8,128)S(1)} %get-tuple-element.119), channel_id=1, source_target_pairs={{8,0},{16,8},{24,16},{32,24},{40,32},{48,40},{56,48},{64,56},{72,6... | collective-permute-start | bytes 12296 | tf_op jit(solution)/shard_map/ppermute | solution.py:47
  273.9 10.1 %collective-permute-start.46 = (f32[1,32,32]{2,1,0:T(8,128)S(1)}, f32[1,32,32]{2,1,0:T(8,128)S(1)}, u32[]{:S(2)}, u32[]{:S(2)}) collective-permute-start(f32[1,32,32]{2,1,0:T(8,128)S(1)} %get-tuple-element.117), channel_id=1, source_target_pairs={{8,0},{16,8},{24,16},{32,24},{40,32},{48,40},{56,48},{64,56},{72,6... | collective-permute-start | bytes 12296 | tf_op jit(solution)/shard_map/ppermute | solution.py:47
  285.8 15.9 %collective-permute-start.50 = (f32[8,1,64]{2,1,0:T(1,128)S(1)}, f32[8,1,64]{2,1,0:T(1,128)S(1)}, u32[]{:S(2)}, u32[]{:S(2)}) collective-permute-start(f32[8,1,64]{2,1,0:T(1,128)S(1)} %get-tuple-element.139), channel_id=1, source_target_pairs={{1,0},{2,1},{3,2},{4,3},{5,4},{6,5},{7,6},{0,7},{9,8},{10,9},{11,1... | collective-permute-start | bytes 6152 | tf_op jit(solution)/shard_map/ppermute | solution.py:27
  288.6 13.1 %collective-permute-start.51 = (f32[8,1,64]{2,1,0:T(1,128)S(1)}, f32[8,1,64]{2,1,0:T(1,128)S(1)}, u32[]{:S(2)}, u32[]{:S(2)}) collective-permute-start(f32[8,1,64]{2,1,0:T(1,128)S(1)} %get-tuple-element.138), channel_id=1, source_target_pairs={{0,1},{1,2},{2,3},{3,4},{4,5},{5,6},{6,7},{7,0},{8,9},{9,10},{10,1... | collective-permute-start | bytes 6152 | tf_op jit(solution)/shard_map/ppermute | solution.py:26
  291.1 10.7 %collective-permute-start.48 = (f32[1,8,64]{2,1,0:T(8,128)S(1)}, f32[1,8,64]{2,1,0:T(8,128)S(1)}, u32[]{:S(2)}, u32[]{:S(2)}) collective-permute-start(f32[1,8,64]{2,1,0:T(8,128)S(1)} %get-tuple-element.141), channel_id=1, source_target_pairs={{8,0},{16,8},{24,16},{32,24},{40,32},{48,40},{56,48},{64,56},{72,6... | collective-permute-start | bytes 6152 | tf_op jit(solution)/shard_map/ppermute | solution.py:27
  303.1 17.1 %collective-permute-start.54 = (f32[8,1,64]{2,1,0:T(1,128)S(1)}, f32[8,1,64]{2,1,0:T(1,128)S(1)}, u32[]{:S(2)}, u32[]{:S(2)}) collective-permute-start(f32[8,1,64]{2,1,0:T(1,128)S(1)} %get-tuple-element.135), channel_id=1, source_target_pairs={{1,0},{2,1},{3,2},{4,3},{5,4},{6,5},{7,6},{0,7},{9,8},{10,9},{11,1... | collective-permute-start | bytes 6152 | tf_op jit(solution)/shard_map/ppermute | solution.py:27
  308.0 12.2 %collective-permute-start.55 = (f32[8,1,64]{2,1,0:T(1,128)S(1)}, f32[8,1,64]{2,1,0:T(1,128)S(1)}, u32[]{:S(2)}, u32[]{:S(2)}) collective-permute-start(f32[8,1,64]{2,1,0:T(1,128)S(1)} %get-tuple-element.134), channel_id=1, source_target_pairs={{0,1},{1,2},{2,3},{3,4},{4,5},{5,6},{6,7},{7,0},{8,9},{9,10},{10,1... | collective-permute-start | bytes 6152 | tf_op jit(solution)/shard_map/ppermute | solution.py:26
  310.0 10.3 %collective-permute-start.52 = (f32[1,8,64]{2,1,0:T(8,128)S(1)}, f32[1,8,64]{2,1,0:T(8,128)S(1)}, u32[]{:S(2)}, u32[]{:S(2)}) collective-permute-start(f32[1,8,64]{2,1,0:T(8,128)S(1)} %get-tuple-element.137), channel_id=1, source_target_pairs={{8,0},{16,8},{24,16},{32,24},{40,32},{48,40},{56,48},{64,56},{72,6... | collective-permute-start | bytes 6152 | tf_op jit(solution)/shard_map/ppermute | solution.py:27
  322.5 17.9 %collective-permute-start.58 = (f32[16,1,128]{2,0,1:T(8,128)S(1)}, f32[16,1,128]{2,0,1:T(8,128)S(1)}, u32[]{:S(2)}, u32[]{:S(2)}) collective-permute-start(f32[16,1,128]{2,0,1:T(8,128)S(1)} %bitcast.186), channel_id=1, source_target_pairs={{1,0},{2,1},{3,2},{4,3},{5,4},{6,5},{7,6},{0,7},{9,8},{10,9},{11,1... | collective-permute-start | bytes 24584 | tf_op jit(solution)/shard_map/ppermute | solution.py:27
  328.3 12.2 %collective-permute-start.59 = (f32[16,1,128]{2,0,1:T(8,128)S(1)}, f32[16,1,128]{2,0,1:T(8,128)S(1)}, u32[]{:S(2)}, u32[]{:S(2)}) collective-permute-start(f32[16,1,128]{2,0,1:T(8,128)S(1)} %bitcast.182), channel_id=1, source_target_pairs={{0,1},{1,2},{2,3},{3,4},{4,5},{5,6},{6,7},{7,0},{8,9},{9,10},{10,1... | collective-permute-start | bytes 24584 | tf_op jit(solution)/shard_map/ppermute | solution.py:26
  330.2 10.3 %collective-permute-start.56 = (f32[1,16,128]{2,1,0:T(8,128)S(1)}, f32[1,16,128]{2,1,0:T(8,128)S(1)}, u32[]{:S(2)}, u32[]{:S(2)}) collective-permute-start(f32[1,16,128]{2,1,0:T(8,128)S(1)} %get-tuple-element.71), channel_id=1, source_target_pairs={{8,0},{16,8},{24,16},{32,24},{40,32},{48,40},{56,48},{64,56},{72,6... | collective-permute-start | bytes 24584 | tf_op jit(solution)/shard_map/ppermute | solution.py:27
  342.0 17.9 %collective-permute-start.62 = (f32[16,1,128]{2,0,1:T(8,128)S(1)}, f32[16,1,128]{2,0,1:T(8,128)S(1)}, u32[]{:S(2)}, u32[]{:S(2)}) collective-permute-start(f32[16,1,128]{2,0,1:T(8,128)S(1)} %bitcast.187), channel_id=1, source_target_pairs={{1,0},{2,1},{3,2},{4,3},{5,4},{6,5},{7,6},{0,7},{9,8},{10,9},{11,1... | collective-permute-start | bytes 24584 | tf_op jit(solution)/shard_map/ppermute | solution.py:27
  347.7 12.2 %collective-permute-start.63 = (f32[16,1,128]{2,0,1:T(8,128)S(1)}, f32[16,1,128]{2,0,1:T(8,128)S(1)}, u32[]{:S(2)}, u32[]{:S(2)}) collective-permute-start(f32[16,1,128]{2,0,1:T(8,128)S(1)} %bitcast.183), channel_id=1, source_target_pairs={{0,1},{1,2},{2,3},{3,4},{4,5},{5,6},{6,7},{7,0},{8,9},{9,10},{10,1... | collective-permute-start | bytes 24584 | tf_op jit(solution)/shard_map/ppermute | solution.py:26
  349.7 10.3 %collective-permute-start.60 = (f32[1,16,128]{2,1,0:T(8,128)S(1)}, f32[1,16,128]{2,1,0:T(8,128)S(1)}, u32[]{:S(2)}, u32[]{:S(2)}) collective-permute-start(f32[1,16,128]{2,1,0:T(8,128)S(1)} %get-tuple-element.67), channel_id=1, source_target_pairs={{8,0},{16,8},{24,16},{32,24},{40,32},{48,40},{56,48},{64,56},{72,6... | collective-permute-start | bytes 24584 | tf_op jit(solution)/shard_map/ppermute | solution.py:27
  361.5 17.9 %collective-permute-start.66 = (f32[16,1,128]{2,0,1:T(8,128)S(1)}, f32[16,1,128]{2,0,1:T(8,128)S(1)}, u32[]{:S(2)}, u32[]{:S(2)}) collective-permute-start(f32[16,1,128]{2,0,1:T(8,128)S(1)} %bitcast.188), channel_id=1, source_target_pairs={{1,0},{2,1},{3,2},{4,3},{5,4},{6,5},{7,6},{0,7},{9,8},{10,9},{11,1... | collective-permute-start | bytes 24584 | tf_op jit(solution)/shard_map/ppermute | solution.py:27
  367.3 12.2 %collective-permute-start.67 = (f32[16,1,128]{2,0,1:T(8,128)S(1)}, f32[16,1,128]{2,0,1:T(8,128)S(1)}, u32[]{:S(2)}, u32[]{:S(2)}) collective-permute-start(f32[16,1,128]{2,0,1:T(8,128)S(1)} %bitcast.184), channel_id=1, source_target_pairs={{0,1},{1,2},{2,3},{3,4},{4,5},{5,6},{6,7},{7,0},{8,9},{9,10},{10,1... | collective-permute-start | bytes 24584 | tf_op jit(solution)/shard_map/ppermute | solution.py:26
  369.2 10.3 %collective-permute-start.64 = (f32[1,16,128]{2,1,0:T(8,128)S(1)}, f32[1,16,128]{2,1,0:T(8,128)S(1)}, u32[]{:S(2)}, u32[]{:S(2)}) collective-permute-start(f32[1,16,128]{2,1,0:T(8,128)S(1)} %get-tuple-element.63), channel_id=1, source_target_pairs={{8,0},{16,8},{24,16},{32,24},{40,32},{48,40},{56,48},{64,56},{72,6... | collective-permute-start | bytes 24584 | tf_op jit(solution)/shard_map/ppermute | solution.py:27
  (24 other events, 175.1 us)
where the time goes:
time: 388 us; the launch traced here: 382 us
  starting transfers between devices  311 us (80%)
  waiting for transfers between devices  29.9 us (8%)
  local copies, waits for them, and re-layouts  20.3 us (5%)
  other arithmetic  17.8 us (5%)
    ppermute x22, starting transfers between devices, padded_2(): lax.ppermute(initial, axis, [(b, a) for a, b in up])  148 us
    ppermute x12, starting transfers between devices, with_halo(): lax.ppermute(lax.slice_in_dim(block, 0, width, axis=dim), axis, backward)  91.7 us
    ppermute x22, starting transfers between devices, padded_2(): lax.ppermute(last, axis, up)  43.4 us
    ppermute x12, starting transfers between devices, with_halo(): lax.ppermute(lax.slice_in_dim(block, block.shape[dim] - width, None, axis...  23 us
    ppermute x22, waiting for transfers between devices, padded_2(): lax.ppermute(last, axis, up)  13.2 us
    reshape x3, local copies, waits for them, and re-layouts, coarsen(): values.reshape(values.shape[0] // 2, 2, values.shape[1] // 2, 2, values.s...  11.4 us
    ppermute x12, waiting for transfers between devices, with_halo(): lax.ppermute(lax.slice_in_dim(block, block.shape[dim] - width, None, axis...  10.7 us
  transfers between devices with their start and end apart: 69, of which 20 were waited for; matrix products, arithmetic and copies ran while one was open for 7% of the time, Pallas kernels for 0%

commit v1 on v0

v1 whole, which is shorter than its diff:
```python
import jax
import jax.numpy as jnp
from jax import lax
from jax.experimental import pallas as pl
from jax.experimental.pallas import tpu as pltpu
from jax.sharding import PartitionSpec as P

VH = 9
PH = 7
B = 16
VX = B + 2 * VH
PX = B + 2 * PH
SIDE = 3 * VH + 2 * PH
STEP = 0.1
EDDY = 0.03
COEFF = 0.8 / 12.0
WINDOW = 4
VMEM = pl.BlockSpec(memory_space=pltpu.VMEM)
SMEM = pl.BlockSpec(memory_space=pltpu.SMEM)
F32 = jnp.float32


def shape(*dims):
    return jax.ShapeDtypeStruct(dims, F32)


def call(body, outs, specs, scratch=()):
    return pl.pallas_call(
        body,
        out_shape=outs,
        in_specs=specs,
        out_specs=[VMEM] * len(outs),
        scratch_shapes=[pltpu.VMEM(s, F32) for s in scratch],
        compiler_params=pltpu.CompilerParams(vmem_limit_bytes=48 * 1024 * 1024),
    )


def iota(like, dim):
    return lax.broadcasted_iota(jnp.int32, like.shape, dim)


def lane_of(values):
    return iota(values, values.ndim - 1)


def row_of(values):
    return iota(values, values.ndim - 2)


def turn(values, amount, dim):
    return pltpu.roll(values, amount % values.shape[dim], dim)


def pack_x(place, land, drag_table, velocity, pressure, turbine, near, far, drag):
    core = place[0] % 2
    kinds = land[...]
    ground = jnp.zeros(kinds.shape, F32)
    for kind in range(16):
        ground = jnp.where(kinds == kind, drag_table[kind], ground)
    square = lax.broadcasted_iota(jnp.int32, (B, B), 0) == lax.broadcasted_iota(jnp.int32, (B, B), 1)
    for i in range(B):
        row = jnp.broadcast_to(ground[i : i + 1, :], (B, B))
        column = jnp.sum(jnp.where(square, row, 0.0), axis=1, keepdims=True)
        cells = turbine[i].astype(F32)
        drag[i] = 2.0 * cells + jnp.where(lane_of(cells) == 0, column, 0.0)

    def fill(out, high):
        start = B - VH if high else 0
        for a in range(3):
            out[a * VH : (a + 1) * VH] = velocity[a, start : start + VH]
        start = B - PH if high else 0
        out[3 * VH : 3 * VH + PH] = pressure[start : start + PH]
        out[3 * VH + PH : SIDE] = drag[start : start + PH]

    @pl.when(core == 0)
    def _():
        fill(near, True)
        fill(far, False)

    @pl.when(core == 1)
    def _():
        fill(near, False)
        fill(far, True)


def widen_x(place, velocity, pressure, drag, near, far, wide_v, wide_p, wide_d, near_y, far_y):
    core = place[0] % 2
    odd = place[1] % 2
    for a in range(3):
        wide_v[a, VH : VH + B] = velocity[a]
    wide_p[PH : PH + B] = pressure[...]
    wide_d[PH : PH + B] = drag[...]

    def fill(low, high):
        for a in range(3):
            wide_v[a, :VH] = low[a * VH : (a + 1) * VH]
            wide_v[a, VH + B :] = high[a * VH : (a + 1) * VH]
        wide_p[:PH] = low[3 * VH : 3 * VH + PH]
        wide_p[PH + B :] = high[3 * VH : 3 * VH + PH]
        wide_d[:PH] = low[3 * VH + PH :]
        wide_d[PH + B :] = high[3 * VH + PH :]

    @pl.when(core == 0)
    def _():
        fill(far, near)

    @pl.when(core == 1)
    def _():
        fill(near, far)

    def send(up, down):
        up[...] = wide_v[:, :, B - 4 :, :]
        down[...] = wide_v[:, :, :4, :]
        up[0, 2 : 2 + PX, 0:1, :] = wide_d[:, B - 1 :, :]
        down[0, 2 : 2 + PX, 3:4, :] = wide_d[:, 0:1, :]

    @pl.when(odd == 0)
    def _():
        send(near_y, far_y)

    @pl.when(odd == 1)
    def _():
        send(far_y, near_y)


def advance(place, wide_v, wide_p, wide_d, near, far, star, source, near_y, far_y, v, dr, tau, part):
    odd = place[1] % 2
    v[:, :, 0:B, :] = wide_v[...]
    dr[:, 0:B, :] = wide_d[...]

    def fill(low, high):
        v[:, :, B : B + 4, :] = high[...]
        v[:, :, B + 4 : B + 8, :] = low[...]
        dr[:, B : B + 8, :] = jnp.zeros((PX, 8, 128), F32)
        dr[:, B : B + 1, :] = high[0, 2 : 2 + PX, 3:4, :]
        dr[:, B + 7 : B + 8, :] = low[0, 2 : 2 + PX, 0:1, :]

    @pl.when(odd == 0)
    def _():
        fill(far, near)

    @pl.when(odd == 1)
    def _():
        fill(near, far)

    def zero_shifts(values):
        lane = lane_of(values)
        return (
            jnp.where(lane == 127, 0.0, turn(values, -1, 1)),
            jnp.where(lane == 0, 0.0, turn(values, 1, 1)),
        )

    for i in range(1, VX - 1):
        u = [v[a, i] for a in range(3)]
        gx = [0.5 * (v[a, i + 1] - v[a, i - 1]) for a in range(3)]
        gy = [0.5 * (turn(u[a], -1, 0) - turn(u[a], 1, 0)) for a in range(3)]
        gz = []
        for a in range(3):
            above, below = zero_shifts(u[a])
            gz.append(above - below)
        e01 = gx[1] + gy[0]
        e02 = gx[2] + gz[0]
        e12 = gy[2] + gz[1]
        total = 2.0 * (gx[0] * gx[0] + gy[1] * gy[1] + gz[2] * gz[2]) + (
            e01 * e01 + e02 * e02 + e12 * e12
        )
        visc = EDDY * jnp.sqrt(total)
        tau[0, i] = 2.0 * visc * gx[0]
        tau[1, i] = visc * e01
        tau[2, i] = visc * e02
        if i < 2 or i >= VX - 2:
            continue
        along_y = [visc * e01, 2.0 * visc * gy[1], visc * e12]
        along_z = [visc * e02, visc * e12, 2.0 * visc * gz[2]]
        lane = lane_of(u[0])
        ghost = [jnp.where(lane == 0, u[a], -u[a]) for a in range(3)]
        ghost_visc = EDDY * jnp.sqrt(
            ghost[0] * ghost[0] + ghost[1] * ghost[1] + 2.0 * ghost[2] * ghost[2]
        )
        ghost_tau = [ghost_visc * ghost[0], ghost_visc * ghost[1], 2.0 * ghost_visc * ghost[2]]
        wind = dr[i - 2] * jnp.sqrt(u[0] * u[0] + u[1] * u[1])
        for a in range(3):
            change = 0.5 * (turn(along_y[a], -1, 0) - turn(along_y[a], 1, 0))
            above = jnp.where(lane == 127, ghost_tau[a], turn(along_z[a], -1, 1))
            below = jnp.where(lane == 0, ghost_tau[a], turn(along_z[a], 1, 1))
            change = change + (above - below)
            change = change - (u[0] * gx[a] + u[1] * gy[a] + u[2] * gz[a])
            if a < 2:
                change = change - wind * u[a]
            if a == 0:
                change = change + 1.0
            part[a, i] = u[a] + STEP * change
    for i in range(2, VX - 2):
        for a in range(3):
            part[a, i] = part[a, i] + (0.5 * STEP) * (tau[a, i + 1] - tau[a, i - 1])
    for a in range(3):
        star[a] = part[a, VH : VH + B, 0:B, :]
    for i in range(3, VX - 3):
        along_x = 0.5 * (part[0, i + 1] - part[0, i - 1])
        s1 = part[1, i]
        along_y = 0.5 * (turn(s1, -1, 0) - turn(s1, 1, 0))
        above, below = zero_shifts(part[2, i])
        source[i - 3] = ((along_x + along_y + (above - below)) / STEP)[0:B]

    def send(up, down):
        up[0 : PX - 2] = source[:, B - 8 :, :]
        up[PX - 2 :] = wide_p[:, B - 8 :, :]
        down[0 : PX - 2] = source[:, :8, :]
        down[PX - 2 :] = wide_p[:, :8, :]

    @pl.when(odd == 0)
    def _():
        send(near_y, far_y)

    @pl.when(odd == 1)
    def _():
        send(far_y, near_y)


def neighbours(ref, start, count, dy, dz):
    p = ref[start : start + count]
    lane = lane_of(p)
    below = jnp.where(lane < dz, p, turn(p, dz, 2))
    above = jnp.where(lane >= 128 - dz, p, turn(p, -dz, 2))
    sides = ref[start - 1 : start - 1 + count] + ref[start + 1 : start + 1 + count]
    return p, sides + (turn(p, dy, 1) + turn(p, -dy, 1)) + 4.0 * (below + above)


def chunks(first, last, size=2):
    return [(i, min(size, last - i)) for i in range(first, last, size)]


def sweep(dst, src, right, first, last, dy, dz, offset=0):
    for i, n in chunks(first, last):
        p, around = neighbours(src, i, n, dy, dz)
        dst[i : i + n] = 0.2 * p + COEFF * (around - right[i - offset : i - offset + n])


def scaled_residual(src, right, i, n, dy, dz):
    p, around = neighbours(src, i, n, dy, dz)
    return right[i : i + n] - around + 12.0 * p


def coarsen_pair(pair, dy, dz):
    total = pair[0] + pair[1]
    lane = lane_of(total)
    total = total + jnp.where((lane & dz) == 0, turn(total, -dz, 1), turn(total, dz, 1))
    row = row_of(total)
    total = total + jnp.where((row & dy) == 0, turn(total, -dy, 0), turn(total, dy, 0))
    return 0.5 * total


def presmooth(place, source, wide_p, near, far, finest, right, packed_one, packed_two, p, s, q, f1, a1, b1):
    odd = place[1] % 2
    nx = PX - 2
    p[:, 0:B, :] = wide_p[...]
    s[1 : PX - 1, 0:B, :] = source[...]

    def fill(low, high):
        s[1 : PX - 1, B : B + 8, :] = high[:nx]
        s[1 : PX - 1, B + 8 : B + 16, :] = low[:nx]
        p[:, B : B + 8, :] = high[nx:]
        p[:, B + 8 : B + 16, :] = low[nx:]

    @pl.when(odd == 0)
    def _():
        fill(far, near)

    @pl.when(odd == 1)
    def _():
        fill(near, far)

    sweep(q, p, s, 1, PX - 1, 1, 1)
    sweep(p, q, s, 2, PX - 2, 1, 1)
    finest[...] = p[4 : PX - 4]
    right[...] = s[5 : PX - 5]
    for k in range(12):
        f1[k] = coarsen_pair(scaled_residual(p, s, 3 + 2 * k, 2, 1, 1), 1, 1)
    a1[...] = -COEFF * f1[...]
    sweep(b1, a1, f1, 1, 11, 2, 2)
    f2 = [coarsen_pair(scaled_residual(b1, f1, 2 + 2 * k, 2, 2, 2), 2, 2) for k in range(4)]
    lane = lane_of(f2[0]) & 3
    two = jnp.where(lane == 0, f2[0], jnp.where(lane == 1, f2[1], jnp.where(lane == 2, f2[2], f2[3])))
    for y in range(4):
        packed_two[y : y + 1, :] = two[4 * y : 4 * y + 1, :]
    for g in range(2):
        rows = [f1[2 + 4 * g + j][0:B] for j in range(4)]
        slot = 2 * (row_of(rows[0]) & 1) + (lane_of(rows[0]) & 1)
        packed_one[g] = jnp.where(
            slot == 0, rows[0], jnp.where(slot == 1, rows[1], jnp.where(slot == 2, rows[2], rows[3]))
        )


def pack_y(peers, place, blocks, own, near, far, out):
    core = place[0] % 2
    for j in range(2 * WINDOW + 1):
        piece = blocks[(place[0] + (peers - WINDOW + j)) % peers]
        for k in range(8):
            out[k, 96 + 4 * j : 100 + 4 * j, :] = piece
    for k in range(8):
        out[k, 132:136, :] = jnp.zeros((4, 128), F32)

    def fill(low, high):
        for k in range(8):
            for g in range(2):
                out[k, 16 * g : 16 * g + 16, :] = low[g]
                out[k, 32 + 16 * g : 48 + 16 * g, :] = own[g]
                out[k, 64 + 16 * g : 80 + 16 * g, :] = high[g]

    @pl.when(core == 0)
    def _():
        fill(far, near)

    @pl.when(core == 1)
    def _():
        fill(near, far)


def finish(place, pieces, finest, right, star, velocity_new, pressure_new, z2, f2, a2, b2, f3, a3, b3, f1, a1, b1, e1, p0, q0):
    gy = place[1]
    for j in range(8):
        peer = (gy + j) % 8
        for b in range(9):
            z2[b, 4 * j : 4 * j + 4, :] = pieces[peer, 96 + 4 * b : 100 + 4 * b, :]
    for b in range(9):
        packed = z2[b]
        lane = lane_of(packed) & 3
        for slot in range(4):
            part = jnp.where(lane == slot, packed, 0.0)
            part = part + turn(part, 1 if slot % 2 == 0 else -1, 1)
            part = part + turn(part, 2 if slot < 2 else -2, 1)
            f2[4 * b + slot] = part
            a2[4 * b + slot] = -COEFF * part
    sweep(b2, a2, f2, 1, 35, 1, 4)
    for k in range(2, 16):
        f3[k] = coarsen_pair(scaled_residual(b2, f2, 2 * k, 2, 1, 4), 1, 4)
        a3[k] = -COEFF * f3[k]
    sweep(b3, a3, f3, 3, 15, 2, 8)
    sweep(a3, b3, f3, 4, 14, 2, 8)
    sweep(b3, a3, f3, 5, 13, 2, 8)
    for i in range(6, 12):
        r3 = scaled_residual(b3, f3, i, 1, 2, 8)[0]
        line = jnp.sum(r3, axis=0, keepdims=True) * (COEFF / 32.0)
        fixed = b3[i] - line
        for r in (2 * i, 2 * i + 1):
            a2[r] = b2[r] + fixed
    sweep(b2, a2, f2, 13, 23, 1, 4)
    sweep(a2, b2, f2, 14, 22, 1, 4)
    for place_y, j in ((0, 0), (16, 1), (32, 7)):
        peer = (gy + j) % 8
        for g in range(6):
            packed = pieces[peer, 16 * g : 16 * g + 16, :]
            slots = 2 * (row_of(packed) & 1) + (lane_of(packed) & 1)
            for slot in range(4):
                x = 4 * g + slot
                if x < 3 or x > 20:
                    continue
                part = jnp.where(slots == slot, packed, 0.0)
                part = part + turn(part, 1 if slot % 2 == 0 else -1, 1)
                part = part + turn(part, 1 if slot < 2 else -1, 0)
                f1[x, place_y : place_y + 16, :] = part
                a1[x, place_y : place_y + 16, :] = -COEFF * part
    sweep(b1, a1, f1, 4, 20, 2, 2)
    for q in range(12):
        y = q if q < 8 else q + 20
        e1[:, 4 * q : 4 * q + 4, :] = jnp.broadcast_to(a2[14:22, y : y + 1, :], (8, 4, 128))
    for r in range(4, 20):
        a1[r] = b1[r] + e1[(r - 4) // 2]
    sweep(b1, a1, f1, 5, 19, 2, 2)
    sweep(a1, b1, f1, 6, 18, 2, 2)
    for i in range(22):
        coarse = a1[6 + (i + 1) // 2]
        p0[i, 0:24, :] = finest[i, 0:24, :] + coarse[0:24]
        p0[i, 24:32, :] = finest[i, 24:32, :] + coarse[40:48]
    sweep(q0, p0, right, 1, 21, 1, 1, 1)
    sweep(p0, q0, right, 2, 20, 1, 1, 1)
    for i in range(B):
        p = p0[3 + i]
        lane = lane_of(p)
        above = jnp.where(lane == 127, p, turn(p, -1, 1))
        below = jnp.where(lane == 0, p, turn(p, 1, 1))
        along_x = p0[4 + i] - p0[2 + i]
        along_y = turn(p, -1, 0) - turn(p, 1, 0)
        velocity_new[0, i] = star[0, i] - (0.5 * STEP) * along_x[0:B]
        velocity_new[1, i] = star[1, i] - (0.5 * STEP) * along_y[0:B]
        velocity_new[2, i] = star[2, i] - STEP * (above - below)[0:B]
        pressure_new[i] = p[0:B]


def swaps(count):
    near = [(i, i ^ 1) for i in range(count)]
    far = [(i, (((i + 1) ^ 1) - 1) % count) for i in range(count)]
    return near, far


def exchange(near_block, far_block, axis):
    near, far = swaps(lax.axis_size(axis))
    far_block = lax.ppermute(far_block, axis, far)
    return lax.ppermute(near_block, axis, near), far_block


def per_device(velocity, pressure, land_type, turbine_cells, surface_drag):
    gx = lax.axis_size("gx")
    gy = lax.axis_size("gy")
    place = jnp.stack([lax.axis_index("gx"), lax.axis_index("gy")]).astype(jnp.int32)
    near, far, drag = call(
        pack_x,
        [shape(SIDE, B, 128), shape(SIDE, B, 128), shape(B, B, 128)],
        [SMEM, VMEM, SMEM, VMEM, VMEM, VMEM],
    )(place, land_type, surface_drag, velocity, pressure, turbine_cells)
    near, far = exchange(near, far, "gx")
    wide_v, wide_p, wide_d, near, far = call(
        widen_x,
        [shape(3, VX, B, 128), shape(PX, B, 128), shape(PX, B, 128), shape(3, VX, 4, 128), shape(3, VX, 4, 128)],
        [SMEM] + [VMEM] * 5,
    )(place, velocity, pressure, drag, near, far)
    near, far = exchange(near, far, "gy")
    star, source, near, far = call(
        advance,
        [shape(3, B, B, 128), shape(PX - 2, B, 128), shape(2 * PX - 2, 8, 128), shape(2 * PX - 2, 8, 128)],
        [SMEM] + [VMEM] * 5,
        [(3, VX, 24, 128), (PX, 24, 128), (3, VX, 24, 128), (3, VX, 24, 128)],
    )(place, wide_v, wide_p, wide_d, near, far)
    near, far = exchange(near, far, "gy")
    finest, right, packed_one, packed_two = call(
        presmooth,
        [shape(22, 32, 128), shape(20, 32, 128), shape(2, B, 128), shape(4, 128)],
        [SMEM] + [VMEM] * 4,
        [(PX, 32, 128)] * 3 + [(12, 32, 128)] * 3,
    )(place, source, wide_p, near, far)
    near, far = exchange(packed_one, packed_one, "gx")
    blocks = lax.all_to_all(jnp.broadcast_to(packed_two[None], (gx, 4, 128)), "gx", 0, 0, tiled=True)
    (pieces,) = call(
        lambda *refs: pack_y(gx, *refs), [shape(gy, 136, 128)], [SMEM] + [VMEM] * 4
    )(place, blocks, packed_one, near, far)
    pieces = lax.all_to_all(pieces, "gy", 0, 0, tiled=True)
    velocity_new, pressure_new = call(
        finish,
        [shape(3, B, B, 128), shape(B, B, 128)],
        [SMEM] + [VMEM] * 4,
        [(9, 32, 128)]
        + [(36, 32, 128)] * 3
        + [(18, 32, 128)] * 3
        + [(24, 48, 128)] * 3
        + [(8, 48, 128)]
        + [(22, 32, 128)] * 2,
    )(place, pieces, finest, right, star)
    return velocity_new, pressure_new


def solution(mesh):
    in_specs = (
        P(None, "gx", "gy", None),
        P("gx", "gy", None),
        P("gx", "gy"),
        P("gx", "gy", None),
        P(),
    )
    out_specs = (P(None, "gx", "gy", None), P("gx", "gy", None))
    return jax.shard_map(
        per_device, mesh=mesh, in_specs=in_specs, out_specs=out_specs, check_vma=False
    )
```

time: 388 us -> 105 us (0.27); the launches traced: 382 us -> 104 us
  starting transfers between devices: 311 us -> 50 us
  other arithmetic: 17.8 us -> 0.08 us
  local copies, waits for them, and re-layouts: 20.3 us -> 4.09 us
  Pallas kernels: 0 us -> 15.7 us
  blocking collectives: 0 us -> 12.2 us
  waiting for transfers between devices: 29.9 us -> 21.2 us
    ppermute x68 -> x8, starting transfers between devices: 306 us -> 30.7 us  [the longest x4 19.7 us: exchange(): return (lax.ppermute(near_block, axis, near), far_block)]
    pallas_call x0 -> x6, Pallas kernels: none -> 15.7 us  [the longest x1 6.74 us: per_device(): call(finish, [shape(3, B, B, 128), shape(B, B, 128)], [SMEM] + [VMEM] * 4...]
    all_to_all x1, starting transfers between devices: 5.12 us -> 19.3 us  [per_device(): lax.all_to_all(jnp.broadcast_to(packed_two[None], (gx, 4, 128)), 'gx', 0,...]
    reshape x9 -> x0, local copies, waits for them, and re-layouts: 12.5 us -> none  [the longest x3 11.4 us: coarsen(): values.reshape(values.shape[0] // 2, 2, values.shape[1] // 2, 2, values.s...]
    all_to_all x0 -> x1, blocking collectives: none -> 12.2 us  [per_device(): pieces = lax.all_to_all(pieces, 'gy', 0, 0, tiled=True)]
    ppermute x68 -> x8, waiting for transfers between devices: 24.9 us -> 19.4 us  [the longest x4 14.6 us: exchange(): far_block = lax.ppermute(far_block, axis, far)]
    reduce_sum x5 -> x0, other arithmetic: 5.34 us -> none  [the longest x3 4.33 us: coarsen(): return values.reshape(values.shape[0] // 2, 2, values.shape[1] // 2, 2, v...]
  transfers between devices with their start and end apart: 69 -> 9, of which waited for: 20 -> 7; matrix products, arithmetic and copies ran while one was open for 7% -> 0% of each run, Pallas kernels for 0% -> 0%
where the time goes in v1:
time: 105 us; the launch traced here: 104 us
  starting transfers between devices  50 us (48%)
  waiting for transfers between devices  21.2 us (20%)
  Pallas kernels  15.7 us (15%)
  blocking collectives  12.2 us (12%)
  local copies, waits for them, and re-layouts  4.09 us (4%)
    ppermute x4, starting transfers between devices, exchange(): return (lax.ppermute(near_block, axis, near), far_block)  19.7 us
    all_to_all x1, starting transfers between devices, per_device(): lax.all_to_all(jnp.broadcast_to(packed_two[None], (gx, 4, 128)), 'gx', 0,...  19.3 us
    ppermute x4, waiting for transfers between devices, exchange(): far_block = lax.ppermute(far_block, axis, far)  14.6 us
    all_to_all x1, blocking collectives, per_device(): pieces = lax.all_to_all(pieces, 'gy', 0, 0, tiled=True)  12.2 us
    ppermute x4, starting transfers between devices, exchange(): far_block = lax.ppermute(far_block, axis, far)  11 us
    pallas_call x1, Pallas kernels, per_device(): call(finish, [shape(3, B, B, 128), shape(B, B, 128)], [SMEM] + [VMEM] * 4...  6.74 us
    ppermute x4, waiting for transfers between devices, exchange(): return (lax.ppermute(near_block, axis, near), far_block)  4.84 us
    pallas_call x1, Pallas kernels, per_device(): call(advance, [shape(3, B, B, 128), shape(PX - 2, B, 128), shape(2 * PX -...  4.23 us
  transfers between devices with their start and end apart: 9, of which 7 were waited for; matrix products, arithmetic and copies ran while one was open for 0% of the time, Pallas kernels for 0%

profile of v1, /device:TPU:1, one launch (start us, length us, event | category | flops | bytes accessed | tf_op | source)
XLA Modules:
  0.0 104.0 jit_solution(1156453007771685212)
XLA Ops:
  0.6 0.0 copy-start.5
  0.6 0.0 copy-start.6
  0.7 0.1 pad_add_fusion.place.refs_0_
  0.7 0.6 copy-done.5
  1.3 0.0 copy-done.6
  1.3 0.0 copy-start
  1.3 1.0 copy-done
  2.3 0.0 copy-start.2
  2.3 0.9 copy-done.2
  3.2 0.0 copy-start.4
  3.2 0.9 copy-done.4
  4.1 0.0 copy-start.1
  4.1 0.0 copy-start.3
  4.1 0.7 shard_map.68
  4.9 8.8 %collective-permute-start = (f32[41,16,128]{2,1,0:T(8,128)S(1)}, f32[41,16,128]{2,1,0:T(8,128)S(1)}, u32[]{:S(2)}, u32[]{:S(2)}) collective-permute-start(f32[41,16,128]{2,1,0:T(8,128)S(1)} %get-tuple-element.19), channel_id=1, source_target_pairs={{0,8},{8,0},{16,24},{24,16},{32,40},{40,32},{48,56},{56,48},{64,72... | collective-permute-start | bytes 1007624 | tf_op jit(solution)/shard_map/ppermute | solution.py:399
  13.6 1.9 %collective-permute-start.1 = (f32[41,16,128]{2,1,0:T(8,128)S(1)}, f32[41,16,128]{2,1,0:T(8,128)S(1)}, u32[]{:S(2)}, u32[]{:S(2)}) collective-permute-start(f32[41,16,128]{2,1,0:T(8,128)S(1)} %get-tuple-element.20), channel_id=1, source_target_pairs={{0,504},{8,16},{16,8},{24,32},{32,24},{40,48},{48,40},{56,64},{64,... | collective-permute-start | bytes 1007624 | tf_op jit(solution)/shard_map/ppermute | solution.py:398
  15.6 0.0 collective-permute-done.near
  15.6 6.5 %collective-permute-done.1.far = f32[41,16,128]{2,1,0:T(8,128)S(1)} collective-permute-done((f32[41,16,128]{2,1,0:T(8,128)S(1)}, f32[41,16,128]{2,1,0:T(8,128)S(1)}, u32[]{:S(2)}, u32[]{:S(2)}) %collective-permute-start.1) | collective-permute-done | bytes 335904 | tf_op jit(solution)/shard_map/ppermute | solution.py:398
  22.1 0.0 copy-done.1
  22.1 0.0 copy-done.3
  22.1 0.7 shard_map.69
  22.9 1.9 %collective-permute-start.2 = (f32[3,34,4,128]{3,2,1,0:T(4,128)S(1)}, f32[3,34,4,128]{3,2,1,0:T(4,128)S(1)}, u32[]{:S(2)}, u32[]{:S(2)}) collective-permute-start(f32[3,34,4,128]{3,2,1,0:T(4,128)S(1)} %get-tuple-element.24), channel_id=1, source_target_pairs={{0,1},{1,0},{2,3},{3,2},{4,5},{5,4},{6,7},{7,6},{8,9},{9,8},{10,11... | collective-permute-start | bytes 626696 | tf_op jit(solution)/shard_map/ppermute | solution.py:399
  24.8 1.9 %collective-permute-start.3 = (f32[3,34,4,128]{3,2,1,0:T(4,128)S(1)}, f32[3,34,4,128]{3,2,1,0:T(4,128)S(1)}, u32[]{:S(2)}, u32[]{:S(2)}) collective-permute-start(f32[3,34,4,128]{3,2,1,0:T(4,128)S(1)} %get-tuple-element.25), channel_id=1, source_target_pairs={{0,7},{1,2},{2,1},{3,4},{4,3},{5,6},{6,5},{7,0},{8,15},{9,10},{10,... | collective-permute-start | bytes 626696 | tf_op jit(solution)/shard_map/ppermute | solution.py:398
  26.7 2.7 %collective-permute-done.2.near = f32[3,34,4,128]{3,2,1,0:T(4,128)S(1)} collective-permute-done((f32[3,34,4,128]{3,2,1,0:T(4,128)S(1)}, f32[3,34,4,128]{3,2,1,0:T(4,128)S(1)}, u32[]{:S(2)}, u32[]{:S(2)}) %collective-permute-start.2) | collective-permute-done | bytes 208928 | tf_op jit(solution)/shard_map/ppermute | solution.py:399
  29.4 4.0 %collective-permute-done.3.far = f32[3,34,4,128]{3,2,1,0:T(4,128)S(1)} collective-permute-done((f32[3,34,4,128]{3,2,1,0:T(4,128)S(1)}, f32[3,34,4,128]{3,2,1,0:T(4,128)S(1)}, u32[]{:S(2)}, u32[]{:S(2)}) %collective-permute-start.3) | collective-permute-done | bytes 208928 | tf_op jit(solution)/shard_map/ppermute | solution.py:398
  33.4 4.2 %shard_map.70 = (f32[3,16,16,128]{3,2,1,0:T(8,128)S(1)}, f32[28,16,128]{2,1,0:T(8,128)S(1)}, f32[58,8,128]{2,1,0:T(8,128)S(1)}, f32[58,8,128]{2,1,0:T(8,128)S(1)}) custom-call(s32[2]{0:T(128)S(1)} %pad_add_fusion.place.refs_0_, f32[3,34,16,128]{3,2,1,0:T(8,128)S(1)} %get-tuple-element.21.wide_v, f32[30,16,128]{2,1,0:T(8,128)S(1)} %get-tuple-element.22.wide_p, ...), custom_call_target="tpu_custom_call" | custom-call | tf_op jit(solution)/shard_map/pallas_call | solution.py:418
  37.7 2.4 %collective-permute-start.4 = (f32[58,8,128]{2,1,0:T(8,128)S(1)}, f32[58,8,128]{2,1,0:T(8,128)S(1)}, u32[]{:S(2)}, u32[]{:S(2)}) collective-permute-start(f32[58,8,128]{2,1,0:T(8,128)S(1)} %get-tuple-element.27), channel_id=1, source_target_pairs={{0,1},{1,0},{2,3},{3,2},{4,5},{5,4},{6,7},{7,6},{8,9},{9,8},{10,11... | collective-permute-start | bytes 712712 | tf_op jit(solution)/shard_map/ppermute | solution.py:399
  40.1 3.6 %collective-permute-start.5 = (f32[58,8,128]{2,1,0:T(8,128)S(1)}, f32[58,8,128]{2,1,0:T(8,128)S(1)}, u32[]{:S(2)}, u32[]{:S(2)}) collective-permute-start(f32[58,8,128]{2,1,0:T(8,128)S(1)} %get-tuple-element.28), channel_id=1, source_target_pairs={{0,7},{1,2},{2,1},{3,4},{4,3},{5,6},{6,5},{7,0},{8,15},{9,10},{10,... | collective-permute-start | bytes 712712 | tf_op jit(solution)/shard_map/ppermute | solution.py:398
  43.7 1.3 %collective-permute-done.4.near = f32[58,8,128]{2,1,0:T(8,128)S(1)} collective-permute-done((f32[58,8,128]{2,1,0:T(8,128)S(1)}, f32[58,8,128]{2,1,0:T(8,128)S(1)}, u32[]{:S(2)}, u32[]{:S(2)}) %collective-permute-start.4) | collective-permute-done | bytes 237600 | tf_op jit(solution)/shard_map/ppermute | solution.py:399
  45.1 4.0 %collective-permute-done.5.far = f32[58,8,128]{2,1,0:T(8,128)S(1)} collective-permute-done((f32[58,8,128]{2,1,0:T(8,128)S(1)}, f32[58,8,128]{2,1,0:T(8,128)S(1)}, u32[]{:S(2)}, u32[]{:S(2)}) %collective-permute-start.5) | collective-permute-done | bytes 237600 | tf_op jit(solution)/shard_map/ppermute | solution.py:398
  49.0 2.7 %shard_map.71 = (f32[22,32,128]{2,1,0:T(8,128)S(1)}, f32[20,32,128]{2,1,0:T(8,128)S(1)}, f32[2,16,128]{2,1,0:T(8,128)S(1)}, f32[4,128]{1,0:T(4,128)S(1)}) custom-call(s32[2]{0:T(128)S(1)} %pad_add_fusion.place.refs_0_, f32[28,16,128]{2,1,0:T(8,128)S(1)} %get-tuple-element.26.source, f32[30,16,128]{2,1,0:T(8,128)S(1)} %get-tuple-element.22.wide_p, ...), custom_call_target="tpu_custom_call" | custom-call | tf_op jit(solution)/shard_map/pallas_call | solution.py:425
  51.7 0.7 broadcast_in_dim.2
  52.4 19.3 %all-to-all-start = ((f32[64,4,128]{2,1,0:T(4,128)}), f32[64,4,128]{2,1,0:T(4,128)S(1)}, u32[]{:S(2)}, u32[]{:S(2)}) async-start(f32[64,4,128]{2,1,0:T(4,128)} %broadcast_in_dim.2), calls=%async_computation | async-start | bytes 262144 | tf_op jit(solution)/shard_map/all_to_all | solution.py:432
  71.7 3.5 %collective-permute-start.7 = (f32[2,16,128]{2,1,0:T(8,128)S(1)}, f32[2,16,128]{2,1,0:T(8,128)S(1)}, u32[]{:S(2)}, u32[]{:S(2)}) collective-permute-start(f32[2,16,128]{2,1,0:T(8,128)S(1)} %get-tuple-element.30.refs_2_), channel_id=1, source_target_pairs={{0,504},{8,16},{16,8},{24,32},{32,24},{40,48},{48,40},{56,64},{64,... | collective-permute-start | bytes 49160 | tf_op jit(solution)/shard_map/ppermute | solution.py:398
  75.2 6.6 %collective-permute-start.6 = (f32[2,16,128]{2,1,0:T(8,128)S(1)}, f32[2,16,128]{2,1,0:T(8,128)S(1)}, u32[]{:S(2)}, u32[]{:S(2)}) collective-permute-start(f32[2,16,128]{2,1,0:T(8,128)S(1)} %get-tuple-element.30.refs_2_), channel_id=1, source_target_pairs={{0,8},{8,0},{16,24},{24,16},{32,40},{40,32},{48,56},{56,48},{64,72... | collective-permute-start | bytes 49160 | tf_op jit(solution)/shard_map/ppermute | solution.py:399
  81.8 0.0 collective-permute-done.7.refs_4_
  81.8 0.8 collective-permute-done.6.refs_3_
  82.6 1.8 %all-to-all-done.refs_1_ = f32[64,4,128]{2,1,0:T(4,128)S(1)} async-done(((f32[64,4,128]{2,1,0:T(4,128)}), f32[64,4,128]{2,1,0:T(4,128)S(1)}, u32[]{:S(2)}, u32[]{:S(2)}) %all-to-all-start) | async-done | bytes 131104 | tf_op jit(solution)/shard_map/all_to_all | solution.py:432
  84.4 0.6 shard_map.72
  85.1 12.2 %all_to_all.10.pieces = f32[8,136,128]{2,1,0:T(8,128)S(1)} all-to-all(f32[8,136,128]{2,1,0:T(8,128)S(1)} %shard_map.72), channel_id=1, replica_groups=mesh['gx'=64,'gy'=8] {'gy'}, dimensions={0} | all-to-all | bytes 1114112 | tf_op jit(solution)/shard_map/all_to_all | solution.py:436
  97.3 6.7 %shard_map.73 = (f32[3,16,16,128]{3,2,1,0:T(8,128)}, f32[16,16,128]{2,1,0:T(8,128)}) custom-call(s32[2]{0:T(128)S(1)} %pad_add_fusion.place.refs_0_, f32[8,136,128]{2,1,0:T(8,128)S(1)} %all_to_all.10.pieces, f32[22,32,128]{2,1,0:T(8,128)S(1)} %get-tuple-element.31.finest, f32[20,32,128]{2,1,0:T(8,128)S(1)} %get-tuple-element.32.right, ...), custom_call_target="tpu_custom_call" | custom-call | tf_op jit(solution)/shard_map/pallas_call | solution.py:437
Async XLA Ops:
  0.6 0.7 copy-start.5
  0.6 0.7 copy-start.6
  1.3 1.0 copy-start
  2.3 0.9 copy-start.2
  3.2 0.9 copy-start.4
  4.1 18.0 %copy-start.1 = (f32[3,16,16,128]{3,2,1,0:T(8,128)S(1)}, f32[3,16,16,128]{3,2,1,0:T(8,128)}, u32[]{:S(2)}) copy-start(f32[3,16,16,128]{3,2,1,0:T(8,128)} %velocity.3) | copy-start | bytes 1179652
  4.1 18.0 %copy-start.3 = (f32[16,16,128]{2,1,0:T(8,128)S(1)}, f32[16,16,128]{2,1,0:T(8,128)}, u32[]{:S(2)}) copy-start(f32[16,16,128]{2,1,0:T(8,128)} %pressure.3) | copy-start | bytes 393220
  4.9 10.7 %collective-permute-start = (f32[41,16,128]{2,1,0:T(8,128)S(1)}, f32[41,16,128]{2,1,0:T(8,128)S(1)}, u32[]{:S(2)}, u32[]{:S(2)}) collective-permute-start(f32[41,16,128]{2,1,0:T(8,128)S(1)} %get-tuple-element.19), channel_id=1, source_target_pairs={{0,8},{8,0},{16,24},{24,16},{32,40},{40,32},{48,56},{56,48},{64,72... | collective-permute-start | bytes 1007624 | tf_op jit(solution)/shard_map/ppermute | solution.py:399
  13.6 8.5 %collective-permute-start.1 = (f32[41,16,128]{2,1,0:T(8,128)S(1)}, f32[41,16,128]{2,1,0:T(8,128)S(1)}, u32[]{:S(2)}, u32[]{:S(2)}) collective-permute-start(f32[41,16,128]{2,1,0:T(8,128)S(1)} %get-tuple-element.20), channel_id=1, source_target_pairs={{0,504},{8,16},{16,8},{24,32},{32,24},{40,48},{48,40},{56,64},{64,... | collective-permute-start | bytes 1007624 | tf_op jit(solution)/shard_map/ppermute | solution.py:398
  22.9 6.5 %collective-permute-start.2 = (f32[3,34,4,128]{3,2,1,0:T(4,128)S(1)}, f32[3,34,4,128]{3,2,1,0:T(4,128)S(1)}, u32[]{:S(2)}, u32[]{:S(2)}) collective-permute-start(f32[3,34,4,128]{3,2,1,0:T(4,128)S(1)} %get-tuple-element.24), channel_id=1, source_target_pairs={{0,1},{1,0},{2,3},{3,2},{4,5},{5,4},{6,7},{7,6},{8,9},{9,8},{10,11... | collective-permute-start | bytes 626696 | tf_op jit(solution)/shard_map/ppermute | solution.py:399
  24.8 8.7 %collective-permute-start.3 = (f32[3,34,4,128]{3,2,1,0:T(4,128)S(1)}, f32[3,34,4,128]{3,2,1,0:T(4,128)S(1)}, u32[]{:S(2)}, u32[]{:S(2)}) collective-permute-start(f32[3,34,4,128]{3,2,1,0:T(4,128)S(1)} %get-tuple-element.25), channel_id=1, source_target_pairs={{0,7},{1,2},{2,1},{3,4},{4,3},{5,6},{6,5},{7,0},{8,15},{9,10},{10,... | collective-permute-start | bytes 626696 | tf_op jit(solution)/shard_map/ppermute | solution.py:398
  37.7 7.4 %collective-permute-start.4 = (f32[58,8,128]{2,1,0:T(8,128)S(1)}, f32[58,8,128]{2,1,0:T(8,128)S(1)}, u32[]{:S(2)}, u32[]{:S(2)}) collective-permute-start(f32[58,8,128]{2,1,0:T(8,128)S(1)} %get-tuple-element.27), channel_id=1, source_target_pairs={{0,1},{1,0},{2,3},{3,2},{4,5},{5,4},{6,7},{7,6},{8,9},{9,8},{10,11... | collective-permute-start | bytes 712712 | tf_op jit(solution)/shard_map/ppermute | solution.py:399
  40.1 9.0 %collective-permute-start.5 = (f32[58,8,128]{2,1,0:T(8,128)S(1)}, f32[58,8,128]{2,1,0:T(8,128)S(1)}, u32[]{:S(2)}, u32[]{:S(2)}) collective-permute-start(f32[58,8,128]{2,1,0:T(8,128)S(1)} %get-tuple-element.28), channel_id=1, source_target_pairs={{0,7},{1,2},{2,1},{3,4},{4,3},{5,6},{6,5},{7,0},{8,15},{9,10},{10,... | collective-permute-start | bytes 712712 | tf_op jit(solution)/shard_map/ppermute | solution.py:398
  52.4 32.1 %all-to-all-start = ((f32[64,4,128]{2,1,0:T(4,128)}), f32[64,4,128]{2,1,0:T(4,128)S(1)}, u32[]{:S(2)}, u32[]{:S(2)}) async-start(f32[64,4,128]{2,1,0:T(4,128)} %broadcast_in_dim.2), calls=%async_computation | async-start | bytes 262144 | tf_op jit(solution)/shard_map/all_to_all | solution.py:432
  71.7 10.1 %collective-permute-start.7 = (f32[2,16,128]{2,1,0:T(8,128)S(1)}, f32[2,16,128]{2,1,0:T(8,128)S(1)}, u32[]{:S(2)}, u32[]{:S(2)}) collective-permute-start(f32[2,16,128]{2,1,0:T(8,128)S(1)} %get-tuple-element.30.refs_2_), channel_id=1, source_target_pairs={{0,504},{8,16},{16,8},{24,32},{32,24},{40,48},{48,40},{56,64},{64,... | collective-permute-start | bytes 49160 | tf_op jit(solution)/shard_map/ppermute | solution.py:398
  75.2 7.4 %collective-permute-start.6 = (f32[2,16,128]{2,1,0:T(8,128)S(1)}, f32[2,16,128]{2,1,0:T(8,128)S(1)}, u32[]{:S(2)}, u32[]{:S(2)}) collective-permute-start(f32[2,16,128]{2,1,0:T(8,128)S(1)} %get-tuple-element.30.refs_2_), channel_id=1, source_target_pairs={{0,8},{8,0},{16,24},{24,16},{32,40},{40,32},{48,56},{56,48},{64,72... | collective-permute-start | bytes 49160 | tf_op jit(solution)/shard_map/ppermute | solution.py:399

commit v2 on v1

--- a/solution.py
+++ b/solution.py
@@ -17,6 +17,18 @@
 WINDOW = 4
 VMEM = pl.BlockSpec(memory_space=pltpu.VMEM)
 SMEM = pl.BlockSpec(memory_space=pltpu.SMEM)
+ANY = pl.BlockSpec(memory_space=pl.ANY)
+UNITS = (
+    (0, 0, 5, 18, True),
+    (18, 0, 5, 18, False),
+    (36, 0, 1, 4, False),
+    (40, 0, 23, 4, False),
+    (44, 1, 5, 20, True),
+    (64, 1, 5, 20, False),
+    (84, 1, 1, 4, False),
+    (88, 1, 25, 4, False),
+)
+N_UNITS = 92
 F32 = jnp.float32
 
 
@@ -30,7 +42,7 @@
         out_shape=outs,
         in_specs=specs,
         out_specs=[VMEM] * len(outs),
-        scratch_shapes=[pltpu.VMEM(s, F32) for s in scratch],
+        scratch_shapes=[pltpu.VMEM(s, F32) if isinstance(s, tuple) else s for s in scratch],
         compiler_params=pltpu.CompilerParams(vmem_limit_bytes=48 * 1024 * 1024),
     )
 
@@ -51,36 +63,54 @@
     return pltpu.roll(values, amount % values.shape[dim], dim)
 
 
-def pack_x(place, land, drag_table, velocity, pressure, turbine, near, far, drag):
+def pack_x(place, drag_table, land, velocity, pressure, turbine, near, far, drag, kinds_ref, cells_ref, sems):
     core = place[0] % 2
-    kinds = land[...]
+    copies = [
+        pltpu.make_async_copy(land, kinds_ref, sems.at[0]),
+        pltpu.make_async_copy(turbine, cells_ref, sems.at[1]),
+    ]
+    for side, out in ((0, near), (1, far)):
+        high = (core + side) % 2 == 0
+        start = jnp.where(high, B - VH, 0)
+        for a in range(3):
+            copies.append(
+                pltpu.make_async_copy(
+                    velocity.at[a, pl.ds(start, VH)], out.at[pl.ds(a * VH, VH)], sems.at[2 + 4 * side + a]
+                )
+            )
+        start = jnp.where(high, B - PH, 0)
+        copies.append(
+            pltpu.make_async_copy(
+                pressure.at[pl.ds(start, PH)], out.at[pl.ds(3 * VH, PH)], sems.at[5 + 4 * side]
+            )
+        )
+    for copy in copies:
+        copy.start()
+    copies[0].wait()
+    kinds = kinds_ref[...]
     ground = jnp.zeros(kinds.shape, F32)
     for kind in range(16):
         ground = jnp.where(kinds == kind, drag_table[kind], ground)
     square = lax.broadcasted_iota(jnp.int32, (B, B), 0) == lax.broadcasted_iota(jnp.int32, (B, B), 1)
+    copies[1].wait()
     for i in range(B):
         row = jnp.broadcast_to(ground[i : i + 1, :], (B, B))
         column = jnp.sum(jnp.where(square, row, 0.0), axis=1, keepdims=True)
-        cells = turbine[i].astype(F32)
+        cells = cells_ref[i].astype(F32)
         drag[i] = 2.0 * cells + jnp.where(lane_of(cells) == 0, column, 0.0)
 
-    def fill(out, high):
-        start = B - VH if high else 0
-        for a in range(3):
-            out[a * VH : (a + 1) * VH] = velocity[a, start : start + VH]
-        start = B - PH if high else 0
-        out[3 * VH : 3 * VH + PH] = pressure[start : start + PH]
-        out[3 * VH + PH : SIDE] = drag[start : start + PH]
-
     @pl.when(core == 0)
     def _():
-        fill(near, True)
-        fill(far, False)
+        near[3 * VH + PH : SIDE] = drag[B - PH :]
+        far[3 * VH + PH : SIDE] = drag[:PH]
 
     @pl.when(core == 1)
     def _():
-        fill(near, False)
-        fill(far, True)
+        near[3 * VH + PH : SIDE] = drag[:PH]
+        far[3 * VH + PH : SIDE] = drag[B - PH :]
+
+    for copy in copies[2:]:
+        copy.wait()
 
 
 def widen_x(place, velocity, pressure, drag, near, far, wide_v, wide_p, wide_d, near_y, far_y):
@@ -109,10 +139,17 @@
         fill(near, far)
 
     def send(up, down):
-        up[...] = wide_v[:, :, B - 4 :, :]
-        down[...] = wide_v[:, :, :4, :]
-        up[0, 2 : 2 + PX, 0:1, :] = wide_d[:, B - 1 :, :]
-        down[0, 2 : 2 + PX, 3:4, :] = wide_d[:, 0:1, :]
+        for g in range(8):
+            for j in range(4):
+                x = 1 + 4 * g + j
+                for a in range(3):
+                    rows = slice(10 * j + 3 * a, 10 * j + 3 * a + 3)
+                    up[g, rows, :] = wide_v[a, x, B - 3 :, :]
+                    down[g, rows, :] = wide_v[a, x, :3, :]
+                row = slice(10 * j + 9, 10 * j + 10)
+                d = min(max(x - 2, 0), PX - 1)
+                up[g, row, :] = wide_d[d, B - 1 :, :]
+                down[g, row, :] = wide_d[d, 0:1, :]
 
     @pl.when(odd == 0)
     def _():
@@ -129,11 +166,17 @@
     dr[:, 0:B, :] = wide_d[...]
 
     def fill(low, high):
-        v[:, :, B : B + 4, :] = high[...]
-        v[:, :, B + 4 : B + 8, :] = low[...]
-        dr[:, B : B + 8, :] = jnp.zeros((PX, 8, 128), F32)
-        dr[:, B : B + 1, :] = high[0, 2 : 2 + PX, 3:4, :]
-        dr[:, B + 7 : B + 8, :] = low[0, 2 : 2 + PX, 0:1, :]
+        for g in range(8):
+            for j in range(4):
+                x = 1 + 4 * g + j
+                for a in range(3):
+                    rows = slice(10 * j + 3 * a, 10 * j + 3 * a + 3)
+                    v[a, x, B : B + 3, :] = high[g, rows, :]
+                    v[a, x, B + 5 : B + 8, :] = low[g, rows, :]
+                if 2 <= x < 2 + PX:
+                    row = slice(10 * j + 9, 10 * j + 10)
+                    dr[x - 2, B : B + 1, :] = high[g, row, :]
+                    dr[x - 2, B + 7 : B + 8, :] = low[g, row, :]
 
     @pl.when(odd == 0)
     def _():
@@ -203,10 +246,11 @@
         source[i - 3] = ((along_x + along_y + (above - below)) / STEP)[0:B]
 
     def send(up, down):
-        up[0 : PX - 2] = source[:, B - 8 :, :]
-        up[PX - 2 :] = wide_p[:, B - 8 :, :]
-        down[0 : PX - 2] = source[:, :8, :]
-        down[PX - 2 :] = wide_p[:, :8, :]
+        for message, outer, inner in ((up, B - 4, B - 8), (down, 0, 4)):
+            for unit, kind, start, count, deep in UNITS:
+                field = source if kind == 0 else wide_p
+                first = inner if deep else outer
+                message[unit : unit + count] = field[start : start + count, first : first + 4, :]
 
     @pl.when(odd == 0)
     def _():
@@ -252,15 +296,17 @@
 
 def presmooth(place, source, wide_p, near, far, finest, right, packed_one, packed_two, p, s, q, f1, a1, b1):
     odd = place[1] % 2
-    nx = PX - 2
     p[:, 0:B, :] = wide_p[...]
     s[1 : PX - 1, 0:B, :] = source[...]
 
     def fill(low, high):
-        s[1 : PX - 1, B : B + 8, :] = high[:nx]
-        s[1 : PX - 1, B + 8 : B + 16, :] = low[:nx]
-        p[:, B : B + 8, :] = high[nx:]
-        p[:, B + 8 : B + 16, :] = low[nx:]
+        for unit, kind, start, count, deep in UNITS:
+            field = s if kind == 0 else p
+            rows = slice(start + 1 - kind, start + 1 - kind + count)
+            first = B + 4 if deep else B
+            field[rows, first : first + 4, :] = high[unit : unit + count]
+            first = B + 8 if deep else B + 12
+            field[rows, first : first + 4, :] = low[unit : unit + count]
 
     @pl.when(odd == 0)
     def _():
@@ -272,8 +318,10 @@
 
     sweep(q, p, s, 1, PX - 1, 1, 1)
     sweep(p, q, s, 2, PX - 2, 1, 1)
-    finest[...] = p[4 : PX - 4]
-    right[...] = s[5 : PX - 5]
+    for out, field, first in ((finest, p, 4), (right, s, 5)):
+        out[:, 0:B, :] = field[first : PX - first, 0:B, :]
+        out[:, B : B + 4, :] = field[first : PX - first, B : B + 4, :]
+        out[:, B + 4 : B + 8, :] = field[first : PX - first, B + 12 : B + 16, :]
     for k in range(12):
         f1[k] = coarsen_pair(scaled_residual(p, s, 3 + 2 * k, 2, 1, 1), 1, 1)
     a1[...] = -COEFF * f1[...]
@@ -281,8 +329,9 @@
     f2 = [coarsen_pair(scaled_residual(b1, f1, 2 + 2 * k, 2, 2, 2), 2, 2) for k in range(4)]
     lane = lane_of(f2[0]) & 3
     two = jnp.where(lane == 0, f2[0], jnp.where(lane == 1, f2[1], jnp.where(lane == 2, f2[2], f2[3])))
-    for y in range(4):
-        packed_two[y : y + 1, :] = two[4 * y : 4 * y + 1, :]
+    four = jnp.concatenate([two[4 * y : 4 * y + 1, :] for y in range(4)], axis=0)
+    for k in range(packed_two.shape[0]):
+        packed_two[k] = four
     for g in range(2):
         rows = [f1[2 + 4 * g + j][0:B] for j in range(4)]
         slot = 2 * (row_of(rows[0]) & 1) + (lane_of(rows[0]) & 1)
@@ -291,21 +340,18 @@
         )
 
 
-def pack_y(peers, place, blocks, own, near, far, out):
+def pack_y(peers, place, blocks, own, near, far, strips, window, near_y, far_y):
     core = place[0] % 2
+    odd = place[1] % 2
     for j in range(2 * WINDOW + 1):
         piece = blocks[(place[0] + (peers - WINDOW + j)) % peers]
         for k in range(8):
-            out[k, 96 + 4 * j : 100 + 4 * j, :] = piece
-    for k in range(8):
-        out[k, 132:136, :] = jnp.zeros((4, 128), F32)
+            strips[k, j] = piece
+    window[2:4] = own[...]
 
     def fill(low, high):
-        for k in range(8):
-            for g in range(2):
-                out[k, 16 * g : 16 * g + 16, :] = low[g]
-                out[k, 32 + 16 * g : 48 + 16 * g, :] = own[g]
-                out[k, 64 + 16 * g : 80 + 16 * g, :] = high[g]
+        window[0:2] = low[...]
+        window[4:6] = high[...]
 
     @pl.when(core == 0)
     def _():
@@ -315,63 +361,119 @@
     def _():
         fill(near, far)
 
-
-def finish(place, pieces, finest, right, star, velocity_new, pressure_new, z2, f2, a2, b2, f3, a3, b3, f1, a1, b1, e1, p0, q0):
+    def send(up, down):
+        up[...] = window[:, 4:16, :]
+        down[...] = window[:, 0:12, :]
+
+    @pl.when(odd == 0)
+    def _():
+        send(near_y, far_y)
+
+    @pl.when(odd == 1)
+    def _():
+        send(far_y, near_y)
+
+
+def packed_neighbours(ref, b, dx, dy, dz):
+    p = ref[b]
+    before = ref[max(b - 1, 0)]
+    after = ref[min(b + 1, 2 * WINDOW)]
+    lane = lane_of(p)
+    slot = lane & 3
+    left = jnp.where(slot < dx, turn(before, dx - 4, 1), turn(p, dx, 1))
+    right = jnp.where(slot >= 4 - dx, turn(after, 4 - dx, 1), turn(p, -dx, 1))
+    below = jnp.where(lane < dz, p, turn(p, dz, 1))
+    above = jnp.where(lane >= 128 - dz, p, turn(p, -dz, 1))
+    return p, (left + right) + (turn(p, dy, 0) + turn(p, -dy, 0)) + 4.0 * (below + above)
+
+
+def packed_sweep(dst, src, right, blocks, dx, dy, dz):
+    for b in blocks:
+        p, around = packed_neighbours(src, b, dx, dy, dz)
+        dst[b] = 0.2 * p + COEFF * (around - right[b])
+
+
+def packed_residual(src, right, b, dx, dy, dz):
+    p, around = packed_neighbours(src, b, dx, dy, dz)
+    return right[b] - around + 12.0 * p
+
+
+def without_middle(values):
+    return jnp.concatenate([values[..., 0:24, :], values[..., 32:40, :]], axis=-2)
+
+
+def finish(place, strips, window, near, far, finest, right, star, velocity_new, pressure_new, f2, a2, b2, f3, a3, b3, g1, f1, a1, b1, c1, d1, e1, p0, q0):
     gy = place[1]
+    odd = gy % 2
     for j in range(8):
         peer = (gy + j) % 8
-        for b in range(9):
-            z2[b, 4 * j : 4 * j + 4, :] = pieces[peer, 96 + 4 * b : 100 + 4 * b, :]
+        for b in range(2 * WINDOW + 1):
+            f2[b, 4 * j : 4 * j + 4, :] = strips[peer, b]
     for b in range(9):
-        packed = z2[b]
-        lane = lane_of(packed) & 3
-        for slot in range(4):
-            part = jnp.where(lane == slot, packed, 0.0)
-            part = part + turn(part, 1 if slot % 2 == 0 else -1, 1)
-            part = part + turn(part, 2 if slot < 2 else -2, 1)
-            f2[4 * b + slot] = part
-            a2[4 * b + slot] = -COEFF * part
-    sweep(b2, a2, f2, 1, 35, 1, 4)
-    for k in range(2, 16):
-        f3[k] = coarsen_pair(scaled_residual(b2, f2, 2 * k, 2, 1, 4), 1, 4)
-        a3[k] = -COEFF * f3[k]
-    sweep(b3, a3, f3, 3, 15, 2, 8)
-    sweep(a3, b3, f3, 4, 14, 2, 8)
-    sweep(b3, a3, f3, 5, 13, 2, 8)
-    for i in range(6, 12):
-        r3 = scaled_residual(b3, f3, i, 1, 2, 8)[0]
-        line = jnp.sum(r3, axis=0, keepdims=True) * (COEFF / 32.0)
-        fixed = b3[i] - line
-        for r in (2 * i, 2 * i + 1):
-            a2[r] = b2[r] + fixed
-    sweep(b2, a2, f2, 13, 23, 1, 4)
-    sweep(a2, b2, f2, 14, 22, 1, 4)
-    for place_y, j in ((0, 0), (16, 1), (32, 7)):
-        peer = (gy + j) % 8
-        for g in range(6):
-            packed = pieces[peer, 16 * g : 16 * g + 16, :]
-            slots = 2 * (row_of(packed) & 1) + (lane_of(packed) & 1)
-            for slot in range(4):
-                x = 4 * g + slot
-                if x < 3 or x > 20:
-                    continue
-                part = jnp.where(slots == slot, packed, 0.0)
-                part = part + turn(part, 1 if slot % 2 == 0 else -1, 1)
-                part = part + turn(part, 1 if slot < 2 else -1, 0)
-                f1[x, place_y : place_y + 16, :] = part
-                a1[x, place_y : place_y + 16, :] = -COEFF * part
+        a2[b] = -COEFF * f2[b]
+    packed_sweep(b2, a2, f2, range(9), 1, 1, 4)
+    for b in range(1, 8):
+        total = packed_residual(b2, f2, b, 1, 1, 4)
+        lane = lane_of(total)
+        total = total + jnp.where((lane & 1) == 0, turn(total, -1, 1), turn(total, 1, 1))
+        total = total + jnp.where((lane & 4) == 0, turn(total, -4, 1), turn(total, 4, 1))
+        row = row_of(total)
+        total = total + jnp.where((row & 1) == 0, turn(total, -1, 0), turn(total, 1, 0))
+        f3[b] = 0.5 * total
+        a3[b] = (-0.5 * COEFF) * total
+    packed_sweep(b3, a3, f3, range(1, 8), 2, 2, 8)
+    packed_sweep(a3, b3, f3, range(2, 7), 2, 2, 8)
+    packed_sweep(b3, a3, f3, range(2, 7), 2, 2, 8)
+    for b in range(3, 6):
+        line = jnp.sum(packed_residual(b3, f3, b, 2, 2, 8), axis=0, keepdims=True) * (COEFF / 32.0)
+        a2[b] = b2[b] + (b3[b] - line)
+    packed_sweep(b2, a2, f2, range(3, 6), 1, 1, 4)
+    packed_sweep(a2, b2, f2, range(3, 6), 1, 1, 4)
+    g1[:, 0:B, :] = window[...]
+
+    def fill(low, high):
+        g1[:, B : B + 12, :] = high[...]
+        g1[:, B + 12 : B + 24, :] = low[...]
+
+    @pl.when(odd == 0)
+    def _():
+        fill(far, near)
+
+    @pl.when(odd == 1)
+    def _():
+        fill(near, far)
+
+    for x in range(3, 21):
+        packed = g1[x // 4]
+        slots = 2 * (row_of(packed) & 1) + (lane_of(packed) & 1)
+        slot = x % 4
+        part = jnp.where(slots == slot, packed, 0.0)
+        part = part + turn(part, 1 if slot % 2 == 0 else -1, 1)
+        part = part + turn(part, 1 if slot < 2 else -1, 0)
+        f1[x] = part
+        a1[x] = -COEFF * part
     sweep(b1, a1, f1, 4, 20, 2, 2)
-    for q in range(12):
-        y = q if q < 8 else q + 20
-        e1[:, 4 * q : 4 * q + 4, :] = jnp.broadcast_to(a2[14:22, y : y + 1, :], (8, 4, 128))
+    for k in range(8):
+        block = a2[3 + (k + 2) // 4]
+        slot = (k + 2) % 4
+        low, high = block[0:8], block[24:32]
+        part = jnp.where(row_of(low) < 6, low, high)
+        part = jnp.where((lane_of(part) & 3) == slot, part, 0.0)
+        part = part + turn(part, 1 if slot % 2 == 0 else -1, 1)
+        part = part + turn(part, 2 if slot < 2 else -2, 1)
+        for q in range(8):
+            e1[k, 4 * q : 4 * q + 4, :] = jnp.broadcast_to(part[q : q + 1, :], (4, 128))
     for r in range(4, 20):
-        a1[r] = b1[r] + e1[(r - 4) // 2]
-    sweep(b1, a1, f1, 5, 19, 2, 2)
-    sweep(a1, b1, f1, 6, 18, 2, 2)
+        c1[r] = without_middle(b1[r]) + e1[(r - 4) // 2]
+    for dst, src, first, last in ((d1, c1, 5, 19), (c1, d1, 6, 18)):
+        for i, n in chunks(first, last):
+            p, around = neighbours(src, i, n, 2, 2)
+            dst[i : i + n] = 0.2 * p + COEFF * (around - without_middle(f1[i : i + n]))
     for i in range(22):
-        coarse = a1[6 + (i + 1) // 2]
-        p0[i, 0:24, :] = finest[i, 0:24, :] + coarse[0:24]
-        p0[i, 24:32, :] = finest[i, 24:32, :] + coarse[40:48]
+        coarse = c1[6 + (i + 1) // 2]
+        edge = coarse[16:24]
+        p0[i, 0:B, :] = finest[i, 0:B, :] + coarse[0:B]
+        p0[i, B:, :] = finest[i, B:, :] + jnp.where(row_of(edge) < 4, edge, coarse[24:32])
     sweep(q0, p0, right, 1, 21, 1, 1, 1)
     sweep(p0, q0, right, 2, 20, 1, 1, 1)
     for i in range(B):
@@ -406,45 +508,49 @@
     near, far, drag = call(
         pack_x,
         [shape(SIDE, B, 128), shape(SIDE, B, 128), shape(B, B, 128)],
-        [SMEM, VMEM, SMEM, VMEM, VMEM, VMEM],
-    )(place, land_type, surface_drag, velocity, pressure, turbine_cells)
+        [SMEM, SMEM] + [ANY] * 4,
+        [pltpu.VMEM((B, B), jnp.int32), pltpu.VMEM((B, B, 128), jnp.int32), pltpu.SemaphoreType.DMA((10,))],
+    )(place, surface_drag, land_type, velocity, pressure, turbine_cells)
     near, far = exchange(near, far, "gx")
     wide_v, wide_p, wide_d, near, far = call(
         widen_x,
-        [shape(3, VX, B, 128), shape(PX, B, 128), shape(PX, B, 128), shape(3, VX, 4, 128), shape(3, VX, 4, 128)],
+        [shape(3, VX, B, 128), shape(PX, B, 128), shape(PX, B, 128), shape(8, 40, 128), shape(8, 40, 128)],
         [SMEM] + [VMEM] * 5,
     )(place, velocity, pressure, drag, near, far)
     near, far = exchange(near, far, "gy")
     star, source, near, far = call(
         advance,
-        [shape(3, B, B, 128), shape(PX - 2, B, 128), shape(2 * PX - 2, 8, 128), shape(2 * PX - 2, 8, 128)],
+        [shape(3, B, B, 128), shape(PX - 2, B, 128), shape(N_UNITS, 4, 128), shape(N_UNITS, 4, 128)],
         [SMEM] + [VMEM] * 5,
         [(3, VX, 24, 128), (PX, 24, 128), (3, VX, 24, 128), (3, VX, 24, 128)],
     )(place, wide_v, wide_p, wide_d, near, far)
     near, far = exchange(near, far, "gy")
     finest, right, packed_one, packed_two = call(
         presmooth,
-        [shape(22, 32, 128), shape(20, 32, 128), shape(2, B, 128), shape(4, 128)],
+        [shape(22, 24, 128), shape(20, 24, 128), shape(2, B, 128), shape(gx, 4, 128)],
         [SMEM] + [VMEM] * 4,
         [(PX, 32, 128)] * 3 + [(12, 32, 128)] * 3,
     )(place, source, wide_p, near, far)
     near, far = exchange(packed_one, packed_one, "gx")
-    blocks = lax.all_to_all(jnp.broadcast_to(packed_two[None], (gx, 4, 128)), "gx", 0, 0, tiled=True)
-    (pieces,) = call(
-        lambda *refs: pack_y(gx, *refs), [shape(gy, 136, 128)], [SMEM] + [VMEM] * 4
+    blocks = lax.all_to_all(packed_two, "gx", 0, 0, tiled=True)
+    strips, window, near, far = call(
+        lambda *refs: pack_y(gx, *refs),
+        [shape(gy, 9, 4, 128), shape(6, B, 128), shape(6, 12, 128), shape(6, 12, 128)],
+        [SMEM] + [VMEM] * 4,
     )(place, blocks, packed_one, near, far)
-    pieces = lax.all_to_all(pieces, "gy", 0, 0, tiled=True)
+    strips = lax.all_to_all(strips, "gy", 0, 0, tiled=True)
+    near, far = exchange(near, far, "gy")
     velocity_new, pressure_new = call(
         finish,
         [shape(3, B, B, 128), shape(B, B, 128)],
-        [SMEM] + [VMEM] * 4,
-        [(9, 32, 128)]
-        + [(36, 32, 128)] * 3
-        + [(18, 32, 128)] * 3
-        + [(24, 48, 128)] * 3
-        + [(8, 48, 128)]
-        + [(22, 32, 128)] * 2,
-    )(place, pieces, finest, right, star)
+        [SMEM] + [VMEM] * 7,
+        [(9, 32, 128)] * 6
+        + [(6, 40, 128)]
+        + [(24, 40, 128)] * 3
+        + [(24, 32, 128)] * 2
+        + [(8, 32, 128)]
+        + [(22, 24, 128)] * 2,
+    )(place, strips, window, near, far, finest, right, star)
     return velocity_new, pressure_new
 
 

time: 105 us -> 104 us (level)
  blocking collectives: 12.2 us -> 0 us
  starting transfers between devices: 50 us -> 59.4 us
  waiting for transfers between devices: 21.2 us -> 23.3 us
    all_to_all x1 -> x0, blocking collectives: 12.2 us -> none  [per_device(): pieces = lax.all_to_all(pieces, 'gy', 0, 0, tiled=True)]
    ppermute x4 -> x5, starting transfers between devices: 11 us -> 14.8 us  [exchange(): far_block = lax.ppermute(far_block, axis, far)]
    ppermute x4 -> x5, starting transfers between devices: 19.7 us -> 23.1 us  [exchange(): return (lax.ppermute(near_block, axis, near), far_block)]
    ppermute x4 -> x5, waiting for transfers between devices: 14.6 us -> 16.9 us  [exchange(): far_block = lax.ppermute(far_block, axis, far)]
    all_to_all x1 -> x2, starting transfers between devices: 19.3 us -> 21.4 us  [the longest x1 17.1 us: per_device(): blocks = lax.all_to_all(packed_two, 'gx', 0, 0, tiled=True)]
    ppermute x4 -> x5, waiting for transfers between devices: 4.84 us -> 4.58 us  [exchange(): return (lax.ppermute(near_block, axis, near), far_block)]
  transfers between devices with their start and end apart: 9 -> 12, of which waited for: 7 -> 8; matrix products, arithmetic and copies ran while one was open for 0% -> 0% of each run, Pallas kernels for 0% -> 0%
where the time goes in v2:
time: 104 us; the launch traced here: 103 us
  starting transfers between devices  59.4 us (57%)
  waiting for transfers between devices  23.3 us (22%)
  Pallas kernels  16 us (15%)
  local copies, waits for them, and re-layouts  3.42 us (3%)
    ppermute x5, starting transfers between devices, exchange(): return (lax.ppermute(near_block, axis, near), far_block)  23.1 us
    all_to_all x1, starting transfers between devices, per_device(): blocks = lax.all_to_all(packed_two, 'gx', 0, 0, tiled=True)  17.1 us
    ppermute x5, waiting for transfers between devices, exchange(): far_block = lax.ppermute(far_block, axis, far)  16.9 us
    ppermute x5, starting transfers between devices, exchange(): far_block = lax.ppermute(far_block, axis, far)  14.8 us
    pallas_call x1, Pallas kernels, per_device(): call(finish, [shape(3, B, B, 128), shape(B, B, 128)], [SMEM] + [VMEM] * 7...  4.69 us
    ppermute x5, waiting for transfers between devices, exchange(): return (lax.ppermute(near_block, axis, near), far_block)  4.58 us
    all_to_all x1, starting transfers between devices, per_device(): strips = lax.all_to_all(strips, 'gy', 0, 0, tiled=True)  4.29 us
    pallas_call x1, Pallas kernels, per_device(): call(advance, [shape(3, B, B, 128), shape(PX - 2, B, 128), shape(N_UNITS,...  4.26 us
  transfers between devices with their start and end apart: 12, of which 8 were waited for; matrix products, arithmetic and copies ran while one was open for 0% of the time, Pallas kernels for 0%

profile of v2, /device:TPU:1, one launch (start us, length us, event | category | flops | bytes accessed | tf_op | source)
XLA Modules:
  0.0 103.0 jit_solution(112919586798896006)
XLA Ops:
  0.6 0.0 copy-start.5
  0.6 0.0 copy-start.6
  0.7 0.1 pad_add_fusion.place.refs_0_
  0.7 0.6 copy-done.5
  1.3 0.0 copy-done.6
  1.3 0.0 copy-start
  1.3 1.0 copy-done
  2.3 0.0 copy-start.2
  2.3 0.9 copy-done.2
  3.2 0.0 copy-start.4
  3.2 0.9 copy-done.4
  4.1 0.0 copy-start.1
  4.1 0.0 copy-start.3
  4.1 1.7 %shard_map.68 = (f32[41,16,128]{2,1,0:T(8,128)S(1)}, f32[41,16,128]{2,1,0:T(8,128)S(1)}, f32[16,16,128]{2,1,0:T(8,128)S(1)}) custom-call(s32[2]{0:T(128)S(1)} %pad_add_fusion.place.refs_0_, f32[16]{0:T(128)S(1)} %copy-done.6, s32[16,16]{1,0:T(8,128)S(1)} %copy-done.5, f32[3,16,16,128]{3,2,1,0:T(8,128)S(1)} %copy-done, f32[16,16,128]{2,1,0:T(8,128)S(1)} %copy-done.2, ...), custom_call_target="tpu_custom_call" | custom-call | tf_op jit(solution)/shard_map/pallas_call | solution.py:508
  5.8 8.8 %collective-permute-start = (f32[41,16,128]{2,1,0:T(8,128)S(1)}, f32[41,16,128]{2,1,0:T(8,128)S(1)}, u32[]{:S(2)}, u32[]{:S(2)}) collective-permute-start(f32[41,16,128]{2,1,0:T(8,128)S(1)} %get-tuple-element.23), channel_id=1, source_target_pairs={{0,8},{8,0},{16,24},{24,16},{32,40},{40,32},{48,56},{56,48},{64,72... | collective-permute-start | bytes 1007624 | tf_op jit(solution)/shard_map/ppermute | solution.py:501
  14.6 1.9 %collective-permute-start.1 = (f32[41,16,128]{2,1,0:T(8,128)S(1)}, f32[41,16,128]{2,1,0:T(8,128)S(1)}, u32[]{:S(2)}, u32[]{:S(2)}) collective-permute-start(f32[41,16,128]{2,1,0:T(8,128)S(1)} %get-tuple-element.24), channel_id=1, source_target_pairs={{0,504},{8,16},{16,8},{24,32},{32,24},{40,48},{48,40},{56,64},{64,... | collective-permute-start | bytes 1007624 | tf_op jit(solution)/shard_map/ppermute | solution.py:500
  16.6 0.0 collective-permute-done.near
  16.6 6.5 %collective-permute-done.1.far = f32[41,16,128]{2,1,0:T(8,128)S(1)} collective-permute-done((f32[41,16,128]{2,1,0:T(8,128)S(1)}, f32[41,16,128]{2,1,0:T(8,128)S(1)}, u32[]{:S(2)}, u32[]{:S(2)}) %collective-permute-start.1) | collective-permute-done | bytes 335904 | tf_op jit(solution)/shard_map/ppermute | solution.py:500
  23.1 0.0 copy-done.1
  23.1 0.0 copy-done.3
  23.1 0.7 shard_map.69
  23.9 1.9 %collective-permute-start.2 = (f32[8,40,128]{2,1,0:T(8,128)S(1)}, f32[8,40,128]{2,1,0:T(8,128)S(1)}, u32[]{:S(2)}, u32[]{:S(2)}) collective-permute-start(f32[8,40,128]{2,1,0:T(8,128)S(1)} %get-tuple-element.28), channel_id=1, source_target_pairs={{0,1},{1,0},{2,3},{3,2},{4,5},{5,4},{6,7},{7,6},{8,9},{9,8},{10,11... | collective-permute-start | bytes 491528 | tf_op jit(solution)/shard_map/ppermute | solution.py:501
  25.8 1.9 %collective-permute-start.3 = (f32[8,40,128]{2,1,0:T(8,128)S(1)}, f32[8,40,128]{2,1,0:T(8,128)S(1)}, u32[]{:S(2)}, u32[]{:S(2)}) collective-permute-start(f32[8,40,128]{2,1,0:T(8,128)S(1)} %get-tuple-element.29), channel_id=1, source_target_pairs={{0,7},{1,2},{2,1},{3,4},{4,3},{5,6},{6,5},{7,0},{8,15},{9,10},{10,... | collective-permute-start | bytes 491528 | tf_op jit(solution)/shard_map/ppermute | solution.py:500
  27.7 2.2 %collective-permute-done.2.near = f32[8,40,128]{2,1,0:T(8,128)S(1)} collective-permute-done((f32[8,40,128]{2,1,0:T(8,128)S(1)}, f32[8,40,128]{2,1,0:T(8,128)S(1)}, u32[]{:S(2)}, u32[]{:S(2)}) %collective-permute-start.2) | collective-permute-done | bytes 163872 | tf_op jit(solution)/shard_map/ppermute | solution.py:501
  29.9 4.0 %collective-permute-done.3.far = f32[8,40,128]{2,1,0:T(8,128)S(1)} collective-permute-done((f32[8,40,128]{2,1,0:T(8,128)S(1)}, f32[8,40,128]{2,1,0:T(8,128)S(1)}, u32[]{:S(2)}, u32[]{:S(2)}) %collective-permute-start.3) | collective-permute-done | bytes 163872 | tf_op jit(solution)/shard_map/ppermute | solution.py:500
  34.0 4.3 %shard_map.70 = (f32[3,16,16,128]{3,2,1,0:T(8,128)S(1)}, f32[28,16,128]{2,1,0:T(8,128)S(1)}, f32[92,4,128]{2,1,0:T(4,128)S(1)}, f32[92,4,128]{2,1,0:T(4,128)S(1)}) custom-call(s32[2]{0:T(128)S(1)} %pad_add_fusion.place.refs_0_, f32[3,34,16,128]{3,2,1,0:T(8,128)S(1)} %get-tuple-element.25.wide_v, f32[30,16,128]{2,1,0:T(8,128)S(1)} %get-tuple-element.26.wide_p, ...), custom_call_target="tpu_custom_call" | custom-call | tf_op jit(solution)/shard_map/pallas_call | solution.py:521
  38.2 2.4 %collective-permute-start.4 = (f32[92,4,128]{2,1,0:T(4,128)S(1)}, f32[92,4,128]{2,1,0:T(4,128)S(1)}, u32[]{:S(2)}, u32[]{:S(2)}) collective-permute-start(f32[92,4,128]{2,1,0:T(4,128)S(1)} %get-tuple-element.31), channel_id=1, source_target_pairs={{0,1},{1,0},{2,3},{3,2},{4,5},{5,4},{6,7},{7,6},{8,9},{9,8},{10,11... | collective-permute-start | bytes 565256 | tf_op jit(solution)/shard_map/ppermute | solution.py:501
  40.6 3.2 %collective-permute-start.5 = (f32[92,4,128]{2,1,0:T(4,128)S(1)}, f32[92,4,128]{2,1,0:T(4,128)S(1)}, u32[]{:S(2)}, u32[]{:S(2)}) collective-permute-start(f32[92,4,128]{2,1,0:T(4,128)S(1)} %get-tuple-element.32), channel_id=1, source_target_pairs={{0,7},{1,2},{2,1},{3,4},{4,3},{5,6},{6,5},{7,0},{8,15},{9,10},{10,... | collective-permute-start | bytes 565256 | tf_op jit(solution)/shard_map/ppermute | solution.py:500
  43.8 1.6 %collective-permute-done.4.near = f32[92,4,128]{2,1,0:T(4,128)S(1)} collective-permute-done((f32[92,4,128]{2,1,0:T(4,128)S(1)}, f32[92,4,128]{2,1,0:T(4,128)S(1)}, u32[]{:S(2)}, u32[]{:S(2)}) %collective-permute-start.4) | collective-permute-done | bytes 188448 | tf_op jit(solution)/shard_map/ppermute | solution.py:501
  45.4 3.7 %collective-permute-done.5.far = f32[92,4,128]{2,1,0:T(4,128)S(1)} collective-permute-done((f32[92,4,128]{2,1,0:T(4,128)S(1)}, f32[92,4,128]{2,1,0:T(4,128)S(1)}, u32[]{:S(2)}, u32[]{:S(2)}) %collective-permute-start.5) | collective-permute-done | bytes 188448 | tf_op jit(solution)/shard_map/ppermute | solution.py:500
  49.1 3.4 %shard_map.71 = (f32[22,24,128]{2,1,0:T(8,128)S(1)}, f32[20,24,128]{2,1,0:T(8,128)S(1)}, f32[2,16,128]{2,1,0:T(8,128)S(1)}, f32[64,4,128]{2,1,0:T(4,128)}) custom-call(s32[2]{0:T(128)S(1)} %pad_add_fusion.place.refs_0_, f32[28,16,128]{2,1,0:T(8,128)S(1)} %get-tuple-element.30.source, f32[30,16,128]{2,1,0:T(8,128)S(1)} %get-tuple-element.26.wide_p, ...), custom_call_target="tpu_custom_call" | custom-call | tf_op jit(solution)/shard_map/pallas_call | solution.py:528
  52.4 17.1 %all-to-all-start = ((f32[64,4,128]{2,1,0:T(4,128)}), f32[64,4,128]{2,1,0:T(4,128)S(1)}, u32[]{:S(2)}, u32[]{:S(2)}) async-start(f32[64,4,128]{2,1,0:T(4,128)} %get-tuple-element.33), calls=%async_computation | async-start | bytes 262144 | tf_op jit(solution)/shard_map/all_to_all | solution.py:535
  69.5 3.5 %collective-permute-start.7 = (f32[2,16,128]{2,1,0:T(8,128)S(1)}, f32[2,16,128]{2,1,0:T(8,128)S(1)}, u32[]{:S(2)}, u32[]{:S(2)}) collective-permute-start(f32[2,16,128]{2,1,0:T(8,128)S(1)} %get-tuple-element.34.refs_2_), channel_id=1, source_target_pairs={{0,504},{8,16},{16,8},{24,32},{32,24},{40,48},{48,40},{56,64},{64,... | collective-permute-start | bytes 49160 | tf_op jit(solution)/shard_map/ppermute | solution.py:500
  73.1 6.7 %collective-permute-start.6 = (f32[2,16,128]{2,1,0:T(8,128)S(1)}, f32[2,16,128]{2,1,0:T(8,128)S(1)}, u32[]{:S(2)}, u32[]{:S(2)}) collective-permute-start(f32[2,16,128]{2,1,0:T(8,128)S(1)} %get-tuple-element.34.refs_2_), channel_id=1, source_target_pairs={{0,8},{8,0},{16,24},{24,16},{32,40},{40,32},{48,56},{56,48},{64,72... | collective-permute-start | bytes 49160 | tf_op jit(solution)/shard_map/ppermute | solution.py:501
  79.8 0.0 collective-permute-done.7.refs_4_
  79.8 0.8 collective-permute-done.6.refs_3_
  80.6 1.8 %all-to-all-done.refs_1_ = f32[64,4,128]{2,1,0:T(4,128)S(1)} async-done(((f32[64,4,128]{2,1,0:T(4,128)}), f32[64,4,128]{2,1,0:T(4,128)S(1)}, u32[]{:S(2)}, u32[]{:S(2)}) %all-to-all-start) | async-done | bytes 131104 | tf_op jit(solution)/shard_map/all_to_all | solution.py:535
  82.4 1.3 %shard_map.72 = (f32[8,9,4,128]{3,2,1,0:T(4,128)}, f32[6,16,128]{2,1,0:T(8,128)S(1)}, f32[6,12,128]{2,1,0:T(8,128)S(1)}, f32[6,12,128]{2,1,0:T(8,128)S(1)}) custom-call(s32[2]{0:T(128)S(1)} %pad_add_fusion.place.refs_0_, f32[64,4,128]{2,1,0:T(4,128)S(1)} %all-to-all-done.refs_1_, f32[2,16,128]{2,1,0:T(8,128)S(1)} %get-tuple-element.34.refs_2_, ...), custom_call_target="tpu_custom_call" | custom-call | tf_op jit(solution)/shard_map/pallas_call | solution.py:536
  83.7 4.3 %all-to-all-start.1 = ((f32[8,9,4,128]{3,2,1,0:T(4,128)}), f32[8,9,4,128]{3,2,1,0:T(4,128)S(1)}, u32[]{:S(2)}, u32[]{:S(2)}) async-start(f32[8,9,4,128]{3,2,1,0:T(4,128)} %get-tuple-element.35), calls=%async_computation.1 | async-start | bytes 294912 | tf_op jit(solution)/shard_map/all_to_all | solution.py:541
  88.0 3.4 %collective-permute-start.8 = (f32[6,12,128]{2,1,0:T(8,128)S(1)}, f32[6,12,128]{2,1,0:T(8,128)S(1)}, u32[]{:S(2)}, u32[]{:S(2)}) collective-permute-start(f32[6,12,128]{2,1,0:T(8,128)S(1)} %get-tuple-element.37), channel_id=1, source_target_pairs={{0,1},{1,0},{2,3},{3,2},{4,5},{5,4},{6,7},{7,6},{8,9},{9,8},{10,11... | collective-permute-start | bytes 110600 | tf_op jit(solution)/shard_map/ppermute | solution.py:501
  91.3 4.3 %collective-permute-start.9 = (f32[6,12,128]{2,1,0:T(8,128)S(1)}, f32[6,12,128]{2,1,0:T(8,128)S(1)}, u32[]{:S(2)}, u32[]{:S(2)}) collective-permute-start(f32[6,12,128]{2,1,0:T(8,128)S(1)} %get-tuple-element.38), channel_id=1, source_target_pairs={{0,7},{1,2},{2,1},{3,4},{4,3},{5,6},{6,5},{7,0},{8,15},{9,10},{10,... | collective-permute-start | bytes 110600 | tf_op jit(solution)/shard_map/ppermute | solution.py:500
  95.6 0.0 collective-permute-done.8.near
  95.6 2.6 %collective-permute-done.9.far = f32[6,12,128]{2,1,0:T(8,128)S(1)} collective-permute-done((f32[6,12,128]{2,1,0:T(8,128)S(1)}, f32[6,12,128]{2,1,0:T(8,128)S(1)}, u32[]{:S(2)}, u32[]{:S(2)}) %collective-permute-start.9) | collective-permute-done | bytes 36896 | tf_op jit(solution)/shard_map/ppermute | solution.py:500
  98.3 0.0 all-to-all-done.1.strips
  98.3 4.7 %shard_map.73 = (f32[3,16,16,128]{3,2,1,0:T(8,128)}, f32[16,16,128]{2,1,0:T(8,128)}) custom-call(s32[2]{0:T(128)S(1)} %pad_add_fusion.place.refs_0_, f32[8,9,4,128]{3,2,1,0:T(4,128)S(1)} %all-to-all-done.1.strips, f32[6,16,128]{2,1,0:T(8,128)S(1)} %get-tuple-element.36.window, f32[6,12,128]{2,1,0:T(8,128)S(1)} %collective-permute-done.8.near, ...), custom_call_target="tpu_custom_call" | custom-call | tf_op jit(solution)/shard_map/pallas_call | solution.py:543
Async XLA Ops:
  0.6 0.7 copy-start.5
  0.6 0.7 copy-start.6
  1.3 1.0 copy-start
  2.3 0.9 copy-start.2
  3.2 0.9 copy-start.4
  4.1 19.0 %copy-start.1 = (f32[3,16,16,128]{3,2,1,0:T(8,128)S(1)}, f32[3,16,16,128]{3,2,1,0:T(8,128)}, u32[]{:S(2)}) copy-start(f32[3,16,16,128]{3,2,1,0:T(8,128)} %velocity.3) | copy-start | bytes 1179652
  4.1 19.0 %copy-start.3 = (f32[16,16,128]{2,1,0:T(8,128)S(1)}, f32[16,16,128]{2,1,0:T(8,128)}, u32[]{:S(2)}) copy-start(f32[16,16,128]{2,1,0:T(8,128)} %pressure.3) | copy-start | bytes 393220
  5.8 10.7 %collective-permute-start = (f32[41,16,128]{2,1,0:T(8,128)S(1)}, f32[41,16,128]{2,1,0:T(8,128)S(1)}, u32[]{:S(2)}, u32[]{:S(2)}) collective-permute-start(f32[41,16,128]{2,1,0:T(8,128)S(1)} %get-tuple-element.23), channel_id=1, source_target_pairs={{0,8},{8,0},{16,24},{24,16},{32,40},{40,32},{48,56},{56,48},{64,72... | collective-permute-start | bytes 1007624 | tf_op jit(solution)/shard_map/ppermute | solution.py:501
  14.6 8.5 %collective-permute-start.1 = (f32[41,16,128]{2,1,0:T(8,128)S(1)}, f32[41,16,128]{2,1,0:T(8,128)S(1)}, u32[]{:S(2)}, u32[]{:S(2)}) collective-permute-start(f32[41,16,128]{2,1,0:T(8,128)S(1)} %get-tuple-element.24), channel_id=1, source_target_pairs={{0,504},{8,16},{16,8},{24,32},{32,24},{40,48},{48,40},{56,64},{64,... | collective-permute-start | bytes 1007624 | tf_op jit(solution)/shard_map/ppermute | solution.py:500
  23.9 6.1 %collective-permute-start.2 = (f32[8,40,128]{2,1,0:T(8,128)S(1)}, f32[8,40,128]{2,1,0:T(8,128)S(1)}, u32[]{:S(2)}, u32[]{:S(2)}) collective-permute-start(f32[8,40,128]{2,1,0:T(8,128)S(1)} %get-tuple-element.28), channel_id=1, source_target_pairs={{0,1},{1,0},{2,3},{3,2},{4,5},{5,4},{6,7},{7,6},{8,9},{9,8},{10,11... | collective-permute-start | bytes 491528 | tf_op jit(solution)/shard_map/ppermute | solution.py:501
  25.8 8.2 %collective-permute-start.3 = (f32[8,40,128]{2,1,0:T(8,128)S(1)}, f32[8,40,128]{2,1,0:T(8,128)S(1)}, u32[]{:S(2)}, u32[]{:S(2)}) collective-permute-start(f32[8,40,128]{2,1,0:T(8,128)S(1)} %get-tuple-element.29), channel_id=1, source_target_pairs={{0,7},{1,2},{2,1},{3,4},{4,3},{5,6},{6,5},{7,0},{8,15},{9,10},{10,... | collective-permute-start | bytes 491528 | tf_op jit(solution)/shard_map/ppermute | solution.py:500
  38.2 7.1 %collective-permute-start.4 = (f32[92,4,128]{2,1,0:T(4,128)S(1)}, f32[92,4,128]{2,1,0:T(4,128)S(1)}, u32[]{:S(2)}, u32[]{:S(2)}) collective-permute-start(f32[92,4,128]{2,1,0:T(4,128)S(1)} %get-tuple-element.31), channel_id=1, source_target_pairs={{0,1},{1,0},{2,3},{3,2},{4,5},{5,4},{6,7},{7,6},{8,9},{9,8},{10,11... | collective-permute-start | bytes 565256 | tf_op jit(solution)/shard_map/ppermute | solution.py:501
  40.6 8.4 %collective-permute-start.5 = (f32[92,4,128]{2,1,0:T(4,128)S(1)}, f32[92,4,128]{2,1,0:T(4,128)S(1)}, u32[]{:S(2)}, u32[]{:S(2)}) collective-permute-start(f32[92,4,128]{2,1,0:T(4,128)S(1)} %get-tuple-element.32), channel_id=1, source_target_pairs={{0,7},{1,2},{2,1},{3,4},{4,3},{5,6},{6,5},{7,0},{8,15},{9,10},{10,... | collective-permute-start | bytes 565256 | tf_op jit(solution)/shard_map/ppermute | solution.py:500
  52.4 30.0 %all-to-all-start = ((f32[64,4,128]{2,1,0:T(4,128)}), f32[64,4,128]{2,1,0:T(4,128)S(1)}, u32[]{:S(2)}, u32[]{:S(2)}) async-start(f32[64,4,128]{2,1,0:T(4,128)} %get-tuple-element.33), calls=%async_computation | async-start | bytes 262144 | tf_op jit(solution)/shard_map/all_to_all | solution.py:535
  69.5 10.3 %collective-permute-start.7 = (f32[2,16,128]{2,1,0:T(8,128)S(1)}, f32[2,16,128]{2,1,0:T(8,128)S(1)}, u32[]{:S(2)}, u32[]{:S(2)}) collective-permute-start(f32[2,16,128]{2,1,0:T(8,128)S(1)} %get-tuple-element.34.refs_2_), channel_id=1, source_target_pairs={{0,504},{8,16},{16,8},{24,32},{32,24},{40,48},{48,40},{56,64},{64,... | collective-permute-start | bytes 49160 | tf_op jit(solution)/shard_map/ppermute | solution.py:500
  73.1 7.5 %collective-permute-start.6 = (f32[2,16,128]{2,1,0:T(8,128)S(1)}, f32[2,16,128]{2,1,0:T(8,128)S(1)}, u32[]{:S(2)}, u32[]{:S(2)}) collective-permute-start(f32[2,16,128]{2,1,0:T(8,128)S(1)} %get-tuple-element.34.refs_2_), channel_id=1, source_target_pairs={{0,8},{8,0},{16,24},{24,16},{32,40},{40,32},{48,56},{56,48},{64,72... | collective-permute-start | bytes 49160 | tf_op jit(solution)/shard_map/ppermute | solution.py:501
  83.7 14.6 %all-to-all-start.1 = ((f32[8,9,4,128]{3,2,1,0:T(4,128)}), f32[8,9,4,128]{3,2,1,0:T(4,128)S(1)}, u32[]{:S(2)}, u32[]{:S(2)}) async-start(f32[8,9,4,128]{3,2,1,0:T(4,128)} %get-tuple-element.35), calls=%async_computation.1 | async-start | bytes 294912 | tf_op jit(solution)/shard_map/all_to_all | solution.py:541
  88.0 7.7 %collective-permute-start.8 = (f32[6,12,128]{2,1,0:T(8,128)S(1)}, f32[6,12,128]{2,1,0:T(8,128)S(1)}, u32[]{:S(2)}, u32[]{:S(2)}) collective-permute-start(f32[6,12,128]{2,1,0:T(8,128)S(1)} %get-tuple-element.37), channel_id=1, source_target_pairs={{0,1},{1,0},{2,3},{3,2},{4,5},{5,4},{6,7},{7,6},{8,9},{9,8},{10,11... | collective-permute-start | bytes 110600 | tf_op jit(solution)/shard_map/ppermute | solution.py:501
  91.3 6.9 %collective-permute-start.9 = (f32[6,12,128]{2,1,0:T(8,128)S(1)}, f32[6,12,128]{2,1,0:T(8,128)S(1)}, u32[]{:S(2)}, u32[]{:S(2)}) collective-permute-start(f32[6,12,128]{2,1,0:T(8,128)S(1)} %get-tuple-element.38), channel_id=1, source_target_pairs={{0,7},{1,2},{2,1},{3,4},{4,3},{5,6},{6,5},{7,0},{8,15},{9,10},{10,... | collective-permute-start | bytes 110600 | tf_op jit(solution)/shard_map/ppermute | solution.py:500

commit v3 on v2

--- a/solution.py
+++ b/solution.py
@@ -17,7 +17,7 @@
 WINDOW = 4
 VMEM = pl.BlockSpec(memory_space=pltpu.VMEM)
 SMEM = pl.BlockSpec(memory_space=pltpu.SMEM)
-ANY = pl.BlockSpec(memory_space=pl.ANY)
+HBM = pl.BlockSpec(memory_space=pltpu.HBM)
 UNITS = (
     (0, 0, 5, 18, True),
     (18, 0, 5, 18, False),
@@ -216,17 +216,13 @@
         along_y = [visc * e01, 2.0 * visc * gy[1], visc * e12]
         along_z = [visc * e02, visc * e12, 2.0 * visc * gz[2]]
         lane = lane_of(u[0])
-        ghost = [jnp.where(lane == 0, u[a], -u[a]) for a in range(3)]
-        ghost_visc = EDDY * jnp.sqrt(
-            ghost[0] * ghost[0] + ghost[1] * ghost[1] + 2.0 * ghost[2] * ghost[2]
-        )
-        ghost_tau = [ghost_visc * ghost[0], ghost_visc * ghost[1], 2.0 * ghost_visc * ghost[2]]
-        wind = dr[i - 2] * jnp.sqrt(u[0] * u[0] + u[1] * u[1])
+        flat = u[0] * u[0] + u[1] * u[1]
+        edge = jnp.where((lane == 0) | (lane == 127), EDDY * jnp.sqrt(flat + 2.0 * (u[2] * u[2])), 0.0)
+        wind = dr[i - 2] * jnp.sqrt(flat)
         for a in range(3):
             change = 0.5 * (turn(along_y[a], -1, 0) - turn(along_y[a], 1, 0))
-            above = jnp.where(lane == 127, ghost_tau[a], turn(along_z[a], -1, 1))
-            below = jnp.where(lane == 0, ghost_tau[a], turn(along_z[a], 1, 1))
-            change = change + (above - below)
+            above, below = zero_shifts(along_z[a])
+            change = change + ((above - below) - (edge * u[a] if a < 2 else 2.0 * (edge * u[a])))
             change = change - (u[0] * gx[a] + u[1] * gy[a] + u[2] * gz[a])
             if a < 2:
                 change = change - wind * u[a]
@@ -261,27 +257,47 @@
         send(far_y, near_y)
 
 
-def neighbours(ref, start, count, dy, dz):
+def column_sum(dz, halves):
+    i = lax.broadcasted_iota(jnp.int32, (128, 128), 0)
+    j = lax.broadcasted_iota(jnp.int32, (128, 128), 1)
+    hit = (i - j == dz) | (j - i == dz) | ((i == j) & ((j < dz) | (j >= 128 - dz)))
+    return jnp.concatenate([jnp.where(hit, 4.0, 0.0).astype(jnp.bfloat16)] * halves, axis=0)
+
+
+def exact_product(values, matrix):
+    flat = values.reshape(-1, 128)
+    high = flat.astype(jnp.bfloat16)
+    rest = flat - high.astype(F32)
+    middle = rest.astype(jnp.bfloat16)
+    low = (rest - middle.astype(F32)).astype(jnp.bfloat16)
+    parts = jnp.concatenate([high, middle, low], axis=1)
+    return jnp.dot(parts, matrix, preferred_element_type=F32).reshape(values.shape)
+
+
+def neighbours(ref, start, count, dy, dz, matrix=None):
     p = ref[start : start + count]
+    sides = ref[start - 1 : start - 1 + count] + ref[start + 1 : start + 1 + count]
+    sides = sides + (turn(p, dy, 1) + turn(p, -dy, 1))
+    if matrix is not None:
+        return p, sides + exact_product(p, matrix)
     lane = lane_of(p)
     below = jnp.where(lane < dz, p, turn(p, dz, 2))
     above = jnp.where(lane >= 128 - dz, p, turn(p, -dz, 2))
-    sides = ref[start - 1 : start - 1 + count] + ref[start + 1 : start + 1 + count]
-    return p, sides + (turn(p, dy, 1) + turn(p, -dy, 1)) + 4.0 * (below + above)
+    return p, sides + 4.0 * (below + above)
 
 
 def chunks(first, last, size=2):
     return [(i, min(size, last - i)) for i in range(first, last, size)]
 
 
-def sweep(dst, src, right, first, last, dy, dz, offset=0):
-    for i, n in chunks(first, last):
-        p, around = neighbours(src, i, n, dy, dz)
+def sweep(dst, src, right, first, last, dy, dz, offset=0, matrix=None):
+    for i, n in chunks(first, last, 2 if matrix is None else 4):
+        p, around = neighbours(src, i, n, dy, dz, matrix)
         dst[i : i + n] = 0.2 * p + COEFF * (around - right[i - offset : i - offset + n])
 
 
-def scaled_residual(src, right, i, n, dy, dz):
-    p, around = neighbours(src, i, n, dy, dz)
+def scaled_residual(src, right, i, n, dy, dz, matrix=None):
+    p, around = neighbours(src, i, n, dy, dz, matrix)
     return right[i : i + n] - around + 12.0 * p
 
 
@@ -316,17 +332,22 @@
     def _():
         fill(near, far)
 
-    sweep(q, p, s, 1, PX - 1, 1, 1)
-    sweep(p, q, s, 2, PX - 2, 1, 1)
+    fine = column_sum(1, 3)
+    coarse = column_sum(2, 3)
+    sweep(q, p, s, 1, PX - 1, 1, 1, 0, fine)
+    sweep(p, q, s, 2, PX - 2, 1, 1, 0, fine)
     for out, field, first in ((finest, p, 4), (right, s, 5)):
         out[:, 0:B, :] = field[first : PX - first, 0:B, :]
         out[:, B : B + 4, :] = field[first : PX - first, B : B + 4, :]
         out[:, B + 4 : B + 8, :] = field[first : PX - first, B + 12 : B + 16, :]
-    for k in range(12):
-        f1[k] = coarsen_pair(scaled_residual(p, s, 3 + 2 * k, 2, 1, 1), 1, 1)
+    for k in range(0, 12, 2):
+        rows = scaled_residual(p, s, 3 + 2 * k, 4, 1, 1, fine)
+        f1[k] = coarsen_pair(rows[0:2], 1, 1)
+        f1[k + 1] = coarsen_pair(rows[2:4], 1, 1)
     a1[...] = -COEFF * f1[...]
-    sweep(b1, a1, f1, 1, 11, 2, 2)
-    f2 = [coarsen_pair(scaled_residual(b1, f1, 2 + 2 * k, 2, 2, 2), 2, 2) for k in range(4)]
+    sweep(b1, a1, f1, 1, 11, 2, 2, 0, coarse)
+    rows = scaled_residual(b1, f1, 2, 8, 2, 2, coarse)
+    f2 = [coarsen_pair(rows[2 * k : 2 * k + 2], 2, 2) for k in range(4)]
     lane = lane_of(f2[0]) & 3
     two = jnp.where(lane == 0, f2[0], jnp.where(lane == 1, f2[1], jnp.where(lane == 2, f2[2], f2[3])))
     four = jnp.concatenate([two[4 * y : 4 * y + 1, :] for y in range(4)], axis=0)
@@ -340,9 +361,13 @@
         )
 
 
-def pack_y(peers, place, blocks, own, near, far, strips, window, near_y, far_y):
+GROUPS = ((9, 1, 2), (11, 2, 3), (14, 3, 3), (17, 4, 2))
+N_STRIP = 19
+
+
+def pack_y(peers, place, blocks, own, near, far, strips, window):
     core = place[0] % 2
-    odd = place[1] % 2
+    gy = place[1]
     for j in range(2 * WINDOW + 1):
         piece = blocks[(place[0] + (peers - WINDOW + j)) % peers]
         for k in range(8):
@@ -361,17 +386,14 @@
     def _():
         fill(near, far)
 
-    def send(up, down):
-        up[...] = window[:, 4:16, :]
-        down[...] = window[:, 0:12, :]
-
-    @pl.when(odd == 0)
-    def _():
-        send(near_y, far_y)
-
-    @pl.when(odd == 1)
-    def _():
-        send(far_y, near_y)
+    for step in range(1, 8):
+        peer = (gy + step) % 8
+        for unit, group, count in GROUPS:
+            for k in range(count):
+                first = 4 * k if step == 7 else B - 4 * (count - k)
+                strips[peer, unit + k] = window[group, first : first + 4, :]
+    for k in range(9, N_STRIP):
+        strips[gy, k] = jnp.zeros((4, 128), F32)
 
 
 def packed_neighbours(ref, b, dx, dy, dz):
@@ -402,9 +424,8 @@
     return jnp.concatenate([values[..., 0:24, :], values[..., 32:40, :]], axis=-2)
 
 
-def finish(place, strips, window, near, far, finest, right, star, velocity_new, pressure_new, f2, a2, b2, f3, a3, b3, g1, f1, a1, b1, c1, d1, e1, p0, q0):
+def finish(place, strips, window, finest, right, star, velocity_new, pressure_new, f2, a2, b2, f3, a3, b3, g1, f1, a1, b1, c1, d1, e1, p0, q0):
     gy = place[1]
-    odd = gy % 2
     for j in range(8):
         peer = (gy + j) % 8
         for b in range(2 * WINDOW + 1):
@@ -430,19 +451,12 @@
     packed_sweep(b2, a2, f2, range(3, 6), 1, 1, 4)
     packed_sweep(a2, b2, f2, range(3, 6), 1, 1, 4)
     g1[:, 0:B, :] = window[...]
-
-    def fill(low, high):
-        g1[:, B : B + 12, :] = high[...]
-        g1[:, B + 12 : B + 24, :] = low[...]
-
-    @pl.when(odd == 0)
-    def _():
-        fill(far, near)
-
-    @pl.when(odd == 1)
-    def _():
-        fill(near, far)
-
+    for unit, group, count in GROUPS:
+        for k in range(count):
+            first = B + 4 * k
+            g1[group, first : first + 4, :] = strips[(gy + 1) % 8, unit + k]
+            first = B + 24 - 4 * (count - k)
+            g1[group, first : first + 4, :] = strips[(gy + 7) % 8, unit + k]
     for x in range(3, 21):
         packed = g1[x // 4]
         slots = 2 * (row_of(packed) & 1) + (lane_of(packed) & 1)
@@ -508,7 +522,7 @@
     near, far, drag = call(
         pack_x,
         [shape(SIDE, B, 128), shape(SIDE, B, 128), shape(B, B, 128)],
-        [SMEM, SMEM] + [ANY] * 4,
+        [SMEM, SMEM] + [HBM] * 4,
         [pltpu.VMEM((B, B), jnp.int32), pltpu.VMEM((B, B, 128), jnp.int32), pltpu.SemaphoreType.DMA((10,))],
     )(place, surface_drag, land_type, velocity, pressure, turbine_cells)
     near, far = exchange(near, far, "gx")
@@ -533,24 +547,23 @@
     )(place, source, wide_p, near, far)
     near, far = exchange(packed_one, packed_one, "gx")
     blocks = lax.all_to_all(packed_two, "gx", 0, 0, tiled=True)
-    strips, window, near, far = call(
+    strips, window = call(
         lambda *refs: pack_y(gx, *refs),
-        [shape(gy, 9, 4, 128), shape(6, B, 128), shape(6, 12, 128), shape(6, 12, 128)],
+        [shape(gy, N_STRIP, 4, 128), shape(6, B, 128)],
         [SMEM] + [VMEM] * 4,
     )(place, blocks, packed_one, near, far)
     strips = lax.all_to_all(strips, "gy", 0, 0, tiled=True)
-    near, far = exchange(near, far, "gy")
     velocity_new, pressure_new = call(
         finish,
         [shape(3, B, B, 128), shape(B, B, 128)],
-        [SMEM] + [VMEM] * 7,
+        [SMEM] + [VMEM] * 5,
         [(9, 32, 128)] * 6
         + [(6, 40, 128)]
         + [(24, 40, 128)] * 3
         + [(24, 32, 128)] * 2
         + [(8, 32, 128)]
         + [(22, 24, 128)] * 2,
-    )(place, strips, window, near, far, finest, right, star)
+    )(place, strips, window, finest, right, star)
     return velocity_new, pressure_new
 
 

time: 104 us -> 98.8 us (0.950)
  starting transfers between devices: 59.4 us -> 47.4 us
  blocking collectives: 0 us -> 11.3 us
  waiting for transfers between devices: 23.3 us -> 20.7 us
  Pallas kernels: 16 us -> 14.6 us
    all_to_all x0 -> x1, blocking collectives: none -> 11.3 us  [per_device(): strips = lax.all_to_all(strips, 'gy', 0, 0, tiled=True)]
    ppermute x5 -> x4, starting transfers between devices: 14.8 us -> 10.5 us  [exchange(): far_block = lax.ppermute(far_block, axis, far)]
    all_to_all x1 -> x0, starting transfers between devices: 4.29 us -> none  [per_device(): strips = lax.all_to_all(strips, 'gy', 0, 0, tiled=True)]
    ppermute x5 -> x4, starting transfers between devices: 23.1 us -> 19.8 us  [exchange(): return (lax.ppermute(near_block, axis, near), far_block)]
    ppermute x5 -> x4, waiting for transfers between devices: 16.9 us -> 14.3 us  [exchange(): far_block = lax.ppermute(far_block, axis, far)]
    ppermute x5 -> x4, waiting for transfers between devices: 4.58 us -> 4.58 us  [exchange(): return (lax.ppermute(near_block, axis, near), far_block)]
  transfers between devices with their start and end apart: 12 -> 9, of which waited for: 8 -> 7; matrix products, arithmetic and copies ran while one was open for 0% -> 0% of each run, Pallas kernels for 0% -> 0%
where the time goes in v3:
time: 98.8 us; the launch traced here: 98.3 us
  starting transfers between devices  47.4 us (48%)
  waiting for transfers between devices  20.7 us (21%)
  Pallas kernels  14.6 us (15%)
  blocking collectives  11.3 us (11%)
  local copies, waits for them, and re-layouts  3.42 us (3%)
    ppermute x4, starting transfers between devices, exchange(): return (lax.ppermute(near_block, axis, near), far_block)  19.8 us
    all_to_all x1, starting transfers between devices, per_device(): blocks = lax.all_to_all(packed_two, 'gx', 0, 0, tiled=True)  17.1 us
    ppermute x4, waiting for transfers between devices, exchange(): far_block = lax.ppermute(far_block, axis, far)  14.3 us
    all_to_all x1, blocking collectives, per_device(): strips = lax.all_to_all(strips, 'gy', 0, 0, tiled=True)  11.3 us
    ppermute x4, starting transfers between devices, exchange(): far_block = lax.ppermute(far_block, axis, far)  10.5 us
    ppermute x4, waiting for transfers between devices, exchange(): return (lax.ppermute(near_block, axis, near), far_block)  4.58 us
    pallas_call x1, Pallas kernels, per_device(): call(finish, [shape(3, B, B, 128), shape(B, B, 128)], [SMEM] + [VMEM] * 5...  4.57 us
    pallas_call x1, Pallas kernels, per_device(): call(advance, [shape(3, B, B, 128), shape(PX - 2, B, 128), shape(N_UNITS,...  4.26 us
  transfers between devices with their start and end apart: 9, of which 7 were waited for; matrix products, arithmetic and copies ran while one was open for 0% of the time, Pallas kernels for 0%

profile of v3, /device:TPU:1, one launch (start us, length us, event | category | flops | bytes accessed | tf_op | source)
XLA Modules:
  0.0 98.3 jit_solution(4502617206246114059)
XLA Ops:
  0.6 0.0 copy-start.5
  0.6 0.0 copy-start.6
  0.7 0.1 pad_add_fusion.place.refs_0_
  0.7 0.6 copy-done.5
  1.3 0.0 copy-done.6
  1.3 0.0 copy-start
  1.3 1.0 %copy-done = f32[3,16,16,128]{3,2,1,0:T(8,128)S(1)} copy-done((f32[3,16,16,128]{3,2,1,0:T(8,128)S(1)}, f32[3,16,16,128]{3,2,1,0:T(8,128)}, u32[]{:S(2)}) %copy-start) | copy-done | bytes 393240
  2.3 0.0 copy-start.2
  2.3 0.9 copy-done.2
  3.2 0.0 copy-start.4
  3.2 0.9 copy-done.4
  4.1 0.0 copy-start.1
  4.1 0.0 copy-start.3
  4.1 1.7 %shard_map.68 = (f32[41,16,128]{2,1,0:T(8,128)S(1)}, f32[41,16,128]{2,1,0:T(8,128)S(1)}, f32[16,16,128]{2,1,0:T(8,128)S(1)}) custom-call(s32[2]{0:T(128)S(1)} %pad_add_fusion.place.refs_0_, f32[16]{0:T(128)S(1)} %copy-done.6, s32[16,16]{1,0:T(8,128)S(1)} %copy-done.5, f32[3,16,16,128]{3,2,1,0:T(8,128)S(1)} %copy-done, f32[16,16,128]{2,1,0:T(8,128)S(1)} %copy-done.2, ...), custom_call_target="tpu_custom_call" | custom-call | tf_op jit(solution)/shard_map/pallas_call | solution.py:522
  5.8 8.8 %collective-permute-start = (f32[41,16,128]{2,1,0:T(8,128)S(1)}, f32[41,16,128]{2,1,0:T(8,128)S(1)}, u32[]{:S(2)}, u32[]{:S(2)}) collective-permute-start(f32[41,16,128]{2,1,0:T(8,128)S(1)} %get-tuple-element.21), channel_id=1, source_target_pairs={{0,8},{8,0},{16,24},{24,16},{32,40},{40,32},{48,56},{56,48},{64,72... | collective-permute-start | bytes 1007624 | tf_op jit(solution)/shard_map/ppermute | solution.py:515
  14.6 1.9 %collective-permute-start.1 = (f32[41,16,128]{2,1,0:T(8,128)S(1)}, f32[41,16,128]{2,1,0:T(8,128)S(1)}, u32[]{:S(2)}, u32[]{:S(2)}) collective-permute-start(f32[41,16,128]{2,1,0:T(8,128)S(1)} %get-tuple-element.22), channel_id=1, source_target_pairs={{0,504},{8,16},{16,8},{24,32},{32,24},{40,48},{48,40},{56,64},{64,... | collective-permute-start | bytes 1007624 | tf_op jit(solution)/shard_map/ppermute | solution.py:514
  16.6 0.0 collective-permute-done.near
  16.6 6.5 %collective-permute-done.1.far = f32[41,16,128]{2,1,0:T(8,128)S(1)} collective-permute-done((f32[41,16,128]{2,1,0:T(8,128)S(1)}, f32[41,16,128]{2,1,0:T(8,128)S(1)}, u32[]{:S(2)}, u32[]{:S(2)}) %collective-permute-start.1) | collective-permute-done | bytes 335904 | tf_op jit(solution)/shard_map/ppermute | solution.py:514
  23.1 0.0 copy-done.1
  23.1 0.0 copy-done.3
  23.1 0.7 shard_map.69
  23.9 1.9 %collective-permute-start.2 = (f32[8,40,128]{2,1,0:T(8,128)S(1)}, f32[8,40,128]{2,1,0:T(8,128)S(1)}, u32[]{:S(2)}, u32[]{:S(2)}) collective-permute-start(f32[8,40,128]{2,1,0:T(8,128)S(1)} %get-tuple-element.26), channel_id=1, source_target_pairs={{0,1},{1,0},{2,3},{3,2},{4,5},{5,4},{6,7},{7,6},{8,9},{9,8},{10,11... | collective-permute-start | bytes 491528 | tf_op jit(solution)/shard_map/ppermute | solution.py:515
  25.8 1.9 %collective-permute-start.3 = (f32[8,40,128]{2,1,0:T(8,128)S(1)}, f32[8,40,128]{2,1,0:T(8,128)S(1)}, u32[]{:S(2)}, u32[]{:S(2)}) collective-permute-start(f32[8,40,128]{2,1,0:T(8,128)S(1)} %get-tuple-element.27), channel_id=1, source_target_pairs={{0,7},{1,2},{2,1},{3,4},{4,3},{5,6},{6,5},{7,0},{8,15},{9,10},{10,... | collective-permute-start | bytes 491528 | tf_op jit(solution)/shard_map/ppermute | solution.py:514
  27.7 2.2 %collective-permute-done.2.near = f32[8,40,128]{2,1,0:T(8,128)S(1)} collective-permute-done((f32[8,40,128]{2,1,0:T(8,128)S(1)}, f32[8,40,128]{2,1,0:T(8,128)S(1)}, u32[]{:S(2)}, u32[]{:S(2)}) %collective-permute-start.2) | collective-permute-done | bytes 163872 | tf_op jit(solution)/shard_map/ppermute | solution.py:515
  29.9 4.0 %collective-permute-done.3.far = f32[8,40,128]{2,1,0:T(8,128)S(1)} collective-permute-done((f32[8,40,128]{2,1,0:T(8,128)S(1)}, f32[8,40,128]{2,1,0:T(8,128)S(1)}, u32[]{:S(2)}, u32[]{:S(2)}) %collective-permute-start.3) | collective-permute-done | bytes 163872 | tf_op jit(solution)/shard_map/ppermute | solution.py:514
  34.0 4.3 %shard_map.70 = (f32[3,16,16,128]{3,2,1,0:T(8,128)S(1)}, f32[28,16,128]{2,1,0:T(8,128)S(1)}, f32[92,4,128]{2,1,0:T(4,128)S(1)}, f32[92,4,128]{2,1,0:T(4,128)S(1)}) custom-call(s32[2]{0:T(128)S(1)} %pad_add_fusion.place.refs_0_, f32[3,34,16,128]{3,2,1,0:T(8,128)S(1)} %get-tuple-element.23.wide_v, f32[30,16,128]{2,1,0:T(8,128)S(1)} %get-tuple-element.24.wide_p, ...), custom_call_target="tpu_custom_call" | custom-call | tf_op jit(solution)/shard_map/pallas_call | solution.py:535
  38.2 2.4 %collective-permute-start.4 = (f32[92,4,128]{2,1,0:T(4,128)S(1)}, f32[92,4,128]{2,1,0:T(4,128)S(1)}, u32[]{:S(2)}, u32[]{:S(2)}) collective-permute-start(f32[92,4,128]{2,1,0:T(4,128)S(1)} %get-tuple-element.29), channel_id=1, source_target_pairs={{0,1},{1,0},{2,3},{3,2},{4,5},{5,4},{6,7},{7,6},{8,9},{9,8},{10,11... | collective-permute-start | bytes 565256 | tf_op jit(solution)/shard_map/ppermute | solution.py:515
  40.6 3.2 %collective-permute-start.5 = (f32[92,4,128]{2,1,0:T(4,128)S(1)}, f32[92,4,128]{2,1,0:T(4,128)S(1)}, u32[]{:S(2)}, u32[]{:S(2)}) collective-permute-start(f32[92,4,128]{2,1,0:T(4,128)S(1)} %get-tuple-element.30), channel_id=1, source_target_pairs={{0,7},{1,2},{2,1},{3,4},{4,3},{5,6},{6,5},{7,0},{8,15},{9,10},{10,... | collective-permute-start | bytes 565256 | tf_op jit(solution)/shard_map/ppermute | solution.py:514
  43.8 1.6 %collective-permute-done.4.near = f32[92,4,128]{2,1,0:T(4,128)S(1)} collective-permute-done((f32[92,4,128]{2,1,0:T(4,128)S(1)}, f32[92,4,128]{2,1,0:T(4,128)S(1)}, u32[]{:S(2)}, u32[]{:S(2)}) %collective-permute-start.4) | collective-permute-done | bytes 188448 | tf_op jit(solution)/shard_map/ppermute | solution.py:515
  45.4 3.7 %collective-permute-done.5.far = f32[92,4,128]{2,1,0:T(4,128)S(1)} collective-permute-done((f32[92,4,128]{2,1,0:T(4,128)S(1)}, f32[92,4,128]{2,1,0:T(4,128)S(1)}, u32[]{:S(2)}, u32[]{:S(2)}) %collective-permute-start.5) | collective-permute-done | bytes 188448 | tf_op jit(solution)/shard_map/ppermute | solution.py:514
  49.1 2.8 %shard_map.71 = (f32[22,24,128]{2,1,0:T(8,128)S(1)}, f32[20,24,128]{2,1,0:T(8,128)S(1)}, f32[2,16,128]{2,1,0:T(8,128)S(1)}, f32[64,4,128]{2,1,0:T(4,128)}) custom-call(s32[2]{0:T(128)S(1)} %pad_add_fusion.place.refs_0_, f32[28,16,128]{2,1,0:T(8,128)S(1)} %get-tuple-element.28.source, f32[30,16,128]{2,1,0:T(8,128)S(1)} %get-tuple-element.24.wide_p, ...), custom_call_target="tpu_custom_call" | custom-call | tf_op jit(solution)/shard_map/pallas_call | solution.py:542
  51.8 17.1 %all-to-all-start = ((f32[64,4,128]{2,1,0:T(4,128)}), f32[64,4,128]{2,1,0:T(4,128)S(1)}, u32[]{:S(2)}, u32[]{:S(2)}) async-start(f32[64,4,128]{2,1,0:T(4,128)} %get-tuple-element.31), calls=%async_computation | async-start | bytes 262144 | tf_op jit(solution)/shard_map/all_to_all | solution.py:549
  68.9 3.5 %collective-permute-start.7 = (f32[2,16,128]{2,1,0:T(8,128)S(1)}, f32[2,16,128]{2,1,0:T(8,128)S(1)}, u32[]{:S(2)}, u32[]{:S(2)}) collective-permute-start(f32[2,16,128]{2,1,0:T(8,128)S(1)} %get-tuple-element.32.refs_2_), channel_id=1, source_target_pairs={{0,504},{8,16},{16,8},{24,32},{32,24},{40,48},{48,40},{56,64},{64,... | collective-permute-start | bytes 49160 | tf_op jit(solution)/shard_map/ppermute | solution.py:514
  72.5 6.7 %collective-permute-start.6 = (f32[2,16,128]{2,1,0:T(8,128)S(1)}, f32[2,16,128]{2,1,0:T(8,128)S(1)}, u32[]{:S(2)}, u32[]{:S(2)}) collective-permute-start(f32[2,16,128]{2,1,0:T(8,128)S(1)} %get-tuple-element.32.refs_2_), channel_id=1, source_target_pairs={{0,8},{8,0},{16,24},{24,16},{32,40},{40,32},{48,56},{56,48},{64,72... | collective-permute-start | bytes 49160 | tf_op jit(solution)/shard_map/ppermute | solution.py:515
  79.2 0.0 collective-permute-done.7.refs_4_
  79.2 0.8 collective-permute-done.6.refs_3_
  80.0 1.8 %all-to-all-done.refs_1_ = f32[64,4,128]{2,1,0:T(4,128)S(1)} async-done(((f32[64,4,128]{2,1,0:T(4,128)}), f32[64,4,128]{2,1,0:T(4,128)S(1)}, u32[]{:S(2)}, u32[]{:S(2)}) %all-to-all-start) | async-done | bytes 131104 | tf_op jit(solution)/shard_map/all_to_all | solution.py:549
  81.8 0.6 shard_map.72
  82.4 11.3 %all_to_all.10.strips = f32[8,19,4,128]{3,2,1,0:T(4,128)S(1)} all-to-all(f32[8,19,4,128]{3,2,1,0:T(4,128)S(1)} %get-tuple-element.33), channel_id=1, replica_groups=mesh['gx'=64,'gy'=8] {'gy'}, dimensions={0} | all-to-all | bytes 622592 | tf_op jit(solution)/shard_map/all_to_all | solution.py:555
  93.7 4.6 %shard_map.73 = (f32[3,16,16,128]{3,2,1,0:T(8,128)}, f32[16,16,128]{2,1,0:T(8,128)}) custom-call(s32[2]{0:T(128)S(1)} %pad_add_fusion.place.refs_0_, f32[8,19,4,128]{3,2,1,0:T(4,128)S(1)} %all_to_all.10.strips, f32[6,16,128]{2,1,0:T(8,128)S(1)} %get-tuple-element.34.window, f32[22,24,128]{2,1,0:T(8,128)S(1)} %get-tuple-element.35.finest, ...), custom_call_target="tpu_custom_call" | custom-call | tf_op jit(solution)/shard_map/pallas_call | solution.py:556
Async XLA Ops:
  0.6 0.7 copy-start.5
  0.6 0.7 copy-start.6
  1.3 1.0 %copy-start = (f32[3,16,16,128]{3,2,1,0:T(8,128)S(1)}, f32[3,16,16,128]{3,2,1,0:T(8,128)}, u32[]{:S(2)}) copy-start(f32[3,16,16,128]{3,2,1,0:T(8,128)} %velocity.3) | copy-start | bytes 1179652
  2.3 0.9 copy-start.2
  3.2 0.9 copy-start.4
  4.1 19.0 %copy-start.1 = (f32[3,16,16,128]{3,2,1,0:T(8,128)S(1)}, f32[3,16,16,128]{3,2,1,0:T(8,128)}, u32[]{:S(2)}) copy-start(f32[3,16,16,128]{3,2,1,0:T(8,128)} %velocity.3) | copy-start | bytes 1179652
  4.1 19.0 %copy-start.3 = (f32[16,16,128]{2,1,0:T(8,128)S(1)}, f32[16,16,128]{2,1,0:T(8,128)}, u32[]{:S(2)}) copy-start(f32[16,16,128]{2,1,0:T(8,128)} %pressure.3) | copy-start | bytes 393220
  5.8 10.7 %collective-permute-start = (f32[41,16,128]{2,1,0:T(8,128)S(1)}, f32[41,16,128]{2,1,0:T(8,128)S(1)}, u32[]{:S(2)}, u32[]{:S(2)}) collective-permute-start(f32[41,16,128]{2,1,0:T(8,128)S(1)} %get-tuple-element.21), channel_id=1, source_target_pairs={{0,8},{8,0},{16,24},{24,16},{32,40},{40,32},{48,56},{56,48},{64,72... | collective-permute-start | bytes 1007624 | tf_op jit(solution)/shard_map/ppermute | solution.py:515
  14.6 8.5 %collective-permute-start.1 = (f32[41,16,128]{2,1,0:T(8,128)S(1)}, f32[41,16,128]{2,1,0:T(8,128)S(1)}, u32[]{:S(2)}, u32[]{:S(2)}) collective-permute-start(f32[41,16,128]{2,1,0:T(8,128)S(1)} %get-tuple-element.22), channel_id=1, source_target_pairs={{0,504},{8,16},{16,8},{24,32},{32,24},{40,48},{48,40},{56,64},{64,... | collective-permute-start | bytes 1007624 | tf_op jit(solution)/shard_map/ppermute | solution.py:514
  23.9 6.1 %collective-permute-start.2 = (f32[8,40,128]{2,1,0:T(8,128)S(1)}, f32[8,40,128]{2,1,0:T(8,128)S(1)}, u32[]{:S(2)}, u32[]{:S(2)}) collective-permute-start(f32[8,40,128]{2,1,0:T(8,128)S(1)} %get-tuple-element.26), channel_id=1, source_target_pairs={{0,1},{1,0},{2,3},{3,2},{4,5},{5,4},{6,7},{7,6},{8,9},{9,8},{10,11... | collective-permute-start | bytes 491528 | tf_op jit(solution)/shard_map/ppermute | solution.py:515
  25.8 8.2 %collective-permute-start.3 = (f32[8,40,128]{2,1,0:T(8,128)S(1)}, f32[8,40,128]{2,1,0:T(8,128)S(1)}, u32[]{:S(2)}, u32[]{:S(2)}) collective-permute-start(f32[8,40,128]{2,1,0:T(8,128)S(1)} %get-tuple-element.27), channel_id=1, source_target_pairs={{0,7},{1,2},{2,1},{3,4},{4,3},{5,6},{6,5},{7,0},{8,15},{9,10},{10,... | collective-permute-start | bytes 491528 | tf_op jit(solution)/shard_map/ppermute | solution.py:514
  38.2 7.1 %collective-permute-start.4 = (f32[92,4,128]{2,1,0:T(4,128)S(1)}, f32[92,4,128]{2,1,0:T(4,128)S(1)}, u32[]{:S(2)}, u32[]{:S(2)}) collective-permute-start(f32[92,4,128]{2,1,0:T(4,128)S(1)} %get-tuple-element.29), channel_id=1, source_target_pairs={{0,1},{1,0},{2,3},{3,2},{4,5},{5,4},{6,7},{7,6},{8,9},{9,8},{10,11... | collective-permute-start | bytes 565256 | tf_op jit(solution)/shard_map/ppermute | solution.py:515
  40.6 8.4 %collective-permute-start.5 = (f32[92,4,128]{2,1,0:T(4,128)S(1)}, f32[92,4,128]{2,1,0:T(4,128)S(1)}, u32[]{:S(2)}, u32[]{:S(2)}) collective-permute-start(f32[92,4,128]{2,1,0:T(4,128)S(1)} %get-tuple-element.30), channel_id=1, source_target_pairs={{0,7},{1,2},{2,1},{3,4},{4,3},{5,6},{6,5},{7,0},{8,15},{9,10},{10,... | collective-permute-start | bytes 565256 | tf_op jit(solution)/shard_map/ppermute | solution.py:514
  51.8 30.0 %all-to-all-start = ((f32[64,4,128]{2,1,0:T(4,128)}), f32[64,4,128]{2,1,0:T(4,128)S(1)}, u32[]{:S(2)}, u32[]{:S(2)}) async-start(f32[64,4,128]{2,1,0:T(4,128)} %get-tuple-element.31), calls=%async_computation | async-start | bytes 262144 | tf_op jit(solution)/shard_map/all_to_all | solution.py:549
  68.9 10.3 %collective-permute-start.7 = (f32[2,16,128]{2,1,0:T(8,128)S(1)}, f32[2,16,128]{2,1,0:T(8,128)S(1)}, u32[]{:S(2)}, u32[]{:S(2)}) collective-permute-start(f32[2,16,128]{2,1,0:T(8,128)S(1)} %get-tuple-element.32.refs_2_), channel_id=1, source_target_pairs={{0,504},{8,16},{16,8},{24,32},{32,24},{40,48},{48,40},{56,64},{64,... | collective-permute-start | bytes 49160 | tf_op jit(solution)/shard_map/ppermute | solution.py:514
  72.5 7.5 %collective-permute-start.6 = (f32[2,16,128]{2,1,0:T(8,128)S(1)}, f32[2,16,128]{2,1,0:T(8,128)S(1)}, u32[]{:S(2)}, u32[]{:S(2)}) collective-permute-start(f32[2,16,128]{2,1,0:T(8,128)S(1)} %get-tuple-element.32.refs_2_), channel_id=1, source_target_pairs={{0,8},{8,0},{16,24},{24,16},{32,40},{40,32},{48,56},{56,48},{64,72... | collective-permute-start | bytes 49160 | tf_op jit(solution)/shard_map/ppermute | solution.py:515

commit v4 on v3

--- a/solution.py
+++ b/solution.py
@@ -12,6 +12,7 @@
 PX = B + 2 * PH
 SIDE = 3 * VH + 2 * PH
 STEP = 0.1
+ROWS = 8
 EDDY = 0.03
 COEFF = 0.8 / 12.0
 WINDOW = 4
@@ -36,14 +37,14 @@
     return jax.ShapeDtypeStruct(dims, F32)
 
 
-def call(body, outs, specs, scratch=()):
+def call(body, outs, specs, scratch=(), grant=48, out_space=None):
     return pl.pallas_call(
         body,
         out_shape=outs,
         in_specs=specs,
-        out_specs=[VMEM] * len(outs),
+        out_specs=[out_space or VMEM] * len(outs),
         scratch_shapes=[pltpu.VMEM(s, F32) if isinstance(s, tuple) else s for s in scratch],
-        compiler_params=pltpu.CompilerParams(vmem_limit_bytes=48 * 1024 * 1024),
+        compiler_params=pltpu.CompilerParams(vmem_limit_bytes=grant * 1024 * 1024),
     )
 
 
@@ -66,8 +67,8 @@
 def pack_x(place, drag_table, land, velocity, pressure, turbine, near, far, drag, kinds_ref, cells_ref, sems):
     core = place[0] % 2
     copies = [
-        pltpu.make_async_copy(land, kinds_ref, sems.at[0]),
-        pltpu.make_async_copy(turbine, cells_ref, sems.at[1]),
+        pltpu.make_async_copy(turbine, cells_ref, sems.at[0]),
+        pltpu.make_async_copy(land, kinds_ref, sems.at[1]),
     ]
     for side, out in ((0, near), (1, far)):
         high = (core + side) % 2 == 0
@@ -86,18 +87,20 @@
         )
     for copy in copies:
         copy.start()
-    copies[0].wait()
+    copies[1].wait()
     kinds = kinds_ref[...]
     ground = jnp.zeros(kinds.shape, F32)
     for kind in range(16):
         ground = jnp.where(kinds == kind, drag_table[kind], ground)
     square = lax.broadcasted_iota(jnp.int32, (B, B), 0) == lax.broadcasted_iota(jnp.int32, (B, B), 1)
-    copies[1].wait()
+    columns = []
     for i in range(B):
         row = jnp.broadcast_to(ground[i : i + 1, :], (B, B))
-        column = jnp.sum(jnp.where(square, row, 0.0), axis=1, keepdims=True)
+        columns.append(jnp.sum(jnp.where(square, row, 0.0), axis=1, keepdims=True))
+    copies[0].wait()
+    for i in range(B):
         cells = cells_ref[i].astype(F32)
-        drag[i] = 2.0 * cells + jnp.where(lane_of(cells) == 0, column, 0.0)
+        drag[i] = 2.0 * cells + jnp.where(lane_of(cells) == 0, columns[i], 0.0)
 
     @pl.when(core == 0)
     def _():
@@ -160,10 +163,27 @@
         send(far_y, near_y)
 
 
+def exact_product(values, matrix):
+    flat = values.reshape(-1, 128)
+    high = flat.astype(jnp.bfloat16)
+    rest = flat - high.astype(F32)
+    middle = rest.astype(jnp.bfloat16)
+    low = (rest - middle.astype(F32)).astype(jnp.bfloat16)
+    parts = jnp.concatenate([high, middle, low], axis=1)
+    return jnp.dot(parts, matrix, preferred_element_type=F32).reshape(values.shape)
+
+
+def column_difference():
+    i = lax.broadcasted_iota(jnp.int32, (128, 128), 0)
+    j = lax.broadcasted_iota(jnp.int32, (128, 128), 1)
+    one = jnp.where(i - j == 1, 1.0, jnp.where(j - i == 1, -1.0, 0.0))
+    return jnp.concatenate([one.astype(jnp.bfloat16)] * 3, axis=0)
+
+
 def advance(place, wide_v, wide_p, wide_d, near, far, star, source, near_y, far_y, v, dr, tau, part):
     odd = place[1] % 2
     v[:, :, 0:B, :] = wide_v[...]
-    dr[:, 0:B, :] = wide_d[...]
+    dr[2 : 2 + PX, 0:B, :] = wide_d[...]
 
     def fill(low, high):
         for g in range(8):
@@ -175,8 +195,8 @@
                     v[a, x, B + 5 : B + 8, :] = low[g, rows, :]
                 if 2 <= x < 2 + PX:
                     row = slice(10 * j + 9, 10 * j + 10)
-                    dr[x - 2, B : B + 1, :] = high[g, row, :]
-                    dr[x - 2, B + 7 : B + 8, :] = low[g, row, :]
+                    dr[x, B : B + 1, :] = high[g, row, :]
+                    dr[x, B + 7 : B + 8, :] = low[g, row, :]
 
     @pl.when(odd == 0)
     def _():
@@ -186,21 +206,22 @@
     def _():
         fill(near, far)
 
-    def zero_shifts(values):
-        lane = lane_of(values)
-        return (
-            jnp.where(lane == 127, 0.0, turn(values, -1, 1)),
-            jnp.where(lane == 0, 0.0, turn(values, 1, 1)),
-        )
-
-    for i in range(1, VX - 1):
-        u = [v[a, i] for a in range(3)]
-        gx = [0.5 * (v[a, i + 1] - v[a, i - 1]) for a in range(3)]
-        gy = [0.5 * (turn(u[a], -1, 0) - turn(u[a], 1, 0)) for a in range(3)]
-        gz = []
-        for a in range(3):
-            above, below = zero_shifts(u[a])
-            gz.append(above - below)
+    difference = column_difference()
+
+    def along_column(fields):
+        n = fields[0].shape[0]
+        whole = exact_product(jnp.concatenate(fields, axis=0), difference)
+        return [whole[k * n : (k + 1) * n] for k in range(len(fields))]
+
+    def along_row(values):
+        return 0.5 * (turn(values, -1, 1) - turn(values, 1, 1))
+
+    for i in range(1, VX - 1, ROWS):
+        here = slice(i, i + ROWS)
+        u = [v[a, here] for a in range(3)]
+        gx = [0.5 * (v[a, i + 1 : i + 1 + ROWS] - v[a, i - 1 : i - 1 + ROWS]) for a in range(3)]
+        gy = [along_row(u[a]) for a in range(3)]
+        gz = along_column(u)
         e01 = gx[1] + gy[0]
         e02 = gx[2] + gz[0]
         e12 = gy[2] + gz[1]
@@ -208,38 +229,36 @@
             e01 * e01 + e02 * e02 + e12 * e12
         )
         visc = EDDY * jnp.sqrt(total)
-        tau[0, i] = 2.0 * visc * gx[0]
-        tau[1, i] = visc * e01
-        tau[2, i] = visc * e02
-        if i < 2 or i >= VX - 2:
-            continue
-        along_y = [visc * e01, 2.0 * visc * gy[1], visc * e12]
-        along_z = [visc * e02, visc * e12, 2.0 * visc * gz[2]]
+        t01 = visc * e01
+        t02 = visc * e02
+        t12 = visc * e12
+        tau[0, here] = 2.0 * visc * gx[0]
+        tau[1, here] = t01
+        tau[2, here] = t02
+        along_y = [along_row(t) for t in (t01, 2.0 * visc * gy[1], t12)]
+        along_z = along_column([t02, t12, 2.0 * visc * gz[2]])
         lane = lane_of(u[0])
         flat = u[0] * u[0] + u[1] * u[1]
         edge = jnp.where((lane == 0) | (lane == 127), EDDY * jnp.sqrt(flat + 2.0 * (u[2] * u[2])), 0.0)
-        wind = dr[i - 2] * jnp.sqrt(flat)
+        wind = dr[here] * jnp.sqrt(flat)
         for a in range(3):
-            change = 0.5 * (turn(along_y[a], -1, 0) - turn(along_y[a], 1, 0))
-            above, below = zero_shifts(along_z[a])
-            change = change + ((above - below) - (edge * u[a] if a < 2 else 2.0 * (edge * u[a])))
+            change = along_y[a] + (along_z[a] - (edge * u[a] if a < 2 else 2.0 * (edge * u[a])))
             change = change - (u[0] * gx[a] + u[1] * gy[a] + u[2] * gz[a])
             if a < 2:
                 change = change - wind * u[a]
             if a == 0:
                 change = change + 1.0
-            part[a, i] = u[a] + STEP * change
+            part[a, here] = u[a] + STEP * change
     for i in range(2, VX - 2):
         for a in range(3):
             part[a, i] = part[a, i] + (0.5 * STEP) * (tau[a, i + 1] - tau[a, i - 1])
     for a in range(3):
         star[a] = part[a, VH : VH + B, 0:B, :]
-    for i in range(3, VX - 3):
-        along_x = 0.5 * (part[0, i + 1] - part[0, i - 1])
-        s1 = part[1, i]
-        along_y = 0.5 * (turn(s1, -1, 0) - turn(s1, 1, 0))
-        above, below = zero_shifts(part[2, i])
-        source[i - 3] = ((along_x + along_y + (above - below)) / STEP)[0:B]
+    for i in range(3, VX - 3, 4):
+        along_x = 0.5 * (part[0, i + 1 : i + 5] - part[0, i - 1 : i + 3])
+        along_y = along_row(part[1, i : i + 4])
+        (along_z,) = along_column([part[2, i : i + 4, 0:B, :]])
+        source[i - 3 : i + 1] = ((along_x + along_y)[:, 0:B] + along_z) / STEP
 
     def send(up, down):
         for message, outer, inner in ((up, B - 4, B - 8), (down, 0, 4)):
@@ -262,16 +281,6 @@
     j = lax.broadcasted_iota(jnp.int32, (128, 128), 1)
     hit = (i - j == dz) | (j - i == dz) | ((i == j) & ((j < dz) | (j >= 128 - dz)))
     return jnp.concatenate([jnp.where(hit, 4.0, 0.0).astype(jnp.bfloat16)] * halves, axis=0)
-
-
-def exact_product(values, matrix):
-    flat = values.reshape(-1, 128)
-    high = flat.astype(jnp.bfloat16)
-    rest = flat - high.astype(F32)
-    middle = rest.astype(jnp.bfloat16)
-    low = (rest - middle.astype(F32)).astype(jnp.bfloat16)
-    parts = jnp.concatenate([high, middle, low], axis=1)
-    return jnp.dot(parts, matrix, preferred_element_type=F32).reshape(values.shape)
 
 
 def neighbours(ref, start, count, dy, dz, matrix=None):
@@ -523,7 +532,12 @@
         pack_x,
         [shape(SIDE, B, 128), shape(SIDE, B, 128), shape(B, B, 128)],
         [SMEM, SMEM] + [HBM] * 4,
-        [pltpu.VMEM((B, B), jnp.int32), pltpu.VMEM((B, B, 128), jnp.int32), pltpu.SemaphoreType.DMA((10,))],
+        [
+            pltpu.VMEM((B, B), jnp.int32),
+            pltpu.VMEM((B, B, 128), jnp.int32),
+            pltpu.SemaphoreType.DMA((10,)),
+        ],
+        60,
     )(place, surface_drag, land_type, velocity, pressure, turbine_cells)
     near, far = exchange(near, far, "gx")
     wide_v, wide_p, wide_d, near, far = call(
@@ -536,7 +550,7 @@
         advance,
         [shape(3, B, B, 128), shape(PX - 2, B, 128), shape(N_UNITS, 4, 128), shape(N_UNITS, 4, 128)],
         [SMEM] + [VMEM] * 5,
-        [(3, VX, 24, 128), (PX, 24, 128), (3, VX, 24, 128), (3, VX, 24, 128)],
+        [(3, VX, 24, 128), (VX, 24, 128), (3, VX, 24, 128), (3, VX, 24, 128)],
     )(place, wide_v, wide_p, wide_d, near, far)
     near, far = exchange(near, far, "gy")
     finest, right, packed_one, packed_two = call(

time: 98.8 us -> 97.2 us (0.984)
  local copies, waits for them, and re-layouts: 3.42 us -> 0.91 us
    unnamed x14 -> x8, local copies, waits for them, and re-layouts: 3.42 us -> 0.91 us
    ppermute x4, waiting for transfers between devices: 4.58 us -> 6.09 us  [exchange(): return (lax.ppermute(near_block, axis, near), far_block)]
    pallas_call x1, Pallas kernels: 1.69 us -> 2.95 us  [per_device(): call(pack_x, [shape(SIDE, B, 128), shape(SIDE, B, 128), shape(B, B, 128)]...]
    pallas_call x1, Pallas kernels: 4.26 us -> 3.22 us  [per_device(): call(advance, [shape(3, B, B, 128), shape(PX - 2, B, 128), shape(N_UNITS,...]
    ppermute x4, waiting for transfers between devices: 14.3 us -> 13.3 us  [exchange(): far_block = lax.ppermute(far_block, axis, far)]
where the time goes in v4:
time: 97.2 us; the launch traced here: 96.7 us
  starting transfers between devices  46.5 us (48%)
  waiting for transfers between devices  21.2 us (22%)
  Pallas kernels  14.8 us (15%)
  blocking collectives  11.9 us (12%)
    ppermute x4, starting transfers between devices, exchange(): return (lax.ppermute(near_block, axis, near), far_block)  19.6 us
    all_to_all x1, starting transfers between devices, per_device(): blocks = lax.all_to_all(packed_two, 'gx', 0, 0, tiled=True)  16.7 us
    ppermute x4, waiting for transfers between devices, exchange(): far_block = lax.ppermute(far_block, axis, far)  13.3 us
    all_to_all x1, blocking collectives, per_device(): strips = lax.all_to_all(strips, 'gy', 0, 0, tiled=True)  11.9 us
    ppermute x4, starting transfers between devices, exchange(): far_block = lax.ppermute(far_block, axis, far)  10.2 us
    ppermute x4, waiting for transfers between devices, exchange(): return (lax.ppermute(near_block, axis, near), far_block)  6.09 us
    pallas_call x1, Pallas kernels, per_device(): call(finish, [shape(3, B, B, 128), shape(B, B, 128)], [SMEM] + [VMEM] * 5...  4.57 us
    pallas_call x1, Pallas kernels, per_device(): call(advance, [shape(3, B, B, 128), shape(PX - 2, B, 128), shape(N_UNITS,...  3.22 us
  transfers between devices with their start and end apart: 9, of which 7 were waited for; matrix products, arithmetic and copies ran while one was open for 0% of the time, Pallas kernels for 0%

profile of v4, /device:TPU:1, one launch (start us, length us, event | category | flops | bytes accessed | tf_op | source)
XLA Modules:
  0.0 96.7 jit_solution(9627878175618741107)
XLA Ops:
  0.6 0.0 copy-start
  0.6 0.6 pad_add_fusion.place.refs_0_
  1.2 0.0 copy-start.1
  1.2 2.9 %shard_map.68 = (f32[41,16,128]{2,1,0:T(8,128)}, f32[41,16,128]{2,1,0:T(8,128)}, f32[16,16,128]{2,1,0:T(8,128)}) custom-call(s32[2]{0:T(128)} %pad_add_fusion.place.refs_0_, f32[16]{0:T(128)} %drag_table.1, s32[16,16]{1,0:T(8,128)} %land.1, f32[3,16,16,128]{3,2,1,0:T(8,128)} %velocity.3, f32[16,16,128]{2,1,0:T(8,128)} %pressure.3, s32[16,16,128]{2,1,0:T(8,128)} %turbine.1), custom_call_target="tpu_custom_call" | custom-call | tf_op jit(solution)/shard_map/pallas_call | solution.py:531
  4.2 8.8 %collective-permute-start = (f32[41,16,128]{2,1,0:T(8,128)}, f32[41,16,128]{2,1,0:T(8,128)S(1)}, u32[]{:S(2)}, u32[]{:S(2)}) collective-permute-start(f32[41,16,128]{2,1,0:T(8,128)} %get-tuple-element.21), channel_id=1, source_target_pairs={{0,8},{8,0},{16,24},{24,16},{32,40},{40,32},{48,56},{56,48},{64,72... | collective-permute-start | bytes 1007624 | tf_op jit(solution)/shard_map/ppermute | solution.py:524
  13.0 0.0 copy-start.3
  13.0 1.9 %collective-permute-start.1 = (f32[41,16,128]{2,1,0:T(8,128)}, f32[41,16,128]{2,1,0:T(8,128)S(1)}, u32[]{:S(2)}, u32[]{:S(2)}) collective-permute-start(f32[41,16,128]{2,1,0:T(8,128)} %get-tuple-element.22), channel_id=1, source_target_pairs={{0,504},{8,16},{16,8},{24,32},{32,24},{40,48},{48,40},{56,64},{64,... | collective-permute-start | bytes 1007624 | tf_op jit(solution)/shard_map/ppermute | solution.py:523
  14.9 0.0 collective-permute-done.near
  14.9 6.8 %collective-permute-done.1.far = f32[41,16,128]{2,1,0:T(8,128)S(1)} collective-permute-done((f32[41,16,128]{2,1,0:T(8,128)}, f32[41,16,128]{2,1,0:T(8,128)S(1)}, u32[]{:S(2)}, u32[]{:S(2)}) %collective-permute-start.1) | collective-permute-done | bytes 335904 | tf_op jit(solution)/shard_map/ppermute | solution.py:523
  21.7 0.0 copy-done
  21.7 0.0 copy-done.1
  21.7 0.0 copy-done.3
  21.7 0.0 copy-start.2
  21.7 0.9 copy-done.2
  22.6 0.7 shard_map.69
  23.3 1.9 %collective-permute-start.2 = (f32[8,40,128]{2,1,0:T(8,128)S(1)}, f32[8,40,128]{2,1,0:T(8,128)S(1)}, u32[]{:S(2)}, u32[]{:S(2)}) collective-permute-start(f32[8,40,128]{2,1,0:T(8,128)S(1)} %get-tuple-element.26), channel_id=1, source_target_pairs={{0,1},{1,0},{2,3},{3,2},{4,5},{5,4},{6,7},{7,6},{8,9},{9,8},{10,11... | collective-permute-start | bytes 491528 | tf_op jit(solution)/shard_map/ppermute | solution.py:524
  25.3 1.9 %collective-permute-start.3 = (f32[8,40,128]{2,1,0:T(8,128)S(1)}, f32[8,40,128]{2,1,0:T(8,128)S(1)}, u32[]{:S(2)}, u32[]{:S(2)}) collective-permute-start(f32[8,40,128]{2,1,0:T(8,128)S(1)} %get-tuple-element.27), channel_id=1, source_target_pairs={{0,7},{1,2},{2,1},{3,4},{4,3},{5,6},{6,5},{7,0},{8,15},{9,10},{10,... | collective-permute-start | bytes 491528 | tf_op jit(solution)/shard_map/ppermute | solution.py:523
  27.2 2.2 %collective-permute-done.2.near = f32[8,40,128]{2,1,0:T(8,128)S(1)} collective-permute-done((f32[8,40,128]{2,1,0:T(8,128)S(1)}, f32[8,40,128]{2,1,0:T(8,128)S(1)}, u32[]{:S(2)}, u32[]{:S(2)}) %collective-permute-start.2) | collective-permute-done | bytes 163872 | tf_op jit(solution)/shard_map/ppermute | solution.py:524
  29.4 4.0 %collective-permute-done.3.far = f32[8,40,128]{2,1,0:T(8,128)S(1)} collective-permute-done((f32[8,40,128]{2,1,0:T(8,128)S(1)}, f32[8,40,128]{2,1,0:T(8,128)S(1)}, u32[]{:S(2)}, u32[]{:S(2)}) %collective-permute-start.3) | collective-permute-done | bytes 163872 | tf_op jit(solution)/shard_map/ppermute | solution.py:523
  33.4 3.2 %shard_map.70 = (f32[3,16,16,128]{3,2,1,0:T(8,128)S(1)}, f32[28,16,128]{2,1,0:T(8,128)S(1)}, f32[92,4,128]{2,1,0:T(4,128)S(1)}, f32[92,4,128]{2,1,0:T(4,128)S(1)}) custom-call(s32[2]{0:T(128)S(1)} %copy-done.3, f32[3,34,16,128]{3,2,1,0:T(8,128)S(1)} %get-tuple-element.23.wide_v, f32[30,16,128]{2,1,0:T(8,128)S(1)} %get-tuple-element.24.wide_p, ...), custom_call_target="tpu_custom_call" | custom-call | tf_op jit(solution)/shard_map/pallas_call | solution.py:549
  36.7 2.2 %collective-permute-start.4 = (f32[92,4,128]{2,1,0:T(4,128)S(1)}, f32[92,4,128]{2,1,0:T(4,128)S(1)}, u32[]{:S(2)}, u32[]{:S(2)}) collective-permute-start(f32[92,4,128]{2,1,0:T(4,128)S(1)} %get-tuple-element.29), channel_id=1, source_target_pairs={{0,1},{1,0},{2,3},{3,2},{4,5},{5,4},{6,7},{7,6},{8,9},{9,8},{10,11... | collective-permute-start | bytes 565256 | tf_op jit(solution)/shard_map/ppermute | solution.py:524
  38.8 2.9 %collective-permute-start.5 = (f32[92,4,128]{2,1,0:T(4,128)S(1)}, f32[92,4,128]{2,1,0:T(4,128)S(1)}, u32[]{:S(2)}, u32[]{:S(2)}) collective-permute-start(f32[92,4,128]{2,1,0:T(4,128)S(1)} %get-tuple-element.30), channel_id=1, source_target_pairs={{0,7},{1,2},{2,1},{3,4},{4,3},{5,6},{6,5},{7,0},{8,15},{9,10},{10,... | collective-permute-start | bytes 565256 | tf_op jit(solution)/shard_map/ppermute | solution.py:523
  41.7 3.1 %collective-permute-done.4.near = f32[92,4,128]{2,1,0:T(4,128)S(1)} collective-permute-done((f32[92,4,128]{2,1,0:T(4,128)S(1)}, f32[92,4,128]{2,1,0:T(4,128)S(1)}, u32[]{:S(2)}, u32[]{:S(2)}) %collective-permute-start.4) | collective-permute-done | bytes 188448 | tf_op jit(solution)/shard_map/ppermute | solution.py:524
  44.8 2.5 %collective-permute-done.5.far = f32[92,4,128]{2,1,0:T(4,128)S(1)} collective-permute-done((f32[92,4,128]{2,1,0:T(4,128)S(1)}, f32[92,4,128]{2,1,0:T(4,128)S(1)}, u32[]{:S(2)}, u32[]{:S(2)}) %collective-permute-start.5) | collective-permute-done | bytes 188448 | tf_op jit(solution)/shard_map/ppermute | solution.py:523
  47.3 2.8 %shard_map.71 = (f32[22,24,128]{2,1,0:T(8,128)S(1)}, f32[20,24,128]{2,1,0:T(8,128)S(1)}, f32[2,16,128]{2,1,0:T(8,128)S(1)}, f32[64,4,128]{2,1,0:T(4,128)}) custom-call(s32[2]{0:T(128)S(1)} %copy-done.3, f32[28,16,128]{2,1,0:T(8,128)S(1)} %get-tuple-element.28.source, f32[30,16,128]{2,1,0:T(8,128)S(1)} %get-tuple-element.24.wide_p, ...), custom_call_target="tpu_custom_call" | custom-call | tf_op jit(solution)/shard_map/pallas_call | solution.py:556
  50.0 16.7 %all-to-all-start = ((f32[64,4,128]{2,1,0:T(4,128)}), f32[64,4,128]{2,1,0:T(4,128)S(1)}, u32[]{:S(2)}, u32[]{:S(2)}) async-start(f32[64,4,128]{2,1,0:T(4,128)} %get-tuple-element.31), calls=%async_computation | async-start | bytes 262144 | tf_op jit(solution)/shard_map/all_to_all | solution.py:563
  66.8 3.5 %collective-permute-start.7 = (f32[2,16,128]{2,1,0:T(8,128)S(1)}, f32[2,16,128]{2,1,0:T(8,128)S(1)}, u32[]{:S(2)}, u32[]{:S(2)}) collective-permute-start(f32[2,16,128]{2,1,0:T(8,128)S(1)} %get-tuple-element.32.refs_2_), channel_id=1, source_target_pairs={{0,504},{8,16},{16,8},{24,32},{32,24},{40,48},{48,40},{56,64},{64,... | collective-permute-start | bytes 49160 | tf_op jit(solution)/shard_map/ppermute | solution.py:523
  70.3 6.7 %collective-permute-start.6 = (f32[2,16,128]{2,1,0:T(8,128)S(1)}, f32[2,16,128]{2,1,0:T(8,128)S(1)}, u32[]{:S(2)}, u32[]{:S(2)}) collective-permute-start(f32[2,16,128]{2,1,0:T(8,128)S(1)} %get-tuple-element.32.refs_2_), channel_id=1, source_target_pairs={{0,8},{8,0},{16,24},{24,16},{32,40},{40,32},{48,56},{56,48},{64,72... | collective-permute-start | bytes 49160 | tf_op jit(solution)/shard_map/ppermute | solution.py:524
  77.0 0.0 collective-permute-done.7.refs_4_
  77.0 0.8 collective-permute-done.6.refs_3_
  77.8 1.8 %all-to-all-done.refs_1_ = f32[64,4,128]{2,1,0:T(4,128)S(1)} async-done(((f32[64,4,128]{2,1,0:T(4,128)}), f32[64,4,128]{2,1,0:T(4,128)S(1)}, u32[]{:S(2)}, u32[]{:S(2)}) %all-to-all-start) | async-done | bytes 131104 | tf_op jit(solution)/shard_map/all_to_all | solution.py:563
  79.7 0.6 shard_map.72
  80.3 11.9 %all_to_all.10.strips = f32[8,19,4,128]{3,2,1,0:T(4,128)S(1)} all-to-all(f32[8,19,4,128]{3,2,1,0:T(4,128)S(1)} %get-tuple-element.33), channel_id=1, replica_groups=mesh['gx'=64,'gy'=8] {'gy'}, dimensions={0} | all-to-all | bytes 622592 | tf_op jit(solution)/shard_map/all_to_all | solution.py:569
  92.2 4.6 %shard_map.73 = (f32[3,16,16,128]{3,2,1,0:T(8,128)}, f32[16,16,128]{2,1,0:T(8,128)}) custom-call(s32[2]{0:T(128)S(1)} %copy-done.3, f32[8,19,4,128]{3,2,1,0:T(4,128)S(1)} %all_to_all.10.strips, f32[6,16,128]{2,1,0:T(8,128)S(1)} %get-tuple-element.34.window, f32[22,24,128]{2,1,0:T(8,128)S(1)} %get-tuple-element.35.finest, ...), custom_call_target="tpu_custom_call" | custom-call | tf_op jit(solution)/shard_map/pallas_call | solution.py:570
Async XLA Ops:
  0.6 21.1 %copy-start = (f32[3,16,16,128]{3,2,1,0:T(8,128)S(1)}, f32[3,16,16,128]{3,2,1,0:T(8,128)}, u32[]{:S(2)}) copy-start(f32[3,16,16,128]{3,2,1,0:T(8,128)} %velocity.3) | copy-start | bytes 1179652
  1.2 20.5 %copy-start.1 = (f32[16,16,128]{2,1,0:T(8,128)S(1)}, f32[16,16,128]{2,1,0:T(8,128)}, u32[]{:S(2)}) copy-start(f32[16,16,128]{2,1,0:T(8,128)} %pressure.3) | copy-start | bytes 393220
  4.2 10.7 %collective-permute-start = (f32[41,16,128]{2,1,0:T(8,128)}, f32[41,16,128]{2,1,0:T(8,128)S(1)}, u32[]{:S(2)}, u32[]{:S(2)}) collective-permute-start(f32[41,16,128]{2,1,0:T(8,128)} %get-tuple-element.21), channel_id=1, source_target_pairs={{0,8},{8,0},{16,24},{24,16},{32,40},{40,32},{48,56},{56,48},{64,72... | collective-permute-start | bytes 1007624 | tf_op jit(solution)/shard_map/ppermute | solution.py:524
  13.0 8.7 %copy-start.3 = (s32[2]{0:T(128)S(1)}, s32[2]{0:T(128)}, u32[]{:S(2)}) copy-start(s32[2]{0:T(128)} %pad_add_fusion.place.refs_0_) | copy-start | bytes 28
  13.0 8.7 %collective-permute-start.1 = (f32[41,16,128]{2,1,0:T(8,128)}, f32[41,16,128]{2,1,0:T(8,128)S(1)}, u32[]{:S(2)}, u32[]{:S(2)}) collective-permute-start(f32[41,16,128]{2,1,0:T(8,128)} %get-tuple-element.22), channel_id=1, source_target_pairs={{0,504},{8,16},{16,8},{24,32},{32,24},{40,48},{48,40},{56,64},{64,... | collective-permute-start | bytes 1007624 | tf_op jit(solution)/shard_map/ppermute | solution.py:523
  21.7 0.9 copy-start.2
  23.3 6.1 %collective-permute-start.2 = (f32[8,40,128]{2,1,0:T(8,128)S(1)}, f32[8,40,128]{2,1,0:T(8,128)S(1)}, u32[]{:S(2)}, u32[]{:S(2)}) collective-permute-start(f32[8,40,128]{2,1,0:T(8,128)S(1)} %get-tuple-element.26), channel_id=1, source_target_pairs={{0,1},{1,0},{2,3},{3,2},{4,5},{5,4},{6,7},{7,6},{8,9},{9,8},{10,11... | collective-permute-start | bytes 491528 | tf_op jit(solution)/shard_map/ppermute | solution.py:524
  25.3 8.2 %collective-permute-start.3 = (f32[8,40,128]{2,1,0:T(8,128)S(1)}, f32[8,40,128]{2,1,0:T(8,128)S(1)}, u32[]{:S(2)}, u32[]{:S(2)}) collective-permute-start(f32[8,40,128]{2,1,0:T(8,128)S(1)} %get-tuple-element.27), channel_id=1, source_target_pairs={{0,7},{1,2},{2,1},{3,4},{4,3},{5,6},{6,5},{7,0},{8,15},{9,10},{10,... | collective-permute-start | bytes 491528 | tf_op jit(solution)/shard_map/ppermute | solution.py:523
  36.7 8.1 %collective-permute-start.4 = (f32[92,4,128]{2,1,0:T(4,128)S(1)}, f32[92,4,128]{2,1,0:T(4,128)S(1)}, u32[]{:S(2)}, u32[]{:S(2)}) collective-permute-start(f32[92,4,128]{2,1,0:T(4,128)S(1)} %get-tuple-element.29), channel_id=1, source_target_pairs={{0,1},{1,0},{2,3},{3,2},{4,5},{5,4},{6,7},{7,6},{8,9},{9,8},{10,11... | collective-permute-start | bytes 565256 | tf_op jit(solution)/shard_map/ppermute | solution.py:524
  38.8 8.4 %collective-permute-start.5 = (f32[92,4,128]{2,1,0:T(4,128)S(1)}, f32[92,4,128]{2,1,0:T(4,128)S(1)}, u32[]{:S(2)}, u32[]{:S(2)}) collective-permute-start(f32[92,4,128]{2,1,0:T(4,128)S(1)} %get-tuple-element.30), channel_id=1, source_target_pairs={{0,7},{1,2},{2,1},{3,4},{4,3},{5,6},{6,5},{7,0},{8,15},{9,10},{10,... | collective-permute-start | bytes 565256 | tf_op jit(solution)/shard_map/ppermute | solution.py:523
  50.0 29.6 %all-to-all-start = ((f32[64,4,128]{2,1,0:T(4,128)}), f32[64,4,128]{2,1,0:T(4,128)S(1)}, u32[]{:S(2)}, u32[]{:S(2)}) async-start(f32[64,4,128]{2,1,0:T(4,128)} %get-tuple-element.31), calls=%async_computation | async-start | bytes 262144 | tf_op jit(solution)/shard_map/all_to_all | solution.py:563
  66.8 10.3 %collective-permute-start.7 = (f32[2,16,128]{2,1,0:T(8,128)S(1)}, f32[2,16,128]{2,1,0:T(8,128)S(1)}, u32[]{:S(2)}, u32[]{:S(2)}) collective-permute-start(f32[2,16,128]{2,1,0:T(8,128)S(1)} %get-tuple-element.32.refs_2_), channel_id=1, source_target_pairs={{0,504},{8,16},{16,8},{24,32},{32,24},{40,48},{48,40},{56,64},{64,... | collective-permute-start | bytes 49160 | tf_op jit(solution)/shard_map/ppermute | solution.py:523
  70.3 7.5 %collective-permute-start.6 = (f32[2,16,128]{2,1,0:T(8,128)S(1)}, f32[2,16,128]{2,1,0:T(8,128)S(1)}, u32[]{:S(2)}, u32[]{:S(2)}) collective-permute-start(f32[2,16,128]{2,1,0:T(8,128)S(1)} %get-tuple-element.32.refs_2_), channel_id=1, source_target_pairs={{0,8},{8,0},{16,24},{24,16},{32,40},{40,32},{48,56},{56,48},{64,72... | collective-permute-start | bytes 49160 | tf_op jit(solution)/shard_map/ppermute | solution.py:524

commit v5 on v4

--- a/solution.py
+++ b/solution.py
@@ -19,17 +19,10 @@
 VMEM = pl.BlockSpec(memory_space=pltpu.VMEM)
 SMEM = pl.BlockSpec(memory_space=pltpu.SMEM)
 HBM = pl.BlockSpec(memory_space=pltpu.HBM)
-UNITS = (
-    (0, 0, 5, 18, True),
-    (18, 0, 5, 18, False),
-    (36, 0, 1, 4, False),
-    (40, 0, 23, 4, False),
-    (44, 1, 5, 20, True),
-    (64, 1, 5, 20, False),
-    (84, 1, 1, 4, False),
-    (88, 1, 25, 4, False),
-)
-N_UNITS = 92
+S_UNITS = ((0, 5, 18, True), (18, 5, 18, False), (36, 1, 4, False), (40, 23, 4, False))
+P_UNITS = ((0, 5, 20, True), (20, 5, 20, False), (40, 1, 4, False), (44, 25, 4, False))
+N_S = 44
+N_P = 48
 F32 = jnp.float32
 
 
@@ -64,8 +57,40 @@
     return pltpu.roll(values, amount % values.shape[dim], dim)
 
 
-def pack_x(place, drag_table, land, velocity, pressure, turbine, near, far, drag, kinds_ref, cells_ref, sems):
-    core = place[0] % 2
+def ground_columns(kinds, drag_table):
+    ground = jnp.zeros(kinds.shape, F32)
+    for kind in range(16):
+        ground = jnp.where(kinds == kind, drag_table[kind], ground)
+    square = lax.broadcasted_iota(jnp.int32, (B, B), 0) == lax.broadcasted_iota(jnp.int32, (B, B), 1)
+    columns = []
+    for i in range(B):
+        row = jnp.broadcast_to(ground[i : i + 1, :], (B, B))
+        columns.append(jnp.sum(jnp.where(square, row, 0.0), axis=1, keepdims=True))
+    return columns
+
+
+def drag_row(cells, column):
+    return 2.0 * cells.astype(F32) + jnp.where(lane_of(cells) == 0, column, 0.0)
+
+
+def edge_units(units, field, up, down):
+    for message, outer, inner in ((up, B - 4, B - 8), (down, 0, 4)):
+        for unit, start, count, deep in units:
+            first = inner if deep else outer
+            message[unit : unit + count] = field[start : start + count, first : first + 4, :]
+
+
+def place_units(units, field, shift, low, high):
+    for unit, start, count, deep in units:
+        rows = slice(start + shift, start + shift + count)
+        first = B + 4 if deep else B
+        field[rows, first : first + 4, :] = high[unit : unit + count]
+        first = B + 8 if deep else B + 12
+        field[rows, first : first + 4, :] = low[unit : unit + count]
+
+
+def pack_x(drag_table, land, velocity, pressure, turbine, near, far, kinds_ref, cells_ref, drag, sems):
+    core = lax.axis_index("gx") % 2
     copies = [
         pltpu.make_async_copy(turbine, cells_ref, sems.at[0]),
         pltpu.make_async_copy(land, kinds_ref, sems.at[1]),
@@ -88,19 +113,10 @@
     for copy in copies:
         copy.start()
     copies[1].wait()
-    kinds = kinds_ref[...]
-    ground = jnp.zeros(kinds.shape, F32)
-    for kind in range(16):
-        ground = jnp.where(kinds == kind, drag_table[kind], ground)
-    square = lax.broadcasted_iota(jnp.int32, (B, B), 0) == lax.broadcasted_iota(jnp.int32, (B, B), 1)
-    columns = []
-    for i in range(B):
-        row = jnp.broadcast_to(ground[i : i + 1, :], (B, B))
-        columns.append(jnp.sum(jnp.where(square, row, 0.0), axis=1, keepdims=True))
+    columns = ground_columns(kinds_ref[...], drag_table)
     copies[0].wait()
     for i in range(B):
-        cells = cells_ref[i].astype(F32)
-        drag[i] = 2.0 * cells + jnp.where(lane_of(cells) == 0, columns[i], 0.0)
+        drag[i] = drag_row(cells_ref[i], columns[i])
 
     @pl.when(core == 0)
     def _():
@@ -116,13 +132,15 @@
         copy.wait()
 
 
-def widen_x(place, velocity, pressure, drag, near, far, wide_v, wide_p, wide_d, near_y, far_y):
+def widen_x(place, drag_table, land, velocity, pressure, turbine, near, far, wide_v, wide_p, wide_d, near_y, far_y, near_p, far_p):
     core = place[0] % 2
     odd = place[1] % 2
+    columns = ground_columns(land[...], drag_table)
+    for i in range(B):
+        wide_d[PH + i] = drag_row(turbine[i], columns[i])
     for a in range(3):
         wide_v[a, VH : VH + B] = velocity[a]
     wide_p[PH : PH + B] = pressure[...]
-    wide_d[PH : PH + B] = drag[...]
 
     def fill(low, high):
         for a in range(3):
@@ -157,10 +175,12 @@
     @pl.when(odd == 0)
     def _():
         send(near_y, far_y)
+        edge_units(P_UNITS, wide_p, near_p, far_p)
 
     @pl.when(odd == 1)
     def _():
         send(far_y, near_y)
+        edge_units(P_UNITS, wide_p, far_p, near_p)
 
 
 def exact_product(values, matrix):
@@ -180,7 +200,7 @@
     return jnp.concatenate([one.astype(jnp.bfloat16)] * 3, axis=0)
 
 
-def advance(place, wide_v, wide_p, wide_d, near, far, star, source, near_y, far_y, v, dr, tau, part):
+def advance(place, wide_v, wide_d, near, far, star, source, near_y, far_y, v, dr, tau, part):
     odd = place[1] % 2
     v[:, :, 0:B, :] = wide_v[...]
     dr[2 : 2 + PX, 0:B, :] = wide_d[...]
@@ -260,20 +280,13 @@
         (along_z,) = along_column([part[2, i : i + 4, 0:B, :]])
         source[i - 3 : i + 1] = ((along_x + along_y)[:, 0:B] + along_z) / STEP
 
-    def send(up, down):
-        for message, outer, inner in ((up, B - 4, B - 8), (down, 0, 4)):
-            for unit, kind, start, count, deep in UNITS:
-                field = source if kind == 0 else wide_p
-                first = inner if deep else outer
-                message[unit : unit + count] = field[start : start + count, first : first + 4, :]
-
     @pl.when(odd == 0)
     def _():
-        send(near_y, far_y)
+        edge_units(S_UNITS, source, near_y, far_y)
 
     @pl.when(odd == 1)
     def _():
-        send(far_y, near_y)
+        edge_units(S_UNITS, source, far_y, near_y)
 
 
 def column_sum(dz, halves):
@@ -319,27 +332,20 @@
     return 0.5 * total
 
 
-def presmooth(place, source, wide_p, near, far, finest, right, packed_one, packed_two, p, s, q, f1, a1, b1):
+def presmooth(place, source, wide_p, near, far, near_p, far_p, finest, right, packed_one, packed_two, p, s, q, f1, a1, b1):
     odd = place[1] % 2
     p[:, 0:B, :] = wide_p[...]
     s[1 : PX - 1, 0:B, :] = source[...]
 
-    def fill(low, high):
-        for unit, kind, start, count, deep in UNITS:
-            field = s if kind == 0 else p
-            rows = slice(start + 1 - kind, start + 1 - kind + count)
-            first = B + 4 if deep else B
-            field[rows, first : first + 4, :] = high[unit : unit + count]
-            first = B + 8 if deep else B + 12
-            field[rows, first : first + 4, :] = low[unit : unit + count]
-
     @pl.when(odd == 0)
     def _():
-        fill(far, near)
+        place_units(S_UNITS, s, 1, far, near)
+        place_units(P_UNITS, p, 0, far_p, near_p)
 
     @pl.when(odd == 1)
     def _():
-        fill(near, far)
+        place_units(S_UNITS, s, 1, near, far)
+        place_units(P_UNITS, p, 0, near_p, far_p)
 
     fine = column_sum(1, 3)
     coarse = column_sum(2, 3)
@@ -528,37 +534,41 @@
     gx = lax.axis_size("gx")
     gy = lax.axis_size("gy")
     place = jnp.stack([lax.axis_index("gx"), lax.axis_index("gy")]).astype(jnp.int32)
-    near, far, drag = call(
+    near, far = call(
         pack_x,
-        [shape(SIDE, B, 128), shape(SIDE, B, 128), shape(B, B, 128)],
-        [SMEM, SMEM] + [HBM] * 4,
+        [shape(SIDE, B, 128), shape(SIDE, B, 128)],
+        [SMEM] + [HBM] * 4,
         [
             pltpu.VMEM((B, B), jnp.int32),
             pltpu.VMEM((B, B, 128), jnp.int32),
+            (B, B, 128),
             pltpu.SemaphoreType.DMA((10,)),
         ],
         60,
-    )(place, surface_drag, land_type, velocity, pressure, turbine_cells)
+    )(surface_drag, land_type, velocity, pressure, turbine_cells)
     near, far = exchange(near, far, "gx")
-    wide_v, wide_p, wide_d, near, far = call(
+    wide_v, wide_p, wide_d, near, far, near_p, far_p = call(
         widen_x,
-        [shape(3, VX, B, 128), shape(PX, B, 128), shape(PX, B, 128), shape(8, 40, 128), shape(8, 40, 128)],
-        [SMEM] + [VMEM] * 5,
-    )(place, velocity, pressure, drag, near, far)
+        [shape(3, VX, B, 128), shape(PX, B, 128), shape(PX, B, 128)]
+        + [shape(8, 40, 128)] * 2
+        + [shape(N_P, 4, 128)] * 2,
+        [SMEM, SMEM] + [VMEM] * 6,
+    )(place, surface_drag, land_type, velocity, pressure, turbine_cells, near, far)
     near, far = exchange(near, far, "gy")
+    near_p, far_p = exchange(near_p, far_p, "gy")
     star, source, near, far = call(
         advance,
-        [shape(3, B, B, 128), shape(PX - 2, B, 128), shape(N_UNITS, 4, 128), shape(N_UNITS, 4, 128)],
-        [SMEM] + [VMEM] * 5,
+        [shape(3, B, B, 128), shape(PX - 2, B, 128), shape(N_S, 4, 128), shape(N_S, 4, 128)],
+        [SMEM] + [VMEM] * 4,
         [(3, VX, 24, 128), (VX, 24, 128), (3, VX, 24, 128), (3, VX, 24, 128)],
-    )(place, wide_v, wide_p, wide_d, near, far)
+    )(place, wide_v, wide_d, near, far)
     near, far = exchange(near, far, "gy")
     finest, right, packed_one, packed_two = call(
         presmooth,
         [shape(22, 24, 128), shape(20, 24, 128), shape(2, B, 128), shape(gx, 4, 128)],
-        [SMEM] + [VMEM] * 4,
+        [SMEM] + [VMEM] * 6,
         [(PX, 32, 128)] * 3 + [(12, 32, 128)] * 3,
-    )(place, source, wide_p, near, far)
+    )(place, source, wide_p, near, far, near_p, far_p)
     near, far = exchange(packed_one, packed_one, "gx")
     blocks = lax.all_to_all(packed_two, "gx", 0, 0, tiled=True)
     strips, window = call(

time: 97.2 us -> 94.4 us (0.971)
  starting transfers between devices: 46.5 us -> 54.9 us
  waiting for transfers between devices: 21.2 us -> 13.5 us
  blocking collectives: 11.9 us -> 9.62 us
    ppermute x4 -> x5, waiting for transfers between devices: 6.09 us -> 1.43 us  [exchange(): return (lax.ppermute(near_block, axis, near), far_block)]
    ppermute x4 -> x5, starting transfers between devices: 10.2 us -> 14.5 us  [exchange(): far_block = lax.ppermute(far_block, axis, far)]
    ppermute x4 -> x5, starting transfers between devices: 19.6 us -> 22.8 us  [exchange(): return (lax.ppermute(near_block, axis, near), far_block)]
    ppermute x4 -> x5, waiting for transfers between devices: 13.3 us -> 10.3 us  [exchange(): far_block = lax.ppermute(far_block, axis, far)]
    all_to_all x1, blocking collectives: 11.9 us -> 9.62 us  [per_device(): strips = lax.all_to_all(strips, 'gy', 0, 0, tiled=True)]
  transfers between devices with their start and end apart: 9 -> 11, of which waited for: 7 -> 5; matrix products, arithmetic and copies ran while one was open for 0% -> 0% of each run, Pallas kernels for 0% -> 3%
where the time goes in v5:
time: 94.4 us; the launch traced here: 93.9 us
  starting transfers between devices  54.9 us (58%)
  Pallas kernels  14.9 us (16%)
  waiting for transfers between devices  13.5 us (14%)
  blocking collectives  9.62 us (10%)
    ppermute x5, starting transfers between devices, exchange(): return (lax.ppermute(near_block, axis, near), far_block)  22.8 us
    all_to_all x1, starting transfers between devices, per_device(): blocks = lax.all_to_all(packed_two, 'gx', 0, 0, tiled=True)  17.5 us
    ppermute x5, starting transfers between devices, exchange(): far_block = lax.ppermute(far_block, axis, far)  14.5 us
    ppermute x5, waiting for transfers between devices, exchange(): far_block = lax.ppermute(far_block, axis, far)  10.3 us
    all_to_all x1, blocking collectives, per_device(): strips = lax.all_to_all(strips, 'gy', 0, 0, tiled=True)  9.62 us
    pallas_call x1, Pallas kernels, per_device(): call(finish, [shape(3, B, B, 128), shape(B, B, 128)], [SMEM] + [VMEM] * 5...  4.57 us
    pallas_call x1, Pallas kernels, per_device(): call(advance, [shape(3, B, B, 128), shape(PX - 2, B, 128), shape(N_S, 4,...  3.2 us
    pallas_call x1, Pallas kernels, per_device(): call(pack_x, [shape(SIDE, B, 128), shape(SIDE, B, 128)], [SMEM] + [HBM] *...  2.91 us
  transfers between devices with their start and end apart: 11, of which 5 were waited for; matrix products, arithmetic and copies ran while one was open for 0% of the time, Pallas kernels for 3%

profile of v5, /device:TPU:1, one launch (start us, length us, event | category | flops | bytes accessed | tf_op | source)
XLA Modules:
  0.0 93.9 jit_solution(1022957349734191557)
XLA Ops:
  0.6 0.0 copy-start.2
  0.6 0.0 copy-start.1
  0.6 0.0 copy-start
  0.7 2.9 %shard_map.68 = (f32[41,16,128]{2,1,0:T(8,128)}, f32[41,16,128]{2,1,0:T(8,128)}) custom-call(f32[16]{0:T(128)} %drag_table.3, s32[16,16]{1,0:T(8,128)} %land.3, f32[3,16,16,128]{3,2,1,0:T(8,128)} %velocity.3, f32[16,16,128]{2,1,0:T(8,128)} %pressure.3, s32[16,16,128]{2,1,0:T(8,128)} %turbine.3), custom_call_target="tpu_custom_call" | custom-call | tf_op jit(solution)/shard_map/pallas_call | solution.py:537
  3.6 8.8 %collective-permute-start = (f32[41,16,128]{2,1,0:T(8,128)}, f32[41,16,128]{2,1,0:T(8,128)S(1)}, u32[]{:S(2)}, u32[]{:S(2)}) collective-permute-start(f32[41,16,128]{2,1,0:T(8,128)} %get-tuple-element.21), channel_id=1, source_target_pairs={{0,8},{8,0},{16,24},{24,16},{32,40},{40,32},{48,56},{56,48},{64,72... | collective-permute-start | bytes 1007624 | tf_op jit(solution)/shard_map/ppermute | solution.py:530
  12.4 1.9 %collective-permute-start.1 = (f32[41,16,128]{2,1,0:T(8,128)}, f32[41,16,128]{2,1,0:T(8,128)S(1)}, u32[]{:S(2)}, u32[]{:S(2)}) collective-permute-start(f32[41,16,128]{2,1,0:T(8,128)} %get-tuple-element.22), channel_id=1, source_target_pairs={{0,504},{8,16},{16,8},{24,32},{32,24},{40,48},{48,40},{56,64},{64,... | collective-permute-start | bytes 1007624 | tf_op jit(solution)/shard_map/ppermute | solution.py:529
  14.3 0.0 copy-start.3
  14.3 0.0 copy-start.4
  14.3 0.1 pad_add_fusion.place.refs_0_
  14.4 0.0 collective-permute-done.near
  14.4 6.7 %collective-permute-done.1.far = f32[41,16,128]{2,1,0:T(8,128)S(1)} collective-permute-done((f32[41,16,128]{2,1,0:T(8,128)}, f32[41,16,128]{2,1,0:T(8,128)S(1)}, u32[]{:S(2)}, u32[]{:S(2)}) %collective-permute-start.1) | collective-permute-done | bytes 335904 | tf_op jit(solution)/shard_map/ppermute | solution.py:529
  21.1 0.0 copy-done.2
  21.1 0.0 copy-done.1
  21.1 0.0 copy-done
  21.1 0.0 copy-done.3
  21.1 0.0 copy-done.4
  21.1 0.8 shard_map.69
  21.9 1.9 %collective-permute-start.2 = (f32[8,40,128]{2,1,0:T(8,128)S(1)}, f32[8,40,128]{2,1,0:T(8,128)S(1)}, u32[]{:S(2)}, u32[]{:S(2)}) collective-permute-start(f32[8,40,128]{2,1,0:T(8,128)S(1)} %get-tuple-element.25), channel_id=1, source_target_pairs={{0,1},{1,0},{2,3},{3,2},{4,5},{5,4},{6,7},{7,6},{8,9},{9,8},{10,11... | collective-permute-start | bytes 491528 | tf_op jit(solution)/shard_map/ppermute | solution.py:530
  23.9 1.9 %collective-permute-start.3 = (f32[8,40,128]{2,1,0:T(8,128)S(1)}, f32[8,40,128]{2,1,0:T(8,128)S(1)}, u32[]{:S(2)}, u32[]{:S(2)}) collective-permute-start(f32[8,40,128]{2,1,0:T(8,128)S(1)} %get-tuple-element.26), channel_id=1, source_target_pairs={{0,7},{1,2},{2,1},{3,4},{4,3},{5,6},{6,5},{7,0},{8,15},{9,10},{10,... | collective-permute-start | bytes 491528 | tf_op jit(solution)/shard_map/ppermute | solution.py:529
  25.8 3.4 %collective-permute-start.6 = (f32[48,4,128]{2,1,0:T(4,128)S(1)}, f32[48,4,128]{2,1,0:T(4,128)S(1)}, u32[]{:S(2)}, u32[]{:S(2)}) collective-permute-start(f32[48,4,128]{2,1,0:T(4,128)S(1)} %get-tuple-element.31), channel_id=1, source_target_pairs={{0,1},{1,0},{2,3},{3,2},{4,5},{5,4},{6,7},{7,6},{8,9},{9,8},{10,11... | collective-permute-start | bytes 294920 | tf_op jit(solution)/shard_map/ppermute | solution.py:530
  29.2 4.0 %collective-permute-start.7 = (f32[48,4,128]{2,1,0:T(4,128)S(1)}, f32[48,4,128]{2,1,0:T(4,128)S(1)}, u32[]{:S(2)}, u32[]{:S(2)}) collective-permute-start(f32[48,4,128]{2,1,0:T(4,128)S(1)} %get-tuple-element.32), channel_id=1, source_target_pairs={{0,7},{1,2},{2,1},{3,4},{4,3},{5,6},{6,5},{7,0},{8,15},{9,10},{10,... | collective-permute-start | bytes 294920 | tf_op jit(solution)/shard_map/ppermute | solution.py:529
  33.2 0.0 collective-permute-done.2.near
  33.2 0.0 collective-permute-done.3.far
  33.2 3.2 %shard_map.70 = (f32[3,16,16,128]{3,2,1,0:T(8,128)S(1)}, f32[28,16,128]{2,1,0:T(8,128)S(1)}, f32[44,4,128]{2,1,0:T(4,128)S(1)}, f32[44,4,128]{2,1,0:T(4,128)S(1)}) custom-call(s32[2]{0:T(128)S(1)} %pad_add_fusion.place.refs_0_, f32[3,34,16,128]{3,2,1,0:T(8,128)S(1)} %get-tuple-element.23.wide_v, f32[30,16,128]{2,1,0:T(8,128)S(1)} %get-tuple-element.24.wide_d, ...), custom_call_target="tpu_custom_call" | custom-call | tf_op jit(solution)/shard_map/pallas_call | solution.py:559
  36.4 2.2 %collective-permute-start.4 = (f32[44,4,128]{2,1,0:T(4,128)S(1)}, f32[44,4,128]{2,1,0:T(4,128)S(1)}, u32[]{:S(2)}, u32[]{:S(2)}) collective-permute-start(f32[44,4,128]{2,1,0:T(4,128)S(1)} %get-tuple-element.29), channel_id=1, source_target_pairs={{0,1},{1,0},{2,3},{3,2},{4,5},{5,4},{6,7},{7,6},{8,9},{9,8},{10,11... | collective-permute-start | bytes 270344 | tf_op jit(solution)/shard_map/ppermute | solution.py:530
  38.6 3.1 %collective-permute-start.5 = (f32[44,4,128]{2,1,0:T(4,128)S(1)}, f32[44,4,128]{2,1,0:T(4,128)S(1)}, u32[]{:S(2)}, u32[]{:S(2)}) collective-permute-start(f32[44,4,128]{2,1,0:T(4,128)S(1)} %get-tuple-element.30), channel_id=1, source_target_pairs={{0,7},{1,2},{2,1},{3,4},{4,3},{5,6},{6,5},{7,0},{8,15},{9,10},{10,... | collective-permute-start | bytes 270344 | tf_op jit(solution)/shard_map/ppermute | solution.py:529
  41.7 0.0 collective-permute-done.6.near_p
  41.7 0.0 collective-permute-done.7.far_p
  41.8 0.6 collective-permute-done.4.near
  42.4 3.6 %collective-permute-done.5.far = f32[44,4,128]{2,1,0:T(4,128)S(1)} collective-permute-done((f32[44,4,128]{2,1,0:T(4,128)S(1)}, f32[44,4,128]{2,1,0:T(4,128)S(1)}, u32[]{:S(2)}, u32[]{:S(2)}) %collective-permute-start.5) | collective-permute-done | bytes 90144 | tf_op jit(solution)/shard_map/ppermute | solution.py:529
  46.0 2.8 %shard_map.71 = (f32[22,24,128]{2,1,0:T(8,128)S(1)}, f32[20,24,128]{2,1,0:T(8,128)S(1)}, f32[2,16,128]{2,1,0:T(8,128)S(1)}, f32[64,4,128]{2,1,0:T(4,128)}) custom-call(s32[2]{0:T(128)S(1)} %pad_add_fusion.place.refs_0_, f32[28,16,128]{2,1,0:T(8,128)S(1)} %get-tuple-element.27.source, f32[30,16,128]{2,1,0:T(8,128)S(1)} %get-tuple-element.28.wide_p, ...), custom_call_target="tpu_custom_call" | custom-call | tf_op jit(solution)/shard_map/pallas_call | solution.py:566
  48.7 17.5 %all-to-all-start = ((f32[64,4,128]{2,1,0:T(4,128)}), f32[64,4,128]{2,1,0:T(4,128)S(1)}, u32[]{:S(2)}, u32[]{:S(2)}) async-start(f32[64,4,128]{2,1,0:T(4,128)} %get-tuple-element.33), calls=%async_computation | async-start | bytes 262144 | tf_op jit(solution)/shard_map/all_to_all | solution.py:573
  66.3 3.5 %collective-permute-start.9 = (f32[2,16,128]{2,1,0:T(8,128)S(1)}, f32[2,16,128]{2,1,0:T(8,128)S(1)}, u32[]{:S(2)}, u32[]{:S(2)}) collective-permute-start(f32[2,16,128]{2,1,0:T(8,128)S(1)} %get-tuple-element.34.refs_2_), channel_id=1, source_target_pairs={{0,504},{8,16},{16,8},{24,32},{32,24},{40,48},{48,40},{56,64},{64,... | collective-permute-start | bytes 49160 | tf_op jit(solution)/shard_map/ppermute | solution.py:529
  69.8 6.6 %collective-permute-start.8 = (f32[2,16,128]{2,1,0:T(8,128)S(1)}, f32[2,16,128]{2,1,0:T(8,128)S(1)}, u32[]{:S(2)}, u32[]{:S(2)}) collective-permute-start(f32[2,16,128]{2,1,0:T(8,128)S(1)} %get-tuple-element.34.refs_2_), channel_id=1, source_target_pairs={{0,8},{8,0},{16,24},{24,16},{32,40},{40,32},{48,56},{56,48},{64,72... | collective-permute-start | bytes 49160 | tf_op jit(solution)/shard_map/ppermute | solution.py:530
  76.4 0.0 collective-permute-done.9.refs_4_
  76.4 0.8 collective-permute-done.8.refs_3_
  77.2 1.8 %all-to-all-done.refs_1_ = f32[64,4,128]{2,1,0:T(4,128)S(1)} async-done(((f32[64,4,128]{2,1,0:T(4,128)}), f32[64,4,128]{2,1,0:T(4,128)S(1)}, u32[]{:S(2)}, u32[]{:S(2)}) %all-to-all-start) | async-done | bytes 131104 | tf_op jit(solution)/shard_map/all_to_all | solution.py:573
  79.1 0.6 shard_map.72
  79.7 9.6 %all_to_all.10.strips = f32[8,19,4,128]{3,2,1,0:T(4,128)S(1)} all-to-all(f32[8,19,4,128]{3,2,1,0:T(4,128)S(1)} %get-tuple-element.35), channel_id=1, replica_groups=mesh['gx'=64,'gy'=8] {'gy'}, dimensions={0} | all-to-all | bytes 622592 | tf_op jit(solution)/shard_map/all_to_all | solution.py:579
  89.3 4.6 %shard_map.73 = (f32[3,16,16,128]{3,2,1,0:T(8,128)}, f32[16,16,128]{2,1,0:T(8,128)}) custom-call(s32[2]{0:T(128)S(1)} %pad_add_fusion.place.refs_0_, f32[8,19,4,128]{3,2,1,0:T(4,128)S(1)} %all_to_all.10.strips, f32[6,16,128]{2,1,0:T(8,128)S(1)} %get-tuple-element.36.window, f32[22,24,128]{2,1,0:T(8,128)S(1)} %get-tuple-element.37.finest, ...), custom_call_target="tpu_custom_call" | custom-call | tf_op jit(solution)/shard_map/pallas_call | solution.py:580
Async XLA Ops:
  0.6 20.4 %copy-start.2 = (s32[16,16,128]{2,1,0:T(8,128)S(1)}, s32[16,16,128]{2,1,0:T(8,128)}, u32[]{:S(2)}) copy-start(s32[16,16,128]{2,1,0:T(8,128)} %turbine.3) | copy-start | bytes 393220
  0.6 20.4 %copy-start.1 = (f32[16,16,128]{2,1,0:T(8,128)S(1)}, f32[16,16,128]{2,1,0:T(8,128)}, u32[]{:S(2)}) copy-start(f32[16,16,128]{2,1,0:T(8,128)} %pressure.3) | copy-start | bytes 393220
  0.6 20.4 %copy-start = (f32[3,16,16,128]{3,2,1,0:T(8,128)S(1)}, f32[3,16,16,128]{3,2,1,0:T(8,128)}, u32[]{:S(2)}) copy-start(f32[3,16,16,128]{3,2,1,0:T(8,128)} %velocity.3) | copy-start | bytes 1179652
  3.6 10.8 %collective-permute-start = (f32[41,16,128]{2,1,0:T(8,128)}, f32[41,16,128]{2,1,0:T(8,128)S(1)}, u32[]{:S(2)}, u32[]{:S(2)}) collective-permute-start(f32[41,16,128]{2,1,0:T(8,128)} %get-tuple-element.21), channel_id=1, source_target_pairs={{0,8},{8,0},{16,24},{24,16},{32,40},{40,32},{48,56},{56,48},{64,72... | collective-permute-start | bytes 1007624 | tf_op jit(solution)/shard_map/ppermute | solution.py:530
  12.4 8.7 %collective-permute-start.1 = (f32[41,16,128]{2,1,0:T(8,128)}, f32[41,16,128]{2,1,0:T(8,128)S(1)}, u32[]{:S(2)}, u32[]{:S(2)}) collective-permute-start(f32[41,16,128]{2,1,0:T(8,128)} %get-tuple-element.22), channel_id=1, source_target_pairs={{0,504},{8,16},{16,8},{24,32},{32,24},{40,48},{48,40},{56,64},{64,... | collective-permute-start | bytes 1007624 | tf_op jit(solution)/shard_map/ppermute | solution.py:529
  14.3 6.8 %copy-start.3 = (s32[16,16]{1,0:T(8,128)S(1)}, s32[16,16]{1,0:T(8,128)}, u32[]{:S(2)}) copy-start(s32[16,16]{1,0:T(8,128)} %land.3) | copy-start | bytes 3076
  14.3 6.8 %copy-start.4 = (f32[16]{0:T(128)S(1)}, f32[16]{0:T(128)}, u32[]{:S(2)}) copy-start(f32[16]{0:T(128)} %drag_table.3) | copy-start | bytes 196
  21.9 11.3 %collective-permute-start.2 = (f32[8,40,128]{2,1,0:T(8,128)S(1)}, f32[8,40,128]{2,1,0:T(8,128)S(1)}, u32[]{:S(2)}, u32[]{:S(2)}) collective-permute-start(f32[8,40,128]{2,1,0:T(8,128)S(1)} %get-tuple-element.25), channel_id=1, source_target_pairs={{0,1},{1,0},{2,3},{3,2},{4,5},{5,4},{6,7},{7,6},{8,9},{9,8},{10,11... | collective-permute-start | bytes 491528 | tf_op jit(solution)/shard_map/ppermute | solution.py:530
  23.9 9.3 %collective-permute-start.3 = (f32[8,40,128]{2,1,0:T(8,128)S(1)}, f32[8,40,128]{2,1,0:T(8,128)S(1)}, u32[]{:S(2)}, u32[]{:S(2)}) collective-permute-start(f32[8,40,128]{2,1,0:T(8,128)S(1)} %get-tuple-element.26), channel_id=1, source_target_pairs={{0,7},{1,2},{2,1},{3,4},{4,3},{5,6},{6,5},{7,0},{8,15},{9,10},{10,... | collective-permute-start | bytes 491528 | tf_op jit(solution)/shard_map/ppermute | solution.py:529
  25.8 15.9 %collective-permute-start.6 = (f32[48,4,128]{2,1,0:T(4,128)S(1)}, f32[48,4,128]{2,1,0:T(4,128)S(1)}, u32[]{:S(2)}, u32[]{:S(2)}) collective-permute-start(f32[48,4,128]{2,1,0:T(4,128)S(1)} %get-tuple-element.31), channel_id=1, source_target_pairs={{0,1},{1,0},{2,3},{3,2},{4,5},{5,4},{6,7},{7,6},{8,9},{9,8},{10,11... | collective-permute-start | bytes 294920 | tf_op jit(solution)/shard_map/ppermute | solution.py:530
  29.2 12.6 %collective-permute-start.7 = (f32[48,4,128]{2,1,0:T(4,128)S(1)}, f32[48,4,128]{2,1,0:T(4,128)S(1)}, u32[]{:S(2)}, u32[]{:S(2)}) collective-permute-start(f32[48,4,128]{2,1,0:T(4,128)S(1)} %get-tuple-element.32), channel_id=1, source_target_pairs={{0,7},{1,2},{2,1},{3,4},{4,3},{5,6},{6,5},{7,0},{8,15},{9,10},{10,... | collective-permute-start | bytes 294920 | tf_op jit(solution)/shard_map/ppermute | solution.py:529
  36.4 5.9 %collective-permute-start.4 = (f32[44,4,128]{2,1,0:T(4,128)S(1)}, f32[44,4,128]{2,1,0:T(4,128)S(1)}, u32[]{:S(2)}, u32[]{:S(2)}) collective-permute-start(f32[44,4,128]{2,1,0:T(4,128)S(1)} %get-tuple-element.29), channel_id=1, source_target_pairs={{0,1},{1,0},{2,3},{3,2},{4,5},{5,4},{6,7},{7,6},{8,9},{9,8},{10,11... | collective-permute-start | bytes 270344 | tf_op jit(solution)/shard_map/ppermute | solution.py:530
  38.6 7.4 %collective-permute-start.5 = (f32[44,4,128]{2,1,0:T(4,128)S(1)}, f32[44,4,128]{2,1,0:T(4,128)S(1)}, u32[]{:S(2)}, u32[]{:S(2)}) collective-permute-start(f32[44,4,128]{2,1,0:T(4,128)S(1)} %get-tuple-element.30), channel_id=1, source_target_pairs={{0,7},{1,2},{2,1},{3,4},{4,3},{5,6},{6,5},{7,0},{8,15},{9,10},{10,... | collective-permute-start | bytes 270344 | tf_op jit(solution)/shard_map/ppermute | solution.py:529
  48.7 30.3 %all-to-all-start = ((f32[64,4,128]{2,1,0:T(4,128)}), f32[64,4,128]{2,1,0:T(4,128)S(1)}, u32[]{:S(2)}, u32[]{:S(2)}) async-start(f32[64,4,128]{2,1,0:T(4,128)} %get-tuple-element.33), calls=%async_computation | async-start | bytes 262144 | tf_op jit(solution)/shard_map/all_to_all | solution.py:573
  66.3 10.1 %collective-permute-start.9 = (f32[2,16,128]{2,1,0:T(8,128)S(1)}, f32[2,16,128]{2,1,0:T(8,128)S(1)}, u32[]{:S(2)}, u32[]{:S(2)}) collective-permute-start(f32[2,16,128]{2,1,0:T(8,128)S(1)} %get-tuple-element.34.refs_2_), channel_id=1, source_target_pairs={{0,504},{8,16},{16,8},{24,32},{32,24},{40,48},{48,40},{56,64},{64,... | collective-permute-start | bytes 49160 | tf_op jit(solution)/shard_map/ppermute | solution.py:529
  69.8 7.4 %collective-permute-start.8 = (f32[2,16,128]{2,1,0:T(8,128)S(1)}, f32[2,16,128]{2,1,0:T(8,128)S(1)}, u32[]{:S(2)}, u32[]{:S(2)}) collective-permute-start(f32[2,16,128]{2,1,0:T(8,128)S(1)} %get-tuple-element.34.refs_2_), channel_id=1, source_target_pairs={{0,8},{8,0},{16,24},{24,16},{32,40},{40,32},{48,56},{56,48},{64,72... | collective-permute-start | bytes 49160 | tf_op jit(solution)/shard_map/ppermute | solution.py:530

commit v6 on v5

--- a/solution.py
+++ b/solution.py
@@ -89,11 +89,12 @@
         field[rows, first : first + 4, :] = low[unit : unit + count]
 
 
-def pack_x(drag_table, land, velocity, pressure, turbine, near, far, kinds_ref, cells_ref, drag, sems):
+def pack_x(drag_hbm, land, velocity, pressure, turbine, near, far, drag_table, kinds_ref, cells_ref, drag, sems):
     core = lax.axis_index("gx") % 2
     copies = [
         pltpu.make_async_copy(turbine, cells_ref, sems.at[0]),
         pltpu.make_async_copy(land, kinds_ref, sems.at[1]),
+        pltpu.make_async_copy(drag_hbm, drag_table, sems.at[10]),
     ]
     for side, out in ((0, near), (1, far)):
         high = (core + side) % 2 == 0
@@ -113,6 +114,7 @@
     for copy in copies:
         copy.start()
     copies[1].wait()
+    copies[2].wait()
     columns = ground_columns(kinds_ref[...], drag_table)
     copies[0].wait()
     for i in range(B):
@@ -128,7 +130,7 @@
         near[3 * VH + PH : SIDE] = drag[:PH]
         far[3 * VH + PH : SIDE] = drag[B - PH :]
 
-    for copy in copies[2:]:
+    for copy in copies[3:]:
         copy.wait()
 
 
@@ -534,18 +536,19 @@
     gx = lax.axis_size("gx")
     gy = lax.axis_size("gy")
     place = jnp.stack([lax.axis_index("gx"), lax.axis_index("gy")]).astype(jnp.int32)
+    staged = (surface_drag, land_type, velocity, pressure, turbine_cells)
     near, far = call(
         pack_x,
         [shape(SIDE, B, 128), shape(SIDE, B, 128)],
-        [SMEM] + [HBM] * 4,
+        [HBM] * 5,
         [
+            pltpu.SMEM((16,), F32),
             pltpu.VMEM((B, B), jnp.int32),
             pltpu.VMEM((B, B, 128), jnp.int32),
             (B, B, 128),
-            pltpu.SemaphoreType.DMA((10,)),
+            pltpu.SemaphoreType.DMA((11,)),
         ],
-        60,
-    )(surface_drag, land_type, velocity, pressure, turbine_cells)
+    )(*[pltpu.with_memory_space_constraint(x, pltpu.HBM) for x in staged])
     near, far = exchange(near, far, "gx")
     wide_v, wide_p, wide_d, near, far, near_p, far_p = call(
         widen_x,

time: 94.4 us -> 92.6 us (0.981)
  Pallas kernels: 14.9 us -> 13.3 us
    pallas_call x1, Pallas kernels: 2.91 us -> 1.33 us  [per_device(): call(pack_x, [shape(SIDE, B, 128), shape(SIDE, B, 128)], [HBM] * 5, [pltp...]
where the time goes in v6:
time: 92.6 us; the launch traced here: 92.1 us
  starting transfers between devices  54.9 us (59%)
  Pallas kernels  13.3 us (14%)
  waiting for transfers between devices  13.3 us (14%)
  blocking collectives  9.62 us (10%)
    ppermute x5, starting transfers between devices, exchange(): return (lax.ppermute(near_block, axis, near), far_block)  22.8 us
    all_to_all x1, starting transfers between devices, per_device(): blocks = lax.all_to_all(packed_two, 'gx', 0, 0, tiled=True)  17.5 us
    ppermute x5, starting transfers between devices, exchange(): far_block = lax.ppermute(far_block, axis, far)  14.5 us
    ppermute x5, waiting for transfers between devices, exchange(): far_block = lax.ppermute(far_block, axis, far)  10.1 us
    all_to_all x1, blocking collectives, per_device(): strips = lax.all_to_all(strips, 'gy', 0, 0, tiled=True)  9.62 us
    pallas_call x1, Pallas kernels, per_device(): call(finish, [shape(3, B, B, 128), shape(B, B, 128)], [SMEM] + [VMEM] * 5...  4.57 us
    pallas_call x1, Pallas kernels, per_device(): call(advance, [shape(3, B, B, 128), shape(PX - 2, B, 128), shape(N_S, 4,...  3.19 us
    pallas_call x1, Pallas kernels, per_device(): call(presmooth, [shape(22, 24, 128), shape(20, 24, 128), shape(2, B, 128)...  2.77 us
  transfers between devices with their start and end apart: 11, of which 5 were waited for; matrix products, arithmetic and copies ran while one was open for 0% of the time, Pallas kernels for 3%

profile of v6, /device:TPU:1, one launch (start us, length us, event | category | flops | bytes accessed | tf_op | source)
XLA Modules:
  0.0 92.1 jit_solution(2725749418678837648)
XLA Ops:
  0.6 0.0 copy-start.2
  0.6 0.0 copy-start.1
  0.6 0.0 copy-start
  0.7 1.3 %shard_map.68 = (f32[41,16,128]{2,1,0:T(8,128)S(1)}, f32[41,16,128]{2,1,0:T(8,128)S(1)}) custom-call(f32[16]{0:T(128)} %drag_table.1, s32[16,16]{1,0:T(8,128)} %land.3, f32[3,16,16,128]{3,2,1,0:T(8,128)} %velocity.3, f32[16,16,128]{2,1,0:T(8,128)} %pressure.3, s32[16,16,128]{2,1,0:T(8,128)} %turbine.3), custom_call_target="tpu_custom_call" | custom-call | tf_op jit(solution)/shard_map/pallas_call | solution.py:540
  2.0 8.8 %collective-permute-start = (f32[41,16,128]{2,1,0:T(8,128)S(1)}, f32[41,16,128]{2,1,0:T(8,128)S(1)}, u32[]{:S(2)}, u32[]{:S(2)}) collective-permute-start(f32[41,16,128]{2,1,0:T(8,128)S(1)} %get-tuple-element.21), channel_id=1, source_target_pairs={{0,8},{8,0},{16,24},{24,16},{32,40},{40,32},{48,56},{56,48},{64,72... | collective-permute-start | bytes 1007624 | tf_op jit(solution)/shard_map/ppermute | solution.py:532
  10.8 1.9 %collective-permute-start.1 = (f32[41,16,128]{2,1,0:T(8,128)S(1)}, f32[41,16,128]{2,1,0:T(8,128)S(1)}, u32[]{:S(2)}, u32[]{:S(2)}) collective-permute-start(f32[41,16,128]{2,1,0:T(8,128)S(1)} %get-tuple-element.22), channel_id=1, source_target_pairs={{0,504},{8,16},{16,8},{24,32},{32,24},{40,48},{48,40},{56,64},{64,... | collective-permute-start | bytes 1007624 | tf_op jit(solution)/shard_map/ppermute | solution.py:531
  12.7 0.0 copy-start.3
  12.7 0.0 copy-start.4
  12.7 0.1 pad_add_fusion.place.refs_0_
  12.8 0.0 collective-permute-done.near
  12.8 6.4 %collective-permute-done.1.far = f32[41,16,128]{2,1,0:T(8,128)S(1)} collective-permute-done((f32[41,16,128]{2,1,0:T(8,128)S(1)}, f32[41,16,128]{2,1,0:T(8,128)S(1)}, u32[]{:S(2)}, u32[]{:S(2)}) %collective-permute-start.1) | collective-permute-done | bytes 335904 | tf_op jit(solution)/shard_map/ppermute | solution.py:531
  19.3 0.0 copy-done.2
  19.3 0.0 copy-done.1
  19.3 0.0 copy-done
  19.3 0.0 copy-done.3
  19.3 0.0 copy-done.4
  19.3 0.8 shard_map.69
  20.2 1.9 %collective-permute-start.2 = (f32[8,40,128]{2,1,0:T(8,128)S(1)}, f32[8,40,128]{2,1,0:T(8,128)S(1)}, u32[]{:S(2)}, u32[]{:S(2)}) collective-permute-start(f32[8,40,128]{2,1,0:T(8,128)S(1)} %get-tuple-element.25), channel_id=1, source_target_pairs={{0,1},{1,0},{2,3},{3,2},{4,5},{5,4},{6,7},{7,6},{8,9},{9,8},{10,11... | collective-permute-start | bytes 491528 | tf_op jit(solution)/shard_map/ppermute | solution.py:532
  22.1 1.9 %collective-permute-start.3 = (f32[8,40,128]{2,1,0:T(8,128)S(1)}, f32[8,40,128]{2,1,0:T(8,128)S(1)}, u32[]{:S(2)}, u32[]{:S(2)}) collective-permute-start(f32[8,40,128]{2,1,0:T(8,128)S(1)} %get-tuple-element.26), channel_id=1, source_target_pairs={{0,7},{1,2},{2,1},{3,4},{4,3},{5,6},{6,5},{7,0},{8,15},{9,10},{10,... | collective-permute-start | bytes 491528 | tf_op jit(solution)/shard_map/ppermute | solution.py:531
  24.0 3.4 %collective-permute-start.6 = (f32[48,4,128]{2,1,0:T(4,128)S(1)}, f32[48,4,128]{2,1,0:T(4,128)S(1)}, u32[]{:S(2)}, u32[]{:S(2)}) collective-permute-start(f32[48,4,128]{2,1,0:T(4,128)S(1)} %get-tuple-element.31), channel_id=1, source_target_pairs={{0,1},{1,0},{2,3},{3,2},{4,5},{5,4},{6,7},{7,6},{8,9},{9,8},{10,11... | collective-permute-start | bytes 294920 | tf_op jit(solution)/shard_map/ppermute | solution.py:532
  27.4 4.0 %collective-permute-start.7 = (f32[48,4,128]{2,1,0:T(4,128)S(1)}, f32[48,4,128]{2,1,0:T(4,128)S(1)}, u32[]{:S(2)}, u32[]{:S(2)}) collective-permute-start(f32[48,4,128]{2,1,0:T(4,128)S(1)} %get-tuple-element.32), channel_id=1, source_target_pairs={{0,7},{1,2},{2,1},{3,4},{4,3},{5,6},{6,5},{7,0},{8,15},{9,10},{10,... | collective-permute-start | bytes 294920 | tf_op jit(solution)/shard_map/ppermute | solution.py:531
  31.4 0.0 collective-permute-done.2.near
  31.4 0.0 collective-permute-done.3.far
  31.4 3.2 %shard_map.70 = (f32[3,16,16,128]{3,2,1,0:T(8,128)S(1)}, f32[28,16,128]{2,1,0:T(8,128)S(1)}, f32[44,4,128]{2,1,0:T(4,128)S(1)}, f32[44,4,128]{2,1,0:T(4,128)S(1)}) custom-call(s32[2]{0:T(128)S(1)} %pad_add_fusion.place.refs_0_, f32[3,34,16,128]{3,2,1,0:T(8,128)S(1)} %get-tuple-element.23.wide_v, f32[30,16,128]{2,1,0:T(8,128)S(1)} %get-tuple-element.24.wide_d, ...), custom_call_target="tpu_custom_call" | custom-call | tf_op jit(solution)/shard_map/pallas_call | solution.py:562
  34.6 2.2 %collective-permute-start.4 = (f32[44,4,128]{2,1,0:T(4,128)S(1)}, f32[44,4,128]{2,1,0:T(4,128)S(1)}, u32[]{:S(2)}, u32[]{:S(2)}) collective-permute-start(f32[44,4,128]{2,1,0:T(4,128)S(1)} %get-tuple-element.29), channel_id=1, source_target_pairs={{0,1},{1,0},{2,3},{3,2},{4,5},{5,4},{6,7},{7,6},{8,9},{9,8},{10,11... | collective-permute-start | bytes 270344 | tf_op jit(solution)/shard_map/ppermute | solution.py:532
  36.8 3.1 %collective-permute-start.5 = (f32[44,4,128]{2,1,0:T(4,128)S(1)}, f32[44,4,128]{2,1,0:T(4,128)S(1)}, u32[]{:S(2)}, u32[]{:S(2)}) collective-permute-start(f32[44,4,128]{2,1,0:T(4,128)S(1)} %get-tuple-element.30), channel_id=1, source_target_pairs={{0,7},{1,2},{2,1},{3,4},{4,3},{5,6},{6,5},{7,0},{8,15},{9,10},{10,... | collective-permute-start | bytes 270344 | tf_op jit(solution)/shard_map/ppermute | solution.py:531
  39.9 0.0 collective-permute-done.6.near_p
  40.0 0.0 collective-permute-done.7.far_p
  40.0 0.6 collective-permute-done.4.near
  40.6 3.6 %collective-permute-done.5.far = f32[44,4,128]{2,1,0:T(4,128)S(1)} collective-permute-done((f32[44,4,128]{2,1,0:T(4,128)S(1)}, f32[44,4,128]{2,1,0:T(4,128)S(1)}, u32[]{:S(2)}, u32[]{:S(2)}) %collective-permute-start.5) | collective-permute-done | bytes 90144 | tf_op jit(solution)/shard_map/ppermute | solution.py:531
  44.2 2.8 %shard_map.71 = (f32[22,24,128]{2,1,0:T(8,128)S(1)}, f32[20,24,128]{2,1,0:T(8,128)S(1)}, f32[2,16,128]{2,1,0:T(8,128)S(1)}, f32[64,4,128]{2,1,0:T(4,128)}) custom-call(s32[2]{0:T(128)S(1)} %pad_add_fusion.place.refs_0_, f32[28,16,128]{2,1,0:T(8,128)S(1)} %get-tuple-element.27.source, f32[30,16,128]{2,1,0:T(8,128)S(1)} %get-tuple-element.28.wide_p, ...), custom_call_target="tpu_custom_call" | custom-call | tf_op jit(solution)/shard_map/pallas_call | solution.py:569
  47.0 17.5 %all-to-all-start = ((f32[64,4,128]{2,1,0:T(4,128)}), f32[64,4,128]{2,1,0:T(4,128)S(1)}, u32[]{:S(2)}, u32[]{:S(2)}) async-start(f32[64,4,128]{2,1,0:T(4,128)} %get-tuple-element.33), calls=%async_computation | async-start | bytes 262144 | tf_op jit(solution)/shard_map/all_to_all | solution.py:576
  64.5 3.5 %collective-permute-start.9 = (f32[2,16,128]{2,1,0:T(8,128)S(1)}, f32[2,16,128]{2,1,0:T(8,128)S(1)}, u32[]{:S(2)}, u32[]{:S(2)}) collective-permute-start(f32[2,16,128]{2,1,0:T(8,128)S(1)} %get-tuple-element.34.refs_2_), channel_id=1, source_target_pairs={{0,504},{8,16},{16,8},{24,32},{32,24},{40,48},{48,40},{56,64},{64,... | collective-permute-start | bytes 49160 | tf_op jit(solution)/shard_map/ppermute | solution.py:531
  68.1 6.6 %collective-permute-start.8 = (f32[2,16,128]{2,1,0:T(8,128)S(1)}, f32[2,16,128]{2,1,0:T(8,128)S(1)}, u32[]{:S(2)}, u32[]{:S(2)}) collective-permute-start(f32[2,16,128]{2,1,0:T(8,128)S(1)} %get-tuple-element.34.refs_2_), channel_id=1, source_target_pairs={{0,8},{8,0},{16,24},{24,16},{32,40},{40,32},{48,56},{56,48},{64,72... | collective-permute-start | bytes 49160 | tf_op jit(solution)/shard_map/ppermute | solution.py:532
  74.6 0.0 collective-permute-done.9.refs_4_
  74.7 0.8 collective-permute-done.8.refs_3_
  75.5 1.8 %all-to-all-done.refs_1_ = f32[64,4,128]{2,1,0:T(4,128)S(1)} async-done(((f32[64,4,128]{2,1,0:T(4,128)}), f32[64,4,128]{2,1,0:T(4,128)S(1)}, u32[]{:S(2)}, u32[]{:S(2)}) %all-to-all-start) | async-done | bytes 131104 | tf_op jit(solution)/shard_map/all_to_all | solution.py:576
  77.3 0.6 shard_map.72
  77.9 9.6 %all_to_all.10.strips = f32[8,19,4,128]{3,2,1,0:T(4,128)S(1)} all-to-all(f32[8,19,4,128]{3,2,1,0:T(4,128)S(1)} %get-tuple-element.35), channel_id=1, replica_groups=mesh['gx'=64,'gy'=8] {'gy'}, dimensions={0} | all-to-all | bytes 622592 | tf_op jit(solution)/shard_map/all_to_all | solution.py:582
  87.5 4.6 %shard_map.73 = (f32[3,16,16,128]{3,2,1,0:T(8,128)}, f32[16,16,128]{2,1,0:T(8,128)}) custom-call(s32[2]{0:T(128)S(1)} %pad_add_fusion.place.refs_0_, f32[8,19,4,128]{3,2,1,0:T(4,128)S(1)} %all_to_all.10.strips, f32[6,16,128]{2,1,0:T(8,128)S(1)} %get-tuple-element.36.window, f32[22,24,128]{2,1,0:T(8,128)S(1)} %get-tuple-element.37.finest, ...), custom_call_target="tpu_custom_call" | custom-call | tf_op jit(solution)/shard_map/pallas_call | solution.py:583
Async XLA Ops:
  0.6 18.6 %copy-start.2 = (s32[16,16,128]{2,1,0:T(8,128)S(1)}, s32[16,16,128]{2,1,0:T(8,128)}, u32[]{:S(2)}) copy-start(s32[16,16,128]{2,1,0:T(8,128)} %turbine.3) | copy-start | bytes 393220
  0.6 18.6 %copy-start.1 = (f32[16,16,128]{2,1,0:T(8,128)S(1)}, f32[16,16,128]{2,1,0:T(8,128)}, u32[]{:S(2)}) copy-start(f32[16,16,128]{2,1,0:T(8,128)} %pressure.3) | copy-start | bytes 393220
  0.6 18.6 %copy-start = (f32[3,16,16,128]{3,2,1,0:T(8,128)S(1)}, f32[3,16,16,128]{3,2,1,0:T(8,128)}, u32[]{:S(2)}) copy-start(f32[3,16,16,128]{3,2,1,0:T(8,128)} %velocity.3) | copy-start | bytes 1179652
  2.0 10.8 %collective-permute-start = (f32[41,16,128]{2,1,0:T(8,128)S(1)}, f32[41,16,128]{2,1,0:T(8,128)S(1)}, u32[]{:S(2)}, u32[]{:S(2)}) collective-permute-start(f32[41,16,128]{2,1,0:T(8,128)S(1)} %get-tuple-element.21), channel_id=1, source_target_pairs={{0,8},{8,0},{16,24},{24,16},{32,40},{40,32},{48,56},{56,48},{64,72... | collective-permute-start | bytes 1007624 | tf_op jit(solution)/shard_map/ppermute | solution.py:532
  10.8 8.5 %collective-permute-start.1 = (f32[41,16,128]{2,1,0:T(8,128)S(1)}, f32[41,16,128]{2,1,0:T(8,128)S(1)}, u32[]{:S(2)}, u32[]{:S(2)}) collective-permute-start(f32[41,16,128]{2,1,0:T(8,128)S(1)} %get-tuple-element.22), channel_id=1, source_target_pairs={{0,504},{8,16},{16,8},{24,32},{32,24},{40,48},{48,40},{56,64},{64,... | collective-permute-start | bytes 1007624 | tf_op jit(solution)/shard_map/ppermute | solution.py:531
  12.7 6.6 %copy-start.3 = (s32[16,16]{1,0:T(8,128)S(1)}, s32[16,16]{1,0:T(8,128)}, u32[]{:S(2)}) copy-start(s32[16,16]{1,0:T(8,128)} %land.3) | copy-start | bytes 3076
  12.7 6.6 %copy-start.4 = (f32[16]{0:T(128)S(1)}, f32[16]{0:T(128)}, u32[]{:S(2)}) copy-start(f32[16]{0:T(128)} %drag_table.1) | copy-start | bytes 196
  20.2 11.3 %collective-permute-start.2 = (f32[8,40,128]{2,1,0:T(8,128)S(1)}, f32[8,40,128]{2,1,0:T(8,128)S(1)}, u32[]{:S(2)}, u32[]{:S(2)}) collective-permute-start(f32[8,40,128]{2,1,0:T(8,128)S(1)} %get-tuple-element.25), channel_id=1, source_target_pairs={{0,1},{1,0},{2,3},{3,2},{4,5},{5,4},{6,7},{7,6},{8,9},{9,8},{10,11... | collective-permute-start | bytes 491528 | tf_op jit(solution)/shard_map/ppermute | solution.py:532
  22.1 9.3 %collective-permute-start.3 = (f32[8,40,128]{2,1,0:T(8,128)S(1)}, f32[8,40,128]{2,1,0:T(8,128)S(1)}, u32[]{:S(2)}, u32[]{:S(2)}) collective-permute-start(f32[8,40,128]{2,1,0:T(8,128)S(1)} %get-tuple-element.26), channel_id=1, source_target_pairs={{0,7},{1,2},{2,1},{3,4},{4,3},{5,6},{6,5},{7,0},{8,15},{9,10},{10,... | collective-permute-start | bytes 491528 | tf_op jit(solution)/shard_map/ppermute | solution.py:531
  24.0 15.9 %collective-permute-start.6 = (f32[48,4,128]{2,1,0:T(4,128)S(1)}, f32[48,4,128]{2,1,0:T(4,128)S(1)}, u32[]{:S(2)}, u32[]{:S(2)}) collective-permute-start(f32[48,4,128]{2,1,0:T(4,128)S(1)} %get-tuple-element.31), channel_id=1, source_target_pairs={{0,1},{1,0},{2,3},{3,2},{4,5},{5,4},{6,7},{7,6},{8,9},{9,8},{10,11... | collective-permute-start | bytes 294920 | tf_op jit(solution)/shard_map/ppermute | solution.py:532
  27.4 12.6 %collective-permute-start.7 = (f32[48,4,128]{2,1,0:T(4,128)S(1)}, f32[48,4,128]{2,1,0:T(4,128)S(1)}, u32[]{:S(2)}, u32[]{:S(2)}) collective-permute-start(f32[48,4,128]{2,1,0:T(4,128)S(1)} %get-tuple-element.32), channel_id=1, source_target_pairs={{0,7},{1,2},{2,1},{3,4},{4,3},{5,6},{6,5},{7,0},{8,15},{9,10},{10,... | collective-permute-start | bytes 294920 | tf_op jit(solution)/shard_map/ppermute | solution.py:531
  34.6 5.9 %collective-permute-start.4 = (f32[44,4,128]{2,1,0:T(4,128)S(1)}, f32[44,4,128]{2,1,0:T(4,128)S(1)}, u32[]{:S(2)}, u32[]{:S(2)}) collective-permute-start(f32[44,4,128]{2,1,0:T(4,128)S(1)} %get-tuple-element.29), channel_id=1, source_target_pairs={{0,1},{1,0},{2,3},{3,2},{4,5},{5,4},{6,7},{7,6},{8,9},{9,8},{10,11... | collective-permute-start | bytes 270344 | tf_op jit(solution)/shard_map/ppermute | solution.py:532
  36.8 7.4 %collective-permute-start.5 = (f32[44,4,128]{2,1,0:T(4,128)S(1)}, f32[44,4,128]{2,1,0:T(4,128)S(1)}, u32[]{:S(2)}, u32[]{:S(2)}) collective-permute-start(f32[44,4,128]{2,1,0:T(4,128)S(1)} %get-tuple-element.30), channel_id=1, source_target_pairs={{0,7},{1,2},{2,1},{3,4},{4,3},{5,6},{6,5},{7,0},{8,15},{9,10},{10,... | collective-permute-start | bytes 270344 | tf_op jit(solution)/shard_map/ppermute | solution.py:531
  47.0 30.3 %all-to-all-start = ((f32[64,4,128]{2,1,0:T(4,128)}), f32[64,4,128]{2,1,0:T(4,128)S(1)}, u32[]{:S(2)}, u32[]{:S(2)}) async-start(f32[64,4,128]{2,1,0:T(4,128)} %get-tuple-element.33), calls=%async_computation | async-start | bytes 262144 | tf_op jit(solution)/shard_map/all_to_all | solution.py:576
  64.5 10.1 %collective-permute-start.9 = (f32[2,16,128]{2,1,0:T(8,128)S(1)}, f32[2,16,128]{2,1,0:T(8,128)S(1)}, u32[]{:S(2)}, u32[]{:S(2)}) collective-permute-start(f32[2,16,128]{2,1,0:T(8,128)S(1)} %get-tuple-element.34.refs_2_), channel_id=1, source_target_pairs={{0,504},{8,16},{16,8},{24,32},{32,24},{40,48},{48,40},{56,64},{64,... | collective-permute-start | bytes 49160 | tf_op jit(solution)/shard_map/ppermute | solution.py:531
  68.1 7.4 %collective-permute-start.8 = (f32[2,16,128]{2,1,0:T(8,128)S(1)}, f32[2,16,128]{2,1,0:T(8,128)S(1)}, u32[]{:S(2)}, u32[]{:S(2)}) collective-permute-start(f32[2,16,128]{2,1,0:T(8,128)S(1)} %get-tuple-element.34.refs_2_), channel_id=1, source_target_pairs={{0,8},{8,0},{16,24},{24,16},{32,40},{40,32},{48,56},{56,48},{64,72... | collective-permute-start | bytes 49160 | tf_op jit(solution)/shard_map/ppermute | solution.py:532

commit v7 on v6

--- a/solution.py
+++ b/solution.py
@@ -1,4 +1,5 @@
 import jax
+import numpy as np
 import jax.numpy as jnp
 from jax import lax
 from jax.experimental import pallas as pl
@@ -19,9 +20,9 @@
 VMEM = pl.BlockSpec(memory_space=pltpu.VMEM)
 SMEM = pl.BlockSpec(memory_space=pltpu.SMEM)
 HBM = pl.BlockSpec(memory_space=pltpu.HBM)
-S_UNITS = ((0, 5, 18, True), (18, 5, 18, False), (36, 1, 4, False), (40, 23, 4, False))
+S_ROWS = [(6 * i, 6, 5 + i) for i in range(18)] + [(108 + 4 * i, 4, x) for i, x in enumerate((1, 2, 3, 4, 23, 24, 25, 26))]
 P_UNITS = ((0, 5, 20, True), (20, 5, 20, False), (40, 1, 4, False), (44, 25, 4, False))
-N_S = 44
+N_S = 144
 N_P = 48
 F32 = jnp.float32
 
@@ -185,13 +186,16 @@
         edge_units(P_UNITS, wide_p, far_p, near_p)
 
 
-def exact_product(values, matrix):
-    flat = values.reshape(-1, 128)
+def three_parts(flat):
     high = flat.astype(jnp.bfloat16)
     rest = flat - high.astype(F32)
     middle = rest.astype(jnp.bfloat16)
     low = (rest - middle.astype(F32)).astype(jnp.bfloat16)
-    parts = jnp.concatenate([high, middle, low], axis=1)
+    return jnp.concatenate([high, middle, low], axis=1)
+
+
+def exact_product(values, matrix):
+    parts = three_parts(values.reshape(-1, 128))
     return jnp.dot(parts, matrix, preferred_element_type=F32).reshape(values.shape)
 
 
@@ -282,13 +286,18 @@
         (along_z,) = along_column([part[2, i : i + 4, 0:B, :]])
         source[i - 3 : i + 1] = ((along_x + along_y)[:, 0:B] + along_z) / STEP
 
+    def send(up, down):
+        for row, count, x in S_ROWS:
+            up[row : row + count, :] = source[x, B - count :, :]
+            down[row : row + count, :] = source[x, :count, :]
+
     @pl.when(odd == 0)
     def _():
-        edge_units(S_UNITS, source, near_y, far_y)
+        send(near_y, far_y)
 
     @pl.when(odd == 1)
     def _():
-        edge_units(S_UNITS, source, far_y, near_y)
+        send(far_y, near_y)
 
 
 def column_sum(dz, halves):
@@ -339,14 +348,19 @@
     p[:, 0:B, :] = wide_p[...]
     s[1 : PX - 1, 0:B, :] = source[...]
 
+    def place_source(low, high):
+        for row, count, x in S_ROWS:
+            s[x + 1, B : B + count, :] = high[row : row + count, :]
+            s[x + 1, B + 16 - count : B + 16, :] = low[row : row + count, :]
+
     @pl.when(odd == 0)
     def _():
-        place_units(S_UNITS, s, 1, far, near)
+        place_source(far, near)
         place_units(P_UNITS, p, 0, far_p, near_p)
 
     @pl.when(odd == 1)
     def _():
-        place_units(S_UNITS, s, 1, near, far)
+        place_source(near, far)
         place_units(P_UNITS, p, 0, near_p, far_p)
 
     fine = column_sum(1, 3)
@@ -413,35 +427,51 @@
         strips[gy, k] = jnp.zeros((4, 128), F32)
 
 
-def packed_neighbours(ref, b, dx, dy, dz):
-    p = ref[b]
-    before = ref[max(b - 1, 0)]
-    after = ref[min(b + 1, 2 * WINDOW)]
-    lane = lane_of(p)
-    slot = lane & 3
-    left = jnp.where(slot < dx, turn(before, dx - 4, 1), turn(p, dx, 1))
-    right = jnp.where(slot >= 4 - dx, turn(after, 4 - dx, 1), turn(p, -dx, 1))
-    below = jnp.where(lane < dz, p, turn(p, dz, 1))
-    above = jnp.where(lane >= 128 - dz, p, turn(p, -dz, 1))
-    return p, (left + right) + (turn(p, dy, 0) + turn(p, -dy, 0)) + 4.0 * (below + above)
-
-
-def packed_sweep(dst, src, right, blocks, dx, dy, dz):
-    for b in blocks:
-        p, around = packed_neighbours(src, b, dx, dy, dz)
+def packed_matrix(dx, dz):
+    k = np.arange(128)[:, None]
+    j = np.arange(128)[None, :]
+    slot = j % 4
+    own = (k == j - dx) & (slot >= dx)
+    own = own.astype(np.float32) + ((k == j + dx) & (slot < 4 - dx))
+    edge = (k == j) & ((j < dz) | (j >= 128 - dz))
+    own = own + 4.0 * ((k == j - dz) | (k == j + dz)) + 4.0 * edge
+    after = (k == j + 4 - dx) & (slot < dx)
+    before = (k == j - 4 + dx) & (slot >= 4 - dx)
+    whole = np.concatenate([own, after.astype(np.float32), before.astype(np.float32)], axis=1)
+    return jnp.asarray(np.concatenate([whole] * 3, axis=0), jnp.bfloat16)
+
+
+def packed_around(ref, first, last, dy, matrix):
+    low, high = max(first - 1, 0), min(last + 1, 2 * WINDOW + 1)
+    p = ref[low:high]
+    flat = p.reshape(-1, 128)
+    parts = three_parts(flat)
+    out = jnp.dot(parts, matrix, preferred_element_type=F32)
+    result = []
+    for b in range(first, last):
+        rows = lambda c: slice(32 * (c - low), 32 * (c - low) + 32)
+        before, after = max(b - 1, low), min(b + 1, high - 1)
+        sides = out[rows(b), 0:128] + (out[rows(before), 128:256] + out[rows(after), 256:384])
+        own = p[b - low]
+        result.append((own, sides + (turn(own, dy, 0) + turn(own, -dy, 0))))
+    return result
+
+
+def packed_sweep(dst, src, right, blocks, dy, matrix):
+    for b, (p, around) in zip(blocks, packed_around(src, blocks[0], blocks[-1] + 1, dy, matrix)):
         dst[b] = 0.2 * p + COEFF * (around - right[b])
 
 
-def packed_residual(src, right, b, dx, dy, dz):
-    p, around = packed_neighbours(src, b, dx, dy, dz)
-    return right[b] - around + 12.0 * p
+def packed_residual(src, right, blocks, dy, matrix):
+    rows = packed_around(src, blocks[0], blocks[-1] + 1, dy, matrix)
+    return [right[b] - around + 12.0 * p for b, (p, around) in zip(blocks, rows)]
 
 
 def without_middle(values):
     return jnp.concatenate([values[..., 0:24, :], values[..., 32:40, :]], axis=-2)
 
 
-def finish(place, strips, window, finest, right, star, velocity_new, pressure_new, f2, a2, b2, f3, a3, b3, g1, f1, a1, b1, c1, d1, e1, p0, q0):
+def finish(place, strips, window, finest, right, star, second, third, velocity_new, pressure_new, f2, a2, b2, f3, a3, b3, g1, f1, a1, b1, c1, d1, e1, p0, q0):
     gy = place[1]
     for j in range(8):
         peer = (gy + j) % 8
@@ -449,9 +479,8 @@
             f2[b, 4 * j : 4 * j + 4, :] = strips[peer, b]
     for b in range(9):
         a2[b] = -COEFF * f2[b]
-    packed_sweep(b2, a2, f2, range(9), 1, 1, 4)
-    for b in range(1, 8):
-        total = packed_residual(b2, f2, b, 1, 1, 4)
+    packed_sweep(b2, a2, f2, range(9), 1, second[...])
+    for b, total in zip(range(1, 8), packed_residual(b2, f2, range(1, 8), 1, second[...])):
         lane = lane_of(total)
         total = total + jnp.where((lane & 1) == 0, turn(total, -1, 1), turn(total, 1, 1))
         total = total + jnp.where((lane & 4) == 0, turn(total, -4, 1), turn(total, 4, 1))
@@ -459,14 +488,17 @@
         total = total + jnp.where((row & 1) == 0, turn(total, -1, 0), turn(total, 1, 0))
         f3[b] = 0.5 * total
         a3[b] = (-0.5 * COEFF) * total
-    packed_sweep(b3, a3, f3, range(1, 8), 2, 2, 8)
-    packed_sweep(a3, b3, f3, range(2, 7), 2, 2, 8)
-    packed_sweep(b3, a3, f3, range(2, 7), 2, 2, 8)
-    for b in range(3, 6):
-        line = jnp.sum(packed_residual(b3, f3, b, 2, 2, 8), axis=0, keepdims=True) * (COEFF / 32.0)
+    for b in (0, 8):
+        a3[b] = jnp.zeros((32, 128), F32)
+        b3[b] = jnp.zeros((32, 128), F32)
+    packed_sweep(b3, a3, f3, range(1, 8), 2, third[...])
+    packed_sweep(a3, b3, f3, range(2, 7), 2, third[...])
+    packed_sweep(b3, a3, f3, range(2, 7), 2, third[...])
+    for b, total in zip(range(3, 6), packed_residual(b3, f3, range(3, 6), 2, third[...])):
+        line = jnp.sum(total, axis=0, keepdims=True) * (COEFF / 32.0)
         a2[b] = b2[b] + (b3[b] - line)
-    packed_sweep(b2, a2, f2, range(3, 6), 1, 1, 4)
-    packed_sweep(a2, b2, f2, range(3, 6), 1, 1, 4)
+    packed_sweep(b2, a2, f2, range(3, 6), 1, second[...])
+    packed_sweep(a2, b2, f2, range(3, 6), 1, second[...])
     g1[:, 0:B, :] = window[...]
     for unit, group, count in GROUPS:
         for k in range(count):
@@ -561,7 +593,7 @@
     near_p, far_p = exchange(near_p, far_p, "gy")
     star, source, near, far = call(
         advance,
-        [shape(3, B, B, 128), shape(PX - 2, B, 128), shape(N_S, 4, 128), shape(N_S, 4, 128)],
+        [shape(3, B, B, 128), shape(PX - 2, B, 128), shape(N_S, 128), shape(N_S, 128)],
         [SMEM] + [VMEM] * 4,
         [(3, VX, 24, 128), (VX, 24, 128), (3, VX, 24, 128), (3, VX, 24, 128)],
     )(place, wide_v, wide_d, near, far)
@@ -583,14 +615,14 @@
     velocity_new, pressure_new = call(
         finish,
         [shape(3, B, B, 128), shape(B, B, 128)],
-        [SMEM] + [VMEM] * 5,
+        [SMEM] + [VMEM] * 7,
         [(9, 32, 128)] * 6
         + [(6, 40, 128)]
         + [(24, 40, 128)] * 3
         + [(24, 32, 128)] * 2
         + [(8, 32, 128)]
         + [(22, 24, 128)] * 2,
-    )(place, strips, window, finest, right, star)
+    )(place, strips, window, finest, right, star, packed_matrix(1, 4), packed_matrix(2, 8))
     return velocity_new, pressure_new
 
 

time: 92.6 us -> 92.1 us (level)
  no operation moved by 1% of the time
where the time goes in v7:
time: 92.1 us; the launch traced here: 91.6 us
  starting transfers between devices  54.9 us (60%)
  waiting for transfers between devices  13.1 us (14%)
  Pallas kernels  12.8 us (14%)
  blocking collectives  9.77 us (11%)
    ppermute x5, starting transfers between devices, exchange(): return (lax.ppermute(near_block, axis, near), far_block)  22.8 us
    all_to_all x1, starting transfers between devices, per_device(): blocks = lax.all_to_all(packed_two, 'gx', 0, 0, tiled=True)  17.5 us
    ppermute x5, starting transfers between devices, exchange(): far_block = lax.ppermute(far_block, axis, far)  14.5 us
    ppermute x5, waiting for transfers between devices, exchange(): far_block = lax.ppermute(far_block, axis, far)  10 us
    all_to_all x1, blocking collectives, per_device(): strips = lax.all_to_all(strips, 'gy', 0, 0, tiled=True)  9.77 us
    pallas_call x1, Pallas kernels, per_device(): call(finish, [shape(3, B, B, 128), shape(B, B, 128)], [SMEM] + [VMEM] * 7...  4.08 us
    pallas_call x1, Pallas kernels, per_device(): call(advance, [shape(3, B, B, 128), shape(PX - 2, B, 128), shape(N_S, 128...  3.18 us
    pallas_call x1, Pallas kernels, per_device(): call(presmooth, [shape(22, 24, 128), shape(20, 24, 128), shape(2, B, 128)...  2.74 us
  transfers between devices with their start and end apart: 11, of which 5 were waited for; matrix products, arithmetic and copies ran while one was open for 0% of the time, Pallas kernels for 3%

profile of v7, /device:TPU:1, one launch (start us, length us, event | category | flops | bytes accessed | tf_op | source)
XLA Modules:
  0.0 91.6 jit_solution(8364087844454103633)
XLA Ops:
  0.6 0.0 copy-start.2
  0.6 0.0 copy-start.1
  0.6 0.0 copy-start
  0.7 1.3 %shard_map.86 = (f32[41,16,128]{2,1,0:T(8,128)S(1)}, f32[41,16,128]{2,1,0:T(8,128)S(1)}) custom-call(f32[16]{0:T(128)} %drag_table.1, s32[16,16]{1,0:T(8,128)} %land.3, f32[3,16,16,128]{3,2,1,0:T(8,128)} %velocity.3, f32[16,16,128]{2,1,0:T(8,128)} %pressure.3, s32[16,16,128]{2,1,0:T(8,128)} %turbine.3), custom_call_target="tpu_custom_call" | custom-call | tf_op jit(solution)/shard_map/pallas_call | solution.py:572
  2.0 8.8 %collective-permute-start = (f32[41,16,128]{2,1,0:T(8,128)S(1)}, f32[41,16,128]{2,1,0:T(8,128)S(1)}, u32[]{:S(2)}, u32[]{:S(2)}) collective-permute-start(f32[41,16,128]{2,1,0:T(8,128)S(1)} %get-tuple-element.21), channel_id=1, source_target_pairs={{0,8},{8,0},{16,24},{24,16},{32,40},{40,32},{48,56},{56,48},{64,72... | collective-permute-start | bytes 1007624 | tf_op jit(solution)/shard_map/ppermute | solution.py:564
  10.8 1.9 %collective-permute-start.1 = (f32[41,16,128]{2,1,0:T(8,128)S(1)}, f32[41,16,128]{2,1,0:T(8,128)S(1)}, u32[]{:S(2)}, u32[]{:S(2)}) collective-permute-start(f32[41,16,128]{2,1,0:T(8,128)S(1)} %get-tuple-element.22), channel_id=1, source_target_pairs={{0,504},{8,16},{16,8},{24,32},{32,24},{40,48},{48,40},{56,64},{64,... | collective-permute-start | bytes 1007624 | tf_op jit(solution)/shard_map/ppermute | solution.py:563
  12.7 0.0 copy-start.5
  12.7 0.0 copy-start.6
  12.7 0.1 pad_add_fusion.place.refs_0_
  12.8 0.0 collective-permute-done.near
  12.8 6.4 %collective-permute-done.1.far = f32[41,16,128]{2,1,0:T(8,128)S(1)} collective-permute-done((f32[41,16,128]{2,1,0:T(8,128)S(1)}, f32[41,16,128]{2,1,0:T(8,128)S(1)}, u32[]{:S(2)}, u32[]{:S(2)}) %collective-permute-start.1) | collective-permute-done | bytes 335904 | tf_op jit(solution)/shard_map/ppermute | solution.py:563
  19.3 0.0 copy-done.2
  19.3 0.0 copy-done.1
  19.3 0.0 copy-done
  19.3 0.0 copy-done.5
  19.3 0.0 copy-done.6
  19.3 0.8 shard_map.87
  20.2 1.9 %collective-permute-start.2 = (f32[8,40,128]{2,1,0:T(8,128)S(1)}, f32[8,40,128]{2,1,0:T(8,128)S(1)}, u32[]{:S(2)}, u32[]{:S(2)}) collective-permute-start(f32[8,40,128]{2,1,0:T(8,128)S(1)} %get-tuple-element.25), channel_id=1, source_target_pairs={{0,1},{1,0},{2,3},{3,2},{4,5},{5,4},{6,7},{7,6},{8,9},{9,8},{10,11... | collective-permute-start | bytes 491528 | tf_op jit(solution)/shard_map/ppermute | solution.py:564
  22.1 1.9 %collective-permute-start.3 = (f32[8,40,128]{2,1,0:T(8,128)S(1)}, f32[8,40,128]{2,1,0:T(8,128)S(1)}, u32[]{:S(2)}, u32[]{:S(2)}) collective-permute-start(f32[8,40,128]{2,1,0:T(8,128)S(1)} %get-tuple-element.26), channel_id=1, source_target_pairs={{0,7},{1,2},{2,1},{3,4},{4,3},{5,6},{6,5},{7,0},{8,15},{9,10},{10,... | collective-permute-start | bytes 491528 | tf_op jit(solution)/shard_map/ppermute | solution.py:563
  24.0 3.4 %collective-permute-start.6 = (f32[48,4,128]{2,1,0:T(4,128)S(1)}, f32[48,4,128]{2,1,0:T(4,128)S(1)}, u32[]{:S(2)}, u32[]{:S(2)}) collective-permute-start(f32[48,4,128]{2,1,0:T(4,128)S(1)} %get-tuple-element.31), channel_id=1, source_target_pairs={{0,1},{1,0},{2,3},{3,2},{4,5},{5,4},{6,7},{7,6},{8,9},{9,8},{10,11... | collective-permute-start | bytes 294920 | tf_op jit(solution)/shard_map/ppermute | solution.py:564
  27.4 4.0 %collective-permute-start.7 = (f32[48,4,128]{2,1,0:T(4,128)S(1)}, f32[48,4,128]{2,1,0:T(4,128)S(1)}, u32[]{:S(2)}, u32[]{:S(2)}) collective-permute-start(f32[48,4,128]{2,1,0:T(4,128)S(1)} %get-tuple-element.32), channel_id=1, source_target_pairs={{0,7},{1,2},{2,1},{3,4},{4,3},{5,6},{6,5},{7,0},{8,15},{9,10},{10,... | collective-permute-start | bytes 294920 | tf_op jit(solution)/shard_map/ppermute | solution.py:563
  31.4 0.0 collective-permute-done.2.near
  31.4 0.0 collective-permute-done.3.far
  31.4 3.2 %shard_map.88 = (f32[3,16,16,128]{3,2,1,0:T(8,128)S(1)}, f32[28,16,128]{2,1,0:T(8,128)S(1)}, f32[144,128]{1,0:T(8,128)S(1)}, f32[144,128]{1,0:T(8,128)S(1)}) custom-call(s32[2]{0:T(128)S(1)} %pad_add_fusion.place.refs_0_, f32[3,34,16,128]{3,2,1,0:T(8,128)S(1)} %get-tuple-element.23.wide_v, f32[30,16,128]{2,1,0:T(8,128)S(1)} %get-tuple-element.24.wide_d, ...), custom_call_target="tpu_custom_call" | custom-call | tf_op jit(solution)/shard_map/pallas_call | solution.py:594
  34.6 2.2 %collective-permute-start.4 = (f32[144,128]{1,0:T(8,128)S(1)}, f32[144,128]{1,0:T(8,128)S(1)}, u32[]{:S(2)}, u32[]{:S(2)}) collective-permute-start(f32[144,128]{1,0:T(8,128)S(1)} %get-tuple-element.29), channel_id=1, source_target_pairs={{0,1},{1,0},{2,3},{3,2},{4,5},{5,4},{6,7},{7,6},{8,9},{9,8},{10,11... | collective-permute-start | bytes 221192 | tf_op jit(solution)/shard_map/ppermute | solution.py:564
  36.8 3.1 %collective-permute-start.5 = (f32[144,128]{1,0:T(8,128)S(1)}, f32[144,128]{1,0:T(8,128)S(1)}, u32[]{:S(2)}, u32[]{:S(2)}) collective-permute-start(f32[144,128]{1,0:T(8,128)S(1)} %get-tuple-element.30), channel_id=1, source_target_pairs={{0,7},{1,2},{2,1},{3,4},{4,3},{5,6},{6,5},{7,0},{8,15},{9,10},{10,... | collective-permute-start | bytes 221192 | tf_op jit(solution)/shard_map/ppermute | solution.py:563
  39.9 0.0 collective-permute-done.6.near_p
  39.9 0.0 collective-permute-done.7.far_p
  40.0 0.5 collective-permute-done.4.near
  40.4 3.6 %collective-permute-done.5.far = f32[144,128]{1,0:T(8,128)S(1)} collective-permute-done((f32[144,128]{1,0:T(8,128)S(1)}, f32[144,128]{1,0:T(8,128)S(1)}, u32[]{:S(2)}, u32[]{:S(2)}) %collective-permute-start.5) | collective-permute-done | bytes 73760 | tf_op jit(solution)/shard_map/ppermute | solution.py:563
  44.0 2.7 %shard_map.89 = (f32[22,24,128]{2,1,0:T(8,128)S(1)}, f32[20,24,128]{2,1,0:T(8,128)S(1)}, f32[2,16,128]{2,1,0:T(8,128)S(1)}, f32[64,4,128]{2,1,0:T(4,128)}) custom-call(s32[2]{0:T(128)S(1)} %pad_add_fusion.place.refs_0_, f32[28,16,128]{2,1,0:T(8,128)S(1)} %get-tuple-element.27.source, f32[30,16,128]{2,1,0:T(8,128)S(1)} %get-tuple-element.28.wide_p, ...), custom_call_target="tpu_custom_call" | custom-call | tf_op jit(solution)/shard_map/pallas_call | solution.py:601
  46.7 17.5 %all-to-all-start = ((f32[64,4,128]{2,1,0:T(4,128)}), f32[64,4,128]{2,1,0:T(4,128)S(1)}, u32[]{:S(2)}, u32[]{:S(2)}) async-start(f32[64,4,128]{2,1,0:T(4,128)} %get-tuple-element.33), calls=%async_computation | async-start | bytes 262144 | tf_op jit(solution)/shard_map/all_to_all | solution.py:608
  64.3 3.5 %collective-permute-start.9 = (f32[2,16,128]{2,1,0:T(8,128)S(1)}, f32[2,16,128]{2,1,0:T(8,128)S(1)}, u32[]{:S(2)}, u32[]{:S(2)}) collective-permute-start(f32[2,16,128]{2,1,0:T(8,128)S(1)} %get-tuple-element.34.refs_2_), channel_id=1, source_target_pairs={{0,504},{8,16},{16,8},{24,32},{32,24},{40,48},{48,40},{56,64},{64,... | collective-permute-start | bytes 49160 | tf_op jit(solution)/shard_map/ppermute | solution.py:563
  67.8 6.6 %collective-permute-start.8 = (f32[2,16,128]{2,1,0:T(8,128)S(1)}, f32[2,16,128]{2,1,0:T(8,128)S(1)}, u32[]{:S(2)}, u32[]{:S(2)}) collective-permute-start(f32[2,16,128]{2,1,0:T(8,128)S(1)} %get-tuple-element.34.refs_2_), channel_id=1, source_target_pairs={{0,8},{8,0},{16,24},{24,16},{32,40},{40,32},{48,56},{56,48},{64,72... | collective-permute-start | bytes 49160 | tf_op jit(solution)/shard_map/ppermute | solution.py:564
  74.4 0.0 collective-permute-done.9.refs_4_
  74.4 0.8 collective-permute-done.8.refs_3_
  75.2 1.8 %all-to-all-done.refs_1_ = f32[64,4,128]{2,1,0:T(4,128)S(1)} async-done(((f32[64,4,128]{2,1,0:T(4,128)}), f32[64,4,128]{2,1,0:T(4,128)S(1)}, u32[]{:S(2)}, u32[]{:S(2)}) %all-to-all-start) | async-done | bytes 131104 | tf_op jit(solution)/shard_map/all_to_all | solution.py:608
  77.1 0.6 shard_map.90
  77.7 0.0 copy-start.3
  77.7 0.0 copy-start.4
  77.7 9.8 %all_to_all.10.strips = f32[8,19,4,128]{3,2,1,0:T(4,128)S(1)} all-to-all(f32[8,19,4,128]{3,2,1,0:T(4,128)S(1)} %get-tuple-element.35), channel_id=1, replica_groups=mesh['gx'=64,'gy'=8] {'gy'}, dimensions={0} | all-to-all | bytes 622592 | tf_op jit(solution)/shard_map/all_to_all | solution.py:614
  87.5 0.0 copy-done.3
  87.5 0.0 copy-done.4
  87.5 4.1 %shard_map.91 = (f32[3,16,16,128]{3,2,1,0:T(8,128)}, f32[16,16,128]{2,1,0:T(8,128)}) custom-call(s32[2]{0:T(128)S(1)} %pad_add_fusion.place.refs_0_, f32[8,19,4,128]{3,2,1,0:T(4,128)S(1)} %all_to_all.10.strips, f32[6,16,128]{2,1,0:T(8,128)S(1)} %get-tuple-element.36.window, f32[22,24,128]{2,1,0:T(8,128)S(1)} %get-tuple-element.37.finest, ...), custom_call_target="tpu_custom_call" | custom-call | tf_op jit(solution)/shard_map/pallas_call | solution.py:615
Async XLA Ops:
  0.6 18.6 %copy-start.2 = (s32[16,16,128]{2,1,0:T(8,128)S(1)}, s32[16,16,128]{2,1,0:T(8,128)}, u32[]{:S(2)}) copy-start(s32[16,16,128]{2,1,0:T(8,128)} %turbine.3) | copy-start | bytes 393220
  0.6 18.6 %copy-start.1 = (f32[16,16,128]{2,1,0:T(8,128)S(1)}, f32[16,16,128]{2,1,0:T(8,128)}, u32[]{:S(2)}) copy-start(f32[16,16,128]{2,1,0:T(8,128)} %pressure.3) | copy-start | bytes 393220
  0.6 18.6 %copy-start = (f32[3,16,16,128]{3,2,1,0:T(8,128)S(1)}, f32[3,16,16,128]{3,2,1,0:T(8,128)}, u32[]{:S(2)}) copy-start(f32[3,16,16,128]{3,2,1,0:T(8,128)} %velocity.3) | copy-start | bytes 1179652
  2.0 10.8 %collective-permute-start = (f32[41,16,128]{2,1,0:T(8,128)S(1)}, f32[41,16,128]{2,1,0:T(8,128)S(1)}, u32[]{:S(2)}, u32[]{:S(2)}) collective-permute-start(f32[41,16,128]{2,1,0:T(8,128)S(1)} %get-tuple-element.21), channel_id=1, source_target_pairs={{0,8},{8,0},{16,24},{24,16},{32,40},{40,32},{48,56},{56,48},{64,72... | collective-permute-start | bytes 1007624 | tf_op jit(solution)/shard_map/ppermute | solution.py:564
  10.8 8.5 %collective-permute-start.1 = (f32[41,16,128]{2,1,0:T(8,128)S(1)}, f32[41,16,128]{2,1,0:T(8,128)S(1)}, u32[]{:S(2)}, u32[]{:S(2)}) collective-permute-start(f32[41,16,128]{2,1,0:T(8,128)S(1)} %get-tuple-element.22), channel_id=1, source_target_pairs={{0,504},{8,16},{16,8},{24,32},{32,24},{40,48},{48,40},{56,64},{64,... | collective-permute-start | bytes 1007624 | tf_op jit(solution)/shard_map/ppermute | solution.py:563
  12.7 6.6 %copy-start.5 = (s32[16,16]{1,0:T(8,128)S(1)}, s32[16,16]{1,0:T(8,128)}, u32[]{:S(2)}) copy-start(s32[16,16]{1,0:T(8,128)} %land.3) | copy-start | bytes 3076
  12.7 6.6 %copy-start.6 = (f32[16]{0:T(128)S(1)}, f32[16]{0:T(128)}, u32[]{:S(2)}) copy-start(f32[16]{0:T(128)} %drag_table.1) | copy-start | bytes 196
  20.2 11.3 %collective-permute-start.2 = (f32[8,40,128]{2,1,0:T(8,128)S(1)}, f32[8,40,128]{2,1,0:T(8,128)S(1)}, u32[]{:S(2)}, u32[]{:S(2)}) collective-permute-start(f32[8,40,128]{2,1,0:T(8,128)S(1)} %get-tuple-element.25), channel_id=1, source_target_pairs={{0,1},{1,0},{2,3},{3,2},{4,5},{5,4},{6,7},{7,6},{8,9},{9,8},{10,11... | collective-permute-start | bytes 491528 | tf_op jit(solution)/shard_map/ppermute | solution.py:564
  22.1 9.3 %collective-permute-start.3 = (f32[8,40,128]{2,1,0:T(8,128)S(1)}, f32[8,40,128]{2,1,0:T(8,128)S(1)}, u32[]{:S(2)}, u32[]{:S(2)}) collective-permute-start(f32[8,40,128]{2,1,0:T(8,128)S(1)} %get-tuple-element.26), channel_id=1, source_target_pairs={{0,7},{1,2},{2,1},{3,4},{4,3},{5,6},{6,5},{7,0},{8,15},{9,10},{10,... | collective-permute-start | bytes 491528 | tf_op jit(solution)/shard_map/ppermute | solution.py:563
  24.0 15.9 %collective-permute-start.6 = (f32[48,4,128]{2,1,0:T(4,128)S(1)}, f32[48,4,128]{2,1,0:T(4,128)S(1)}, u32[]{:S(2)}, u32[]{:S(2)}) collective-permute-start(f32[48,4,128]{2,1,0:T(4,128)S(1)} %get-tuple-element.31), channel_id=1, source_target_pairs={{0,1},{1,0},{2,3},{3,2},{4,5},{5,4},{6,7},{7,6},{8,9},{9,8},{10,11... | collective-permute-start | bytes 294920 | tf_op jit(solution)/shard_map/ppermute | solution.py:564
  27.4 12.6 %collective-permute-start.7 = (f32[48,4,128]{2,1,0:T(4,128)S(1)}, f32[48,4,128]{2,1,0:T(4,128)S(1)}, u32[]{:S(2)}, u32[]{:S(2)}) collective-permute-start(f32[48,4,128]{2,1,0:T(4,128)S(1)} %get-tuple-element.32), channel_id=1, source_target_pairs={{0,7},{1,2},{2,1},{3,4},{4,3},{5,6},{6,5},{7,0},{8,15},{9,10},{10,... | collective-permute-start | bytes 294920 | tf_op jit(solution)/shard_map/ppermute | solution.py:563
  34.6 5.8 %collective-permute-start.4 = (f32[144,128]{1,0:T(8,128)S(1)}, f32[144,128]{1,0:T(8,128)S(1)}, u32[]{:S(2)}, u32[]{:S(2)}) collective-permute-start(f32[144,128]{1,0:T(8,128)S(1)} %get-tuple-element.29), channel_id=1, source_target_pairs={{0,1},{1,0},{2,3},{3,2},{4,5},{5,4},{6,7},{7,6},{8,9},{9,8},{10,11... | collective-permute-start | bytes 221192 | tf_op jit(solution)/shard_map/ppermute | solution.py:564
  36.8 7.2 %collective-permute-start.5 = (f32[144,128]{1,0:T(8,128)S(1)}, f32[144,128]{1,0:T(8,128)S(1)}, u32[]{:S(2)}, u32[]{:S(2)}) collective-permute-start(f32[144,128]{1,0:T(8,128)S(1)} %get-tuple-element.30), channel_id=1, source_target_pairs={{0,7},{1,2},{2,1},{3,4},{4,3},{5,6},{6,5},{7,0},{8,15},{9,10},{10,... | collective-permute-start | bytes 221192 | tf_op jit(solution)/shard_map/ppermute | solution.py:563
  46.7 30.3 %all-to-all-start = ((f32[64,4,128]{2,1,0:T(4,128)}), f32[64,4,128]{2,1,0:T(4,128)S(1)}, u32[]{:S(2)}, u32[]{:S(2)}) async-start(f32[64,4,128]{2,1,0:T(4,128)} %get-tuple-element.33), calls=%async_computation | async-start | bytes 262144 | tf_op jit(solution)/shard_map/all_to_all | solution.py:608
  64.3 10.1 %collective-permute-start.9 = (f32[2,16,128]{2,1,0:T(8,128)S(1)}, f32[2,16,128]{2,1,0:T(8,128)S(1)}, u32[]{:S(2)}, u32[]{:S(2)}) collective-permute-start(f32[2,16,128]{2,1,0:T(8,128)S(1)} %get-tuple-element.34.refs_2_), channel_id=1, source_target_pairs={{0,504},{8,16},{16,8},{24,32},{32,24},{40,48},{48,40},{56,64},{64,... | collective-permute-start | bytes 49160 | tf_op jit(solution)/shard_map/ppermute | solution.py:563
  67.8 7.4 %collective-permute-start.8 = (f32[2,16,128]{2,1,0:T(8,128)S(1)}, f32[2,16,128]{2,1,0:T(8,128)S(1)}, u32[]{:S(2)}, u32[]{:S(2)}) collective-permute-start(f32[2,16,128]{2,1,0:T(8,128)S(1)} %get-tuple-element.34.refs_2_), channel_id=1, source_target_pairs={{0,8},{8,0},{16,24},{24,16},{32,40},{40,32},{48,56},{56,48},{64,72... | collective-permute-start | bytes 49160 | tf_op jit(solution)/shard_map/ppermute | solution.py:564
  77.7 9.8 %copy-start.3 = (bf16[384,384]{1,0:T(8,128)(2,1)S(1)}, bf16[384,384]{1,0:T(8,128)(2,1)}, u32[]{:S(2)}) copy-start(bf16[384,384]{1,0:T(8,128)(2,1)} %constant.14.clone.third) | copy-start | bytes 884740
  77.7 9.8 %copy-start.4 = (bf16[384,384]{1,0:T(8,128)(2,1)S(1)}, bf16[384,384]{1,0:T(8,128)(2,1)}, u32[]{:S(2)}) copy-start(bf16[384,384]{1,0:T(8,128)(2,1)} %constant.13.clone.second) | copy-start | bytes 884740

commit v8 on v7

--- a/solution.py
+++ b/solution.py
@@ -135,7 +135,7 @@
         copy.wait()
 
 
-def widen_x(place, drag_table, land, velocity, pressure, turbine, near, far, wide_v, wide_p, wide_d, near_y, far_y, near_p, far_p):
+def widen_x(place, drag_table, land, velocity, pressure, turbine, far, near, wide_v, wide_p, wide_d, near_y, far_y, near_p, far_p):
     core = place[0] % 2
     odd = place[1] % 2
     columns = ground_columns(land[...], drag_table)
@@ -206,7 +206,7 @@
     return jnp.concatenate([one.astype(jnp.bfloat16)] * 3, axis=0)
 
 
-def advance(place, wide_v, wide_d, near, far, star, source, near_y, far_y, v, dr, tau, part):
+def advance(place, wide_v, wide_d, far, near, star, source, near_y, far_y, v, dr, tau, part):
     odd = place[1] % 2
     v[:, :, 0:B, :] = wide_v[...]
     dr[2 : 2 + PX, 0:B, :] = wide_d[...]
@@ -343,7 +343,7 @@
     return 0.5 * total
 
 
-def presmooth(place, source, wide_p, near, far, near_p, far_p, finest, right, packed_one, packed_two, p, s, q, f1, a1, b1):
+def presmooth(place, source, wide_p, far, near, far_p, near_p, finest, right, packed_one, packed_two, p, s, q, f1, a1, b1):
     odd = place[1] % 2
     p[:, 0:B, :] = wide_p[...]
     s[1 : PX - 1, 0:B, :] = source[...]
@@ -588,7 +588,7 @@
         + [shape(8, 40, 128)] * 2
         + [shape(N_P, 4, 128)] * 2,
         [SMEM, SMEM] + [VMEM] * 6,
-    )(place, surface_drag, land_type, velocity, pressure, turbine_cells, near, far)
+    )(place, surface_drag, land_type, velocity, pressure, turbine_cells, far, near)
     near, far = exchange(near, far, "gy")
     near_p, far_p = exchange(near_p, far_p, "gy")
     star, source, near, far = call(
@@ -596,14 +596,14 @@
         [shape(3, B, B, 128), shape(PX - 2, B, 128), shape(N_S, 128), shape(N_S, 128)],
         [SMEM] + [VMEM] * 4,
         [(3, VX, 24, 128), (VX, 24, 128), (3, VX, 24, 128), (3, VX, 24, 128)],
-    )(place, wide_v, wide_d, near, far)
+    )(place, wide_v, wide_d, far, near)
     near, far = exchange(near, far, "gy")
     finest, right, packed_one, packed_two = call(
         presmooth,
         [shape(22, 24, 128), shape(20, 24, 128), shape(2, B, 128), shape(gx, 4, 128)],
         [SMEM] + [VMEM] * 6,
         [(PX, 32, 128)] * 3 + [(12, 32, 128)] * 3,
-    )(place, source, wide_p, near, far, near_p, far_p)
+    )(place, source, wide_p, far, near, far_p, near_p)
     near, far = exchange(packed_one, packed_one, "gx")
     blocks = lax.all_to_all(packed_two, "gx", 0, 0, tiled=True)
     strips, window = call(

time: 92.1 us -> 89.5 us (0.972)
  waiting for transfers between devices: 13.1 us -> 6.69 us
  starting transfers between devices: 54.9 us -> 57.7 us
  blocking collectives: 9.77 us -> 10.9 us
    ppermute x5, waiting for transfers between devices: 10 us -> 1.41 us  [exchange(): far_block = lax.ppermute(far_block, axis, far)]
    ppermute x5, starting transfers between devices: 14.5 us -> 20.8 us  [exchange(): far_block = lax.ppermute(far_block, axis, far)]
    all_to_all x1, starting transfers between devices: 17.5 us -> 12.2 us  [per_device(): blocks = lax.all_to_all(packed_two, 'gx', 0, 0, tiled=True)]
    ppermute x5, waiting for transfers between devices: 1.27 us -> 3.47 us  [exchange(): return (lax.ppermute(near_block, axis, near), far_block)]
    ppermute x5, starting transfers between devices: 22.8 us -> 24.7 us  [exchange(): return (lax.ppermute(near_block, axis, near), far_block)]
    all_to_all x1, blocking collectives: 9.77 us -> 10.9 us  [per_device(): strips = lax.all_to_all(strips, 'gy', 0, 0, tiled=True)]
  transfers between devices with their start and end apart: 11 -> 11, of which waited for: 5 -> 5; matrix products, arithmetic and copies ran while one was open for 0% -> 0% of each run, Pallas kernels for 3% -> 4%
where the time goes in v8:
time: 89.5 us; the launch traced here: 89 us
  starting transfers between devices  57.7 us (64%)
  Pallas kernels  12.8 us (14%)
  blocking collectives  10.9 us (12%)
  waiting for transfers between devices  6.69 us (7%)
    ppermute x5, starting transfers between devices, exchange(): return (lax.ppermute(near_block, axis, near), far_block)  24.7 us
    ppermute x5, starting transfers between devices, exchange(): far_block = lax.ppermute(far_block, axis, far)  20.8 us
    all_to_all x1, starting transfers between devices, per_device(): blocks = lax.all_to_all(packed_two, 'gx', 0, 0, tiled=True)  12.2 us
    all_to_all x1, blocking collectives, per_device(): strips = lax.all_to_all(strips, 'gy', 0, 0, tiled=True)  10.9 us
    pallas_call x1, Pallas kernels, per_device(): call(finish, [shape(3, B, B, 128), shape(B, B, 128)], [SMEM] + [VMEM] * 7...  4.08 us
    ppermute x5, waiting for transfers between devices, exchange(): return (lax.ppermute(near_block, axis, near), far_block)  3.47 us
    pallas_call x1, Pallas kernels, per_device(): call(advance, [shape(3, B, B, 128), shape(PX - 2, B, 128), shape(N_S, 128...  3.18 us
    pallas_call x1, Pallas kernels, per_device(): call(presmooth, [shape(22, 24, 128), shape(20, 24, 128), shape(2, B, 128)...  2.74 us
  transfers between devices with their start and end apart: 11, of which 5 were waited for; matrix products, arithmetic and copies ran while one was open for 0% of the time, Pallas kernels for 4%

profile of v8, /device:TPU:1, one launch (start us, length us, event | category | flops | bytes accessed | tf_op | source)
XLA Modules:
  0.0 89.0 jit_solution(3547028554264262334)
XLA Ops:
  0.6 0.0 copy-start.2
  0.6 0.0 copy-start.1
  0.6 0.0 copy-start
  0.7 1.3 %shard_map.86 = (f32[41,16,128]{2,1,0:T(8,128)S(1)}, f32[41,16,128]{2,1,0:T(8,128)S(1)}) custom-call(f32[16]{0:T(128)} %drag_table.1, s32[16,16]{1,0:T(8,128)} %land.3, f32[3,16,16,128]{3,2,1,0:T(8,128)} %velocity.3, f32[16,16,128]{2,1,0:T(8,128)} %pressure.3, s32[16,16,128]{2,1,0:T(8,128)} %turbine.3), custom_call_target="tpu_custom_call" | custom-call | tf_op jit(solution)/shard_map/pallas_call | solution.py:572
  2.0 4.6 %collective-permute-start = (f32[41,16,128]{2,1,0:T(8,128)S(1)}, f32[41,16,128]{2,1,0:T(8,128)S(1)}, u32[]{:S(2)}, u32[]{:S(2)}) collective-permute-start(f32[41,16,128]{2,1,0:T(8,128)S(1)} %get-tuple-element.21), channel_id=1, source_target_pairs={{0,504},{8,16},{16,8},{24,32},{32,24},{40,48},{48,40},{56,64},{64,... | collective-permute-start | bytes 1007624 | tf_op jit(solution)/shard_map/ppermute | solution.py:563
  6.6 12.1 %collective-permute-start.1 = (f32[41,16,128]{2,1,0:T(8,128)S(1)}, f32[41,16,128]{2,1,0:T(8,128)S(1)}, u32[]{:S(2)}, u32[]{:S(2)}) collective-permute-start(f32[41,16,128]{2,1,0:T(8,128)S(1)} %get-tuple-element.22), channel_id=1, source_target_pairs={{0,8},{8,0},{16,24},{24,16},{32,40},{40,32},{48,56},{56,48},{64,72... | collective-permute-start | bytes 1007624 | tf_op jit(solution)/shard_map/ppermute | solution.py:564
  18.7 0.0 copy-start.5
  18.7 0.0 copy-start.6
  18.7 0.1 pad_add_fusion.place.refs_0_
  18.8 0.0 collective-permute-done.far
  18.8 1.1 %collective-permute-done.1.near = f32[41,16,128]{2,1,0:T(8,128)S(1)} collective-permute-done((f32[41,16,128]{2,1,0:T(8,128)S(1)}, f32[41,16,128]{2,1,0:T(8,128)S(1)}, u32[]{:S(2)}, u32[]{:S(2)}) %collective-permute-start.1) | collective-permute-done | bytes 335904 | tf_op jit(solution)/shard_map/ppermute | solution.py:564
  20.0 0.0 copy-done.2
  20.0 0.0 copy-done.1
  20.0 0.0 copy-done
  20.0 0.0 copy-done.5
  20.0 0.0 copy-done.6
  20.0 0.8 shard_map.87
  20.8 5.3 %collective-permute-start.2 = (f32[8,40,128]{2,1,0:T(8,128)S(1)}, f32[8,40,128]{2,1,0:T(8,128)S(1)}, u32[]{:S(2)}, u32[]{:S(2)}) collective-permute-start(f32[8,40,128]{2,1,0:T(8,128)S(1)} %get-tuple-element.25), channel_id=1, source_target_pairs={{0,7},{1,2},{2,1},{3,4},{4,3},{5,6},{6,5},{7,0},{8,15},{9,10},{10,... | collective-permute-start | bytes 491528 | tf_op jit(solution)/shard_map/ppermute | solution.py:563
  26.1 1.9 %collective-permute-start.3 = (f32[8,40,128]{2,1,0:T(8,128)S(1)}, f32[8,40,128]{2,1,0:T(8,128)S(1)}, u32[]{:S(2)}, u32[]{:S(2)}) collective-permute-start(f32[8,40,128]{2,1,0:T(8,128)S(1)} %get-tuple-element.26), channel_id=1, source_target_pairs={{0,1},{1,0},{2,3},{3,2},{4,5},{5,4},{6,7},{7,6},{8,9},{9,8},{10,11... | collective-permute-start | bytes 491528 | tf_op jit(solution)/shard_map/ppermute | solution.py:564
  28.1 3.6 %collective-permute-start.6 = (f32[48,4,128]{2,1,0:T(4,128)S(1)}, f32[48,4,128]{2,1,0:T(4,128)S(1)}, u32[]{:S(2)}, u32[]{:S(2)}) collective-permute-start(f32[48,4,128]{2,1,0:T(4,128)S(1)} %get-tuple-element.31), channel_id=1, source_target_pairs={{0,7},{1,2},{2,1},{3,4},{4,3},{5,6},{6,5},{7,0},{8,15},{9,10},{10,... | collective-permute-start | bytes 294920 | tf_op jit(solution)/shard_map/ppermute | solution.py:563
  31.7 1.9 %collective-permute-start.7 = (f32[48,4,128]{2,1,0:T(4,128)S(1)}, f32[48,4,128]{2,1,0:T(4,128)S(1)}, u32[]{:S(2)}, u32[]{:S(2)}) collective-permute-start(f32[48,4,128]{2,1,0:T(4,128)S(1)} %get-tuple-element.32), channel_id=1, source_target_pairs={{0,1},{1,0},{2,3},{3,2},{4,5},{5,4},{6,7},{7,6},{8,9},{9,8},{10,11... | collective-permute-start | bytes 294920 | tf_op jit(solution)/shard_map/ppermute | solution.py:564
  33.6 0.0 collective-permute-done.2.far
  33.6 0.0 collective-permute-done.3.near
  33.6 3.2 %shard_map.88 = (f32[3,16,16,128]{3,2,1,0:T(8,128)S(1)}, f32[28,16,128]{2,1,0:T(8,128)S(1)}, f32[144,128]{1,0:T(8,128)S(1)}, f32[144,128]{1,0:T(8,128)S(1)}) custom-call(s32[2]{0:T(128)S(1)} %pad_add_fusion.place.refs_0_, f32[3,34,16,128]{3,2,1,0:T(8,128)S(1)} %get-tuple-element.23.wide_v, f32[30,16,128]{2,1,0:T(8,128)S(1)} %get-tuple-element.24.wide_d, ...), custom_call_target="tpu_custom_call" | custom-call | tf_op jit(solution)/shard_map/pallas_call | solution.py:594
  36.8 3.8 %collective-permute-start.4 = (f32[144,128]{1,0:T(8,128)S(1)}, f32[144,128]{1,0:T(8,128)S(1)}, u32[]{:S(2)}, u32[]{:S(2)}) collective-permute-start(f32[144,128]{1,0:T(8,128)S(1)} %get-tuple-element.29), channel_id=1, source_target_pairs={{0,7},{1,2},{2,1},{3,4},{4,3},{5,6},{6,5},{7,0},{8,15},{9,10},{10,... | collective-permute-start | bytes 221192 | tf_op jit(solution)/shard_map/ppermute | solution.py:563
  40.6 2.2 %collective-permute-start.5 = (f32[144,128]{1,0:T(8,128)S(1)}, f32[144,128]{1,0:T(8,128)S(1)}, u32[]{:S(2)}, u32[]{:S(2)}) collective-permute-start(f32[144,128]{1,0:T(8,128)S(1)} %get-tuple-element.30), channel_id=1, source_target_pairs={{0,1},{1,0},{2,3},{3,2},{4,5},{5,4},{6,7},{7,6},{8,9},{9,8},{10,11... | collective-permute-start | bytes 221192 | tf_op jit(solution)/shard_map/ppermute | solution.py:564
  42.8 0.0 collective-permute-done.6.far_p
  42.8 0.0 collective-permute-done.7.near_p
  42.8 1.4 %collective-permute-done.4.far = f32[144,128]{1,0:T(8,128)S(1)} collective-permute-done((f32[144,128]{1,0:T(8,128)S(1)}, f32[144,128]{1,0:T(8,128)S(1)}, u32[]{:S(2)}, u32[]{:S(2)}) %collective-permute-start.4) | collective-permute-done | bytes 73760 | tf_op jit(solution)/shard_map/ppermute | solution.py:563
  44.2 1.5 %collective-permute-done.5.near = f32[144,128]{1,0:T(8,128)S(1)} collective-permute-done((f32[144,128]{1,0:T(8,128)S(1)}, f32[144,128]{1,0:T(8,128)S(1)}, u32[]{:S(2)}, u32[]{:S(2)}) %collective-permute-start.5) | collective-permute-done | bytes 73760 | tf_op jit(solution)/shard_map/ppermute | solution.py:564
  45.7 2.7 %shard_map.89 = (f32[22,24,128]{2,1,0:T(8,128)S(1)}, f32[20,24,128]{2,1,0:T(8,128)S(1)}, f32[2,16,128]{2,1,0:T(8,128)S(1)}, f32[64,4,128]{2,1,0:T(4,128)}) custom-call(s32[2]{0:T(128)S(1)} %pad_add_fusion.place.refs_0_, f32[28,16,128]{2,1,0:T(8,128)S(1)} %get-tuple-element.27.source, f32[30,16,128]{2,1,0:T(8,128)S(1)} %get-tuple-element.28.wide_p, ...), custom_call_target="tpu_custom_call" | custom-call | tf_op jit(solution)/shard_map/pallas_call | solution.py:601
  48.4 12.2 %all-to-all-start = ((f32[64,4,128]{2,1,0:T(4,128)}), f32[64,4,128]{2,1,0:T(4,128)S(1)}, u32[]{:S(2)}, u32[]{:S(2)}) async-start(f32[64,4,128]{2,1,0:T(4,128)} %get-tuple-element.33), calls=%async_computation | async-start | bytes 262144 | tf_op jit(solution)/shard_map/all_to_all | solution.py:608
  60.6 3.5 %collective-permute-start.9 = (f32[2,16,128]{2,1,0:T(8,128)S(1)}, f32[2,16,128]{2,1,0:T(8,128)S(1)}, u32[]{:S(2)}, u32[]{:S(2)}) collective-permute-start(f32[2,16,128]{2,1,0:T(8,128)S(1)} %get-tuple-element.34.refs_2_), channel_id=1, source_target_pairs={{0,504},{8,16},{16,8},{24,32},{32,24},{40,48},{48,40},{56,64},{64,... | collective-permute-start | bytes 49160 | tf_op jit(solution)/shard_map/ppermute | solution.py:563
  64.2 6.6 %collective-permute-start.8 = (f32[2,16,128]{2,1,0:T(8,128)S(1)}, f32[2,16,128]{2,1,0:T(8,128)S(1)}, u32[]{:S(2)}, u32[]{:S(2)}) collective-permute-start(f32[2,16,128]{2,1,0:T(8,128)S(1)} %get-tuple-element.34.refs_2_), channel_id=1, source_target_pairs={{0,8},{8,0},{16,24},{24,16},{32,40},{40,32},{48,56},{56,48},{64,72... | collective-permute-start | bytes 49160 | tf_op jit(solution)/shard_map/ppermute | solution.py:564
  70.8 0.0 collective-permute-done.9.refs_4_
  70.8 0.8 collective-permute-done.8.refs_3_
  71.6 1.8 %all-to-all-done.refs_1_ = f32[64,4,128]{2,1,0:T(4,128)S(1)} async-done(((f32[64,4,128]{2,1,0:T(4,128)}), f32[64,4,128]{2,1,0:T(4,128)S(1)}, u32[]{:S(2)}, u32[]{:S(2)}) %all-to-all-start) | async-done | bytes 131104 | tf_op jit(solution)/shard_map/all_to_all | solution.py:608
  73.4 0.6 shard_map.90
  74.0 0.0 copy-start.3
  74.0 0.0 copy-start.4
  74.0 10.9 %all_to_all.10.strips = f32[8,19,4,128]{3,2,1,0:T(4,128)S(1)} all-to-all(f32[8,19,4,128]{3,2,1,0:T(4,128)S(1)} %get-tuple-element.35), channel_id=1, replica_groups=mesh['gx'=64,'gy'=8] {'gy'}, dimensions={0} | all-to-all | bytes 622592 | tf_op jit(solution)/shard_map/all_to_all | solution.py:614
  84.9 0.0 copy-done.3
  84.9 0.0 copy-done.4
  84.9 4.1 %shard_map.91 = (f32[3,16,16,128]{3,2,1,0:T(8,128)}, f32[16,16,128]{2,1,0:T(8,128)}) custom-call(s32[2]{0:T(128)S(1)} %pad_add_fusion.place.refs_0_, f32[8,19,4,128]{3,2,1,0:T(4,128)S(1)} %all_to_all.10.strips, f32[6,16,128]{2,1,0:T(8,128)S(1)} %get-tuple-element.36.window, f32[22,24,128]{2,1,0:T(8,128)S(1)} %get-tuple-element.37.finest, ...), custom_call_target="tpu_custom_call" | custom-call | tf_op jit(solution)/shard_map/pallas_call | solution.py:615
Async XLA Ops:
  0.6 19.3 %copy-start.2 = (s32[16,16,128]{2,1,0:T(8,128)S(1)}, s32[16,16,128]{2,1,0:T(8,128)}, u32[]{:S(2)}) copy-start(s32[16,16,128]{2,1,0:T(8,128)} %turbine.3) | copy-start | bytes 393220
  0.6 19.3 %copy-start.1 = (f32[16,16,128]{2,1,0:T(8,128)S(1)}, f32[16,16,128]{2,1,0:T(8,128)}, u32[]{:S(2)}) copy-start(f32[16,16,128]{2,1,0:T(8,128)} %pressure.3) | copy-start | bytes 393220
  0.6 19.3 %copy-start = (f32[3,16,16,128]{3,2,1,0:T(8,128)S(1)}, f32[3,16,16,128]{3,2,1,0:T(8,128)}, u32[]{:S(2)}) copy-start(f32[3,16,16,128]{3,2,1,0:T(8,128)} %velocity.3) | copy-start | bytes 1179652
  2.0 16.8 %collective-permute-start = (f32[41,16,128]{2,1,0:T(8,128)S(1)}, f32[41,16,128]{2,1,0:T(8,128)S(1)}, u32[]{:S(2)}, u32[]{:S(2)}) collective-permute-start(f32[41,16,128]{2,1,0:T(8,128)S(1)} %get-tuple-element.21), channel_id=1, source_target_pairs={{0,504},{8,16},{16,8},{24,32},{32,24},{40,48},{48,40},{56,64},{64,... | collective-permute-start | bytes 1007624 | tf_op jit(solution)/shard_map/ppermute | solution.py:563
  6.6 13.4 %collective-permute-start.1 = (f32[41,16,128]{2,1,0:T(8,128)S(1)}, f32[41,16,128]{2,1,0:T(8,128)S(1)}, u32[]{:S(2)}, u32[]{:S(2)}) collective-permute-start(f32[41,16,128]{2,1,0:T(8,128)S(1)} %get-tuple-element.22), channel_id=1, source_target_pairs={{0,8},{8,0},{16,24},{24,16},{32,40},{40,32},{48,56},{56,48},{64,72... | collective-permute-start | bytes 1007624 | tf_op jit(solution)/shard_map/ppermute | solution.py:564
  18.7 1.3 %copy-start.5 = (s32[16,16]{1,0:T(8,128)S(1)}, s32[16,16]{1,0:T(8,128)}, u32[]{:S(2)}) copy-start(s32[16,16]{1,0:T(8,128)} %land.3) | copy-start | bytes 3076
  18.7 1.2 %copy-start.6 = (f32[16]{0:T(128)S(1)}, f32[16]{0:T(128)}, u32[]{:S(2)}) copy-start(f32[16]{0:T(128)} %drag_table.1) | copy-start | bytes 196
  20.8 12.8 %collective-permute-start.2 = (f32[8,40,128]{2,1,0:T(8,128)S(1)}, f32[8,40,128]{2,1,0:T(8,128)S(1)}, u32[]{:S(2)}, u32[]{:S(2)}) collective-permute-start(f32[8,40,128]{2,1,0:T(8,128)S(1)} %get-tuple-element.25), channel_id=1, source_target_pairs={{0,7},{1,2},{2,1},{3,4},{4,3},{5,6},{6,5},{7,0},{8,15},{9,10},{10,... | collective-permute-start | bytes 491528 | tf_op jit(solution)/shard_map/ppermute | solution.py:563
  26.1 7.5 %collective-permute-start.3 = (f32[8,40,128]{2,1,0:T(8,128)S(1)}, f32[8,40,128]{2,1,0:T(8,128)S(1)}, u32[]{:S(2)}, u32[]{:S(2)}) collective-permute-start(f32[8,40,128]{2,1,0:T(8,128)S(1)} %get-tuple-element.26), channel_id=1, source_target_pairs={{0,1},{1,0},{2,3},{3,2},{4,5},{5,4},{6,7},{7,6},{8,9},{9,8},{10,11... | collective-permute-start | bytes 491528 | tf_op jit(solution)/shard_map/ppermute | solution.py:564
  28.1 14.7 %collective-permute-start.6 = (f32[48,4,128]{2,1,0:T(4,128)S(1)}, f32[48,4,128]{2,1,0:T(4,128)S(1)}, u32[]{:S(2)}, u32[]{:S(2)}) collective-permute-start(f32[48,4,128]{2,1,0:T(4,128)S(1)} %get-tuple-element.31), channel_id=1, source_target_pairs={{0,7},{1,2},{2,1},{3,4},{4,3},{5,6},{6,5},{7,0},{8,15},{9,10},{10,... | collective-permute-start | bytes 294920 | tf_op jit(solution)/shard_map/ppermute | solution.py:563
  31.7 11.1 %collective-permute-start.7 = (f32[48,4,128]{2,1,0:T(4,128)S(1)}, f32[48,4,128]{2,1,0:T(4,128)S(1)}, u32[]{:S(2)}, u32[]{:S(2)}) collective-permute-start(f32[48,4,128]{2,1,0:T(4,128)S(1)} %get-tuple-element.32), channel_id=1, source_target_pairs={{0,1},{1,0},{2,3},{3,2},{4,5},{5,4},{6,7},{7,6},{8,9},{9,8},{10,11... | collective-permute-start | bytes 294920 | tf_op jit(solution)/shard_map/ppermute | solution.py:564
  36.8 7.4 %collective-permute-start.4 = (f32[144,128]{1,0:T(8,128)S(1)}, f32[144,128]{1,0:T(8,128)S(1)}, u32[]{:S(2)}, u32[]{:S(2)}) collective-permute-start(f32[144,128]{1,0:T(8,128)S(1)} %get-tuple-element.29), channel_id=1, source_target_pairs={{0,7},{1,2},{2,1},{3,4},{4,3},{5,6},{6,5},{7,0},{8,15},{9,10},{10,... | collective-permute-start | bytes 221192 | tf_op jit(solution)/shard_map/ppermute | solution.py:563
  40.6 5.1 %collective-permute-start.5 = (f32[144,128]{1,0:T(8,128)S(1)}, f32[144,128]{1,0:T(8,128)S(1)}, u32[]{:S(2)}, u32[]{:S(2)}) collective-permute-start(f32[144,128]{1,0:T(8,128)S(1)} %get-tuple-element.30), channel_id=1, source_target_pairs={{0,1},{1,0},{2,3},{3,2},{4,5},{5,4},{6,7},{7,6},{8,9},{9,8},{10,11... | collective-permute-start | bytes 221192 | tf_op jit(solution)/shard_map/ppermute | solution.py:564
  48.4 24.9 %all-to-all-start = ((f32[64,4,128]{2,1,0:T(4,128)}), f32[64,4,128]{2,1,0:T(4,128)S(1)}, u32[]{:S(2)}, u32[]{:S(2)}) async-start(f32[64,4,128]{2,1,0:T(4,128)} %get-tuple-element.33), calls=%async_computation | async-start | bytes 262144 | tf_op jit(solution)/shard_map/all_to_all | solution.py:608
  60.6 10.1 %collective-permute-start.9 = (f32[2,16,128]{2,1,0:T(8,128)S(1)}, f32[2,16,128]{2,1,0:T(8,128)S(1)}, u32[]{:S(2)}, u32[]{:S(2)}) collective-permute-start(f32[2,16,128]{2,1,0:T(8,128)S(1)} %get-tuple-element.34.refs_2_), channel_id=1, source_target_pairs={{0,504},{8,16},{16,8},{24,32},{32,24},{40,48},{48,40},{56,64},{64,... | collective-permute-start | bytes 49160 | tf_op jit(solution)/shard_map/ppermute | solution.py:563
  64.2 7.4 %collective-permute-start.8 = (f32[2,16,128]{2,1,0:T(8,128)S(1)}, f32[2,16,128]{2,1,0:T(8,128)S(1)}, u32[]{:S(2)}, u32[]{:S(2)}) collective-permute-start(f32[2,16,128]{2,1,0:T(8,128)S(1)} %get-tuple-element.34.refs_2_), channel_id=1, source_target_pairs={{0,8},{8,0},{16,24},{24,16},{32,40},{40,32},{48,56},{56,48},{64,72... | collective-permute-start | bytes 49160 | tf_op jit(solution)/shard_map/ppermute | solution.py:564
  74.0 10.9 %copy-start.3 = (bf16[384,384]{1,0:T(8,128)(2,1)S(1)}, bf16[384,384]{1,0:T(8,128)(2,1)}, u32[]{:S(2)}) copy-start(bf16[384,384]{1,0:T(8,128)(2,1)} %constant.14.clone.third) | copy-start | bytes 884740
  74.0 10.9 %copy-start.4 = (bf16[384,384]{1,0:T(8,128)(2,1)S(1)}, bf16[384,384]{1,0:T(8,128)(2,1)}, u32[]{:S(2)}) copy-start(bf16[384,384]{1,0:T(8,128)(2,1)} %constant.13.clone.second) | copy-start | bytes 884740

commit v9 on v8

--- a/solution.py
+++ b/solution.py
@@ -343,7 +343,7 @@
     return 0.5 * total
 
 
-def presmooth(place, source, wide_p, far, near, far_p, near_p, finest, right, packed_one, packed_two, p, s, q, f1, a1, b1):
+def presmooth(place, source, wide_p, far, near, near_p, far_p, finest, right, packed_one, packed_two, p, s, q, f1, a1, b1):
     odd = place[1] % 2
     p[:, 0:B, :] = wide_p[...]
     s[1 : PX - 1, 0:B, :] = source[...]
@@ -603,7 +603,7 @@
         [shape(22, 24, 128), shape(20, 24, 128), shape(2, B, 128), shape(gx, 4, 128)],
         [SMEM] + [VMEM] * 6,
         [(PX, 32, 128)] * 3 + [(12, 32, 128)] * 3,
-    )(place, source, wide_p, far, near, far_p, near_p)
+    )(place, source, wide_p, far, near, near_p, far_p)
     near, far = exchange(packed_one, packed_one, "gx")
     blocks = lax.all_to_all(packed_two, "gx", 0, 0, tiled=True)
     strips, window = call(

time: 89.5 us -> 90.3 us (level)
  starting transfers between devices: 57.7 us -> 59.1 us
    ppermute x5, waiting for transfers between devices: 3.47 us -> 5.06 us  [exchange(): return (lax.ppermute(near_block, axis, near), far_block)]
    ppermute x5, waiting for transfers between devices: 1.41 us -> 0.05 us  [exchange(): far_block = lax.ppermute(far_block, axis, far)]
    ppermute x5, starting transfers between devices: 24.7 us -> 25.9 us  [exchange(): return (lax.ppermute(near_block, axis, near), far_block)]
  transfers between devices with their start and end apart: 11 -> 11, of which waited for: 5 -> 4; matrix products, arithmetic and copies ran while one was open for 0% -> 0% of each run, Pallas kernels for 4% -> 4%
where the time goes in v9:
time: 90.3 us; the launch traced here: 89.8 us
  starting transfers between devices  59.1 us (65%)
  Pallas kernels  12.8 us (14%)
  blocking collectives  10 us (11%)
  waiting for transfers between devices  6.92 us (8%)
    ppermute x5, starting transfers between devices, exchange(): return (lax.ppermute(near_block, axis, near), far_block)  25.9 us
    ppermute x5, starting transfers between devices, exchange(): far_block = lax.ppermute(far_block, axis, far)  20.8 us
    all_to_all x1, starting transfers between devices, per_device(): blocks = lax.all_to_all(packed_two, 'gx', 0, 0, tiled=True)  12.4 us
    all_to_all x1, blocking collectives, per_device(): strips = lax.all_to_all(strips, 'gy', 0, 0, tiled=True)  10 us
    ppermute x5, waiting for transfers between devices, exchange(): return (lax.ppermute(near_block, axis, near), far_block)  5.06 us
    pallas_call x1, Pallas kernels, per_device(): call(finish, [shape(3, B, B, 128), shape(B, B, 128)], [SMEM] + [VMEM] * 7...  4.08 us
    pallas_call x1, Pallas kernels, per_device(): call(advance, [shape(3, B, B, 128), shape(PX - 2, B, 128), shape(N_S, 128...  3.18 us
    pallas_call x1, Pallas kernels, per_device(): call(presmooth, [shape(22, 24, 128), shape(20, 24, 128), shape(2, B, 128)...  2.74 us
  transfers between devices with their start and end apart: 11, of which 4 were waited for; matrix products, arithmetic and copies ran while one was open for 0% of the time, Pallas kernels for 4%

profile of v9, /device:TPU:1, one launch (start us, length us, event | category | flops | bytes accessed | tf_op | source)
XLA Modules:
  0.0 89.8 jit_solution(14959289861479686199)
XLA Ops:
  0.6 0.0 copy-start.2
  0.6 0.0 copy-start.1
  0.6 0.0 copy-start
  0.7 1.3 %shard_map.86 = (f32[41,16,128]{2,1,0:T(8,128)S(1)}, f32[41,16,128]{2,1,0:T(8,128)S(1)}) custom-call(f32[16]{0:T(128)} %drag_table.1, s32[16,16]{1,0:T(8,128)} %land.3, f32[3,16,16,128]{3,2,1,0:T(8,128)} %velocity.3, f32[16,16,128]{2,1,0:T(8,128)} %pressure.3, s32[16,16,128]{2,1,0:T(8,128)} %turbine.3), custom_call_target="tpu_custom_call" | custom-call | tf_op jit(solution)/shard_map/pallas_call | solution.py:572
  2.0 4.6 %collective-permute-start = (f32[41,16,128]{2,1,0:T(8,128)S(1)}, f32[41,16,128]{2,1,0:T(8,128)S(1)}, u32[]{:S(2)}, u32[]{:S(2)}) collective-permute-start(f32[41,16,128]{2,1,0:T(8,128)S(1)} %get-tuple-element.21), channel_id=1, source_target_pairs={{0,504},{8,16},{16,8},{24,32},{32,24},{40,48},{48,40},{56,64},{64,... | collective-permute-start | bytes 1007624 | tf_op jit(solution)/shard_map/ppermute | solution.py:563
  6.6 12.1 %collective-permute-start.1 = (f32[41,16,128]{2,1,0:T(8,128)S(1)}, f32[41,16,128]{2,1,0:T(8,128)S(1)}, u32[]{:S(2)}, u32[]{:S(2)}) collective-permute-start(f32[41,16,128]{2,1,0:T(8,128)S(1)} %get-tuple-element.22), channel_id=1, source_target_pairs={{0,8},{8,0},{16,24},{24,16},{32,40},{40,32},{48,56},{56,48},{64,72... | collective-permute-start | bytes 1007624 | tf_op jit(solution)/shard_map/ppermute | solution.py:564
  18.7 0.0 copy-start.5
  18.7 0.0 copy-start.6
  18.7 0.1 pad_add_fusion.place.refs_0_
  18.8 0.0 collective-permute-done.far
  18.8 1.1 %collective-permute-done.1.near = f32[41,16,128]{2,1,0:T(8,128)S(1)} collective-permute-done((f32[41,16,128]{2,1,0:T(8,128)S(1)}, f32[41,16,128]{2,1,0:T(8,128)S(1)}, u32[]{:S(2)}, u32[]{:S(2)}) %collective-permute-start.1) | collective-permute-done | bytes 335904 | tf_op jit(solution)/shard_map/ppermute | solution.py:564
  20.0 0.0 copy-done.2
  20.0 0.0 copy-done.1
  20.0 0.0 copy-done
  20.0 0.0 copy-done.5
  20.0 0.0 copy-done.6
  20.0 0.8 shard_map.87
  20.8 5.3 %collective-permute-start.2 = (f32[8,40,128]{2,1,0:T(8,128)S(1)}, f32[8,40,128]{2,1,0:T(8,128)S(1)}, u32[]{:S(2)}, u32[]{:S(2)}) collective-permute-start(f32[8,40,128]{2,1,0:T(8,128)S(1)} %get-tuple-element.25), channel_id=1, source_target_pairs={{0,7},{1,2},{2,1},{3,4},{4,3},{5,6},{6,5},{7,0},{8,15},{9,10},{10,... | collective-permute-start | bytes 491528 | tf_op jit(solution)/shard_map/ppermute | solution.py:563
  26.1 1.9 %collective-permute-start.3 = (f32[8,40,128]{2,1,0:T(8,128)S(1)}, f32[8,40,128]{2,1,0:T(8,128)S(1)}, u32[]{:S(2)}, u32[]{:S(2)}) collective-permute-start(f32[8,40,128]{2,1,0:T(8,128)S(1)} %get-tuple-element.26), channel_id=1, source_target_pairs={{0,1},{1,0},{2,3},{3,2},{4,5},{5,4},{6,7},{7,6},{8,9},{9,8},{10,11... | collective-permute-start | bytes 491528 | tf_op jit(solution)/shard_map/ppermute | solution.py:564
  28.1 3.4 %collective-permute-start.6 = (f32[48,4,128]{2,1,0:T(4,128)S(1)}, f32[48,4,128]{2,1,0:T(4,128)S(1)}, u32[]{:S(2)}, u32[]{:S(2)}) collective-permute-start(f32[48,4,128]{2,1,0:T(4,128)S(1)} %get-tuple-element.31), channel_id=1, source_target_pairs={{0,1},{1,0},{2,3},{3,2},{4,5},{5,4},{6,7},{7,6},{8,9},{9,8},{10,11... | collective-permute-start | bytes 294920 | tf_op jit(solution)/shard_map/ppermute | solution.py:564
  31.4 2.2 %collective-permute-start.7 = (f32[48,4,128]{2,1,0:T(4,128)S(1)}, f32[48,4,128]{2,1,0:T(4,128)S(1)}, u32[]{:S(2)}, u32[]{:S(2)}) collective-permute-start(f32[48,4,128]{2,1,0:T(4,128)S(1)} %get-tuple-element.32), channel_id=1, source_target_pairs={{0,7},{1,2},{2,1},{3,4},{4,3},{5,6},{6,5},{7,0},{8,15},{9,10},{10,... | collective-permute-start | bytes 294920 | tf_op jit(solution)/shard_map/ppermute | solution.py:563
  33.6 0.0 collective-permute-done.2.far
  33.6 0.0 collective-permute-done.3.near
  33.6 3.2 %shard_map.88 = (f32[3,16,16,128]{3,2,1,0:T(8,128)S(1)}, f32[28,16,128]{2,1,0:T(8,128)S(1)}, f32[144,128]{1,0:T(8,128)S(1)}, f32[144,128]{1,0:T(8,128)S(1)}) custom-call(s32[2]{0:T(128)S(1)} %pad_add_fusion.place.refs_0_, f32[3,34,16,128]{3,2,1,0:T(8,128)S(1)} %get-tuple-element.23.wide_v, f32[30,16,128]{2,1,0:T(8,128)S(1)} %get-tuple-element.24.wide_d, ...), custom_call_target="tpu_custom_call" | custom-call | tf_op jit(solution)/shard_map/pallas_call | solution.py:594
  36.8 5.2 %collective-permute-start.4 = (f32[144,128]{1,0:T(8,128)S(1)}, f32[144,128]{1,0:T(8,128)S(1)}, u32[]{:S(2)}, u32[]{:S(2)}) collective-permute-start(f32[144,128]{1,0:T(8,128)S(1)} %get-tuple-element.29), channel_id=1, source_target_pairs={{0,7},{1,2},{2,1},{3,4},{4,3},{5,6},{6,5},{7,0},{8,15},{9,10},{10,... | collective-permute-start | bytes 221192 | tf_op jit(solution)/shard_map/ppermute | solution.py:563
  42.1 1.9 %collective-permute-start.5 = (f32[144,128]{1,0:T(8,128)S(1)}, f32[144,128]{1,0:T(8,128)S(1)}, u32[]{:S(2)}, u32[]{:S(2)}) collective-permute-start(f32[144,128]{1,0:T(8,128)S(1)} %get-tuple-element.30), channel_id=1, source_target_pairs={{0,1},{1,0},{2,3},{3,2},{4,5},{5,4},{6,7},{7,6},{8,9},{9,8},{10,11... | collective-permute-start | bytes 221192 | tf_op jit(solution)/shard_map/ppermute | solution.py:564
  44.0 0.0 collective-permute-done.6.near_p
  44.0 0.0 collective-permute-done.7.far_p
  44.0 0.0 collective-permute-done.4.far
  44.0 3.1 %collective-permute-done.5.near = f32[144,128]{1,0:T(8,128)S(1)} collective-permute-done((f32[144,128]{1,0:T(8,128)S(1)}, f32[144,128]{1,0:T(8,128)S(1)}, u32[]{:S(2)}, u32[]{:S(2)}) %collective-permute-start.5) | collective-permute-done | bytes 73760 | tf_op jit(solution)/shard_map/ppermute | solution.py:564
  47.1 2.7 %shard_map.89 = (f32[22,24,128]{2,1,0:T(8,128)S(1)}, f32[20,24,128]{2,1,0:T(8,128)S(1)}, f32[2,16,128]{2,1,0:T(8,128)S(1)}, f32[64,4,128]{2,1,0:T(4,128)}) custom-call(s32[2]{0:T(128)S(1)} %pad_add_fusion.place.refs_0_, f32[28,16,128]{2,1,0:T(8,128)S(1)} %get-tuple-element.27.source, f32[30,16,128]{2,1,0:T(8,128)S(1)} %get-tuple-element.28.wide_p, ...), custom_call_target="tpu_custom_call" | custom-call | tf_op jit(solution)/shard_map/pallas_call | solution.py:601
  49.9 12.4 %all-to-all-start = ((f32[64,4,128]{2,1,0:T(4,128)}), f32[64,4,128]{2,1,0:T(4,128)S(1)}, u32[]{:S(2)}, u32[]{:S(2)}) async-start(f32[64,4,128]{2,1,0:T(4,128)} %get-tuple-element.33), calls=%async_computation | async-start | bytes 262144 | tf_op jit(solution)/shard_map/all_to_all | solution.py:608
  62.3 3.5 %collective-permute-start.9 = (f32[2,16,128]{2,1,0:T(8,128)S(1)}, f32[2,16,128]{2,1,0:T(8,128)S(1)}, u32[]{:S(2)}, u32[]{:S(2)}) collective-permute-start(f32[2,16,128]{2,1,0:T(8,128)S(1)} %get-tuple-element.34.refs_2_), channel_id=1, source_target_pairs={{0,504},{8,16},{16,8},{24,32},{32,24},{40,48},{48,40},{56,64},{64,... | collective-permute-start | bytes 49160 | tf_op jit(solution)/shard_map/ppermute | solution.py:563
  65.8 6.6 %collective-permute-start.8 = (f32[2,16,128]{2,1,0:T(8,128)S(1)}, f32[2,16,128]{2,1,0:T(8,128)S(1)}, u32[]{:S(2)}, u32[]{:S(2)}) collective-permute-start(f32[2,16,128]{2,1,0:T(8,128)S(1)} %get-tuple-element.34.refs_2_), channel_id=1, source_target_pairs={{0,8},{8,0},{16,24},{24,16},{32,40},{40,32},{48,56},{56,48},{64,72... | collective-permute-start | bytes 49160 | tf_op jit(solution)/shard_map/ppermute | solution.py:564
  72.4 0.0 collective-permute-done.9.refs_4_
  72.4 0.8 collective-permute-done.8.refs_3_
  73.2 1.8 %all-to-all-done.refs_1_ = f32[64,4,128]{2,1,0:T(4,128)S(1)} async-done(((f32[64,4,128]{2,1,0:T(4,128)}), f32[64,4,128]{2,1,0:T(4,128)S(1)}, u32[]{:S(2)}, u32[]{:S(2)}) %all-to-all-start) | async-done | bytes 131104 | tf_op jit(solution)/shard_map/all_to_all | solution.py:608
  75.0 0.6 shard_map.90
  75.7 0.0 copy-start.3
  75.7 0.0 copy-start.4
  75.7 10.0 %all_to_all.10.strips = f32[8,19,4,128]{3,2,1,0:T(4,128)S(1)} all-to-all(f32[8,19,4,128]{3,2,1,0:T(4,128)S(1)} %get-tuple-element.35), channel_id=1, replica_groups=mesh['gx'=64,'gy'=8] {'gy'}, dimensions={0} | all-to-all | bytes 622592 | tf_op jit(solution)/shard_map/all_to_all | solution.py:614
  85.7 0.0 copy-done.3
  85.7 0.0 copy-done.4
  85.7 4.1 %shard_map.91 = (f32[3,16,16,128]{3,2,1,0:T(8,128)}, f32[16,16,128]{2,1,0:T(8,128)}) custom-call(s32[2]{0:T(128)S(1)} %pad_add_fusion.place.refs_0_, f32[8,19,4,128]{3,2,1,0:T(4,128)S(1)} %all_to_all.10.strips, f32[6,16,128]{2,1,0:T(8,128)S(1)} %get-tuple-element.36.window, f32[22,24,128]{2,1,0:T(8,128)S(1)} %get-tuple-element.37.finest, ...), custom_call_target="tpu_custom_call" | custom-call | tf_op jit(solution)/shard_map/pallas_call | solution.py:615
Async XLA Ops:
  0.6 19.3 %copy-start.2 = (s32[16,16,128]{2,1,0:T(8,128)S(1)}, s32[16,16,128]{2,1,0:T(8,128)}, u32[]{:S(2)}) copy-start(s32[16,16,128]{2,1,0:T(8,128)} %turbine.3) | copy-start | bytes 393220
  0.6 19.3 %copy-start.1 = (f32[16,16,128]{2,1,0:T(8,128)S(1)}, f32[16,16,128]{2,1,0:T(8,128)}, u32[]{:S(2)}) copy-start(f32[16,16,128]{2,1,0:T(8,128)} %pressure.3) | copy-start | bytes 393220
  0.6 19.3 %copy-start = (f32[3,16,16,128]{3,2,1,0:T(8,128)S(1)}, f32[3,16,16,128]{3,2,1,0:T(8,128)}, u32[]{:S(2)}) copy-start(f32[3,16,16,128]{3,2,1,0:T(8,128)} %velocity.3) | copy-start | bytes 1179652
  2.0 16.8 %collective-permute-start = (f32[41,16,128]{2,1,0:T(8,128)S(1)}, f32[41,16,128]{2,1,0:T(8,128)S(1)}, u32[]{:S(2)}, u32[]{:S(2)}) collective-permute-start(f32[41,16,128]{2,1,0:T(8,128)S(1)} %get-tuple-element.21), channel_id=1, source_target_pairs={{0,504},{8,16},{16,8},{24,32},{32,24},{40,48},{48,40},{56,64},{64,... | collective-permute-start | bytes 1007624 | tf_op jit(solution)/shard_map/ppermute | solution.py:563
  6.6 13.4 %collective-permute-start.1 = (f32[41,16,128]{2,1,0:T(8,128)S(1)}, f32[41,16,128]{2,1,0:T(8,128)S(1)}, u32[]{:S(2)}, u32[]{:S(2)}) collective-permute-start(f32[41,16,128]{2,1,0:T(8,128)S(1)} %get-tuple-element.22), channel_id=1, source_target_pairs={{0,8},{8,0},{16,24},{24,16},{32,40},{40,32},{48,56},{56,48},{64,72... | collective-permute-start | bytes 1007624 | tf_op jit(solution)/shard_map/ppermute | solution.py:564
  18.7 1.3 %copy-start.5 = (s32[16,16]{1,0:T(8,128)S(1)}, s32[16,16]{1,0:T(8,128)}, u32[]{:S(2)}) copy-start(s32[16,16]{1,0:T(8,128)} %land.3) | copy-start | bytes 3076
  18.7 1.2 %copy-start.6 = (f32[16]{0:T(128)S(1)}, f32[16]{0:T(128)}, u32[]{:S(2)}) copy-start(f32[16]{0:T(128)} %drag_table.1) | copy-start | bytes 196
  20.8 12.8 %collective-permute-start.2 = (f32[8,40,128]{2,1,0:T(8,128)S(1)}, f32[8,40,128]{2,1,0:T(8,128)S(1)}, u32[]{:S(2)}, u32[]{:S(2)}) collective-permute-start(f32[8,40,128]{2,1,0:T(8,128)S(1)} %get-tuple-element.25), channel_id=1, source_target_pairs={{0,7},{1,2},{2,1},{3,4},{4,3},{5,6},{6,5},{7,0},{8,15},{9,10},{10,... | collective-permute-start | bytes 491528 | tf_op jit(solution)/shard_map/ppermute | solution.py:563
  26.1 7.5 %collective-permute-start.3 = (f32[8,40,128]{2,1,0:T(8,128)S(1)}, f32[8,40,128]{2,1,0:T(8,128)S(1)}, u32[]{:S(2)}, u32[]{:S(2)}) collective-permute-start(f32[8,40,128]{2,1,0:T(8,128)S(1)} %get-tuple-element.26), channel_id=1, source_target_pairs={{0,1},{1,0},{2,3},{3,2},{4,5},{5,4},{6,7},{7,6},{8,9},{9,8},{10,11... | collective-permute-start | bytes 491528 | tf_op jit(solution)/shard_map/ppermute | solution.py:564
  28.1 15.9 %collective-permute-start.6 = (f32[48,4,128]{2,1,0:T(4,128)S(1)}, f32[48,4,128]{2,1,0:T(4,128)S(1)}, u32[]{:S(2)}, u32[]{:S(2)}) collective-permute-start(f32[48,4,128]{2,1,0:T(4,128)S(1)} %get-tuple-element.31), channel_id=1, source_target_pairs={{0,1},{1,0},{2,3},{3,2},{4,5},{5,4},{6,7},{7,6},{8,9},{9,8},{10,11... | collective-permute-start | bytes 294920 | tf_op jit(solution)/shard_map/ppermute | solution.py:564
  31.4 12.6 %collective-permute-start.7 = (f32[48,4,128]{2,1,0:T(4,128)S(1)}, f32[48,4,128]{2,1,0:T(4,128)S(1)}, u32[]{:S(2)}, u32[]{:S(2)}) collective-permute-start(f32[48,4,128]{2,1,0:T(4,128)S(1)} %get-tuple-element.32), channel_id=1, source_target_pairs={{0,7},{1,2},{2,1},{3,4},{4,3},{5,6},{6,5},{7,0},{8,15},{9,10},{10,... | collective-permute-start | bytes 294920 | tf_op jit(solution)/shard_map/ppermute | solution.py:563
  36.8 7.2 %collective-permute-start.4 = (f32[144,128]{1,0:T(8,128)S(1)}, f32[144,128]{1,0:T(8,128)S(1)}, u32[]{:S(2)}, u32[]{:S(2)}) collective-permute-start(f32[144,128]{1,0:T(8,128)S(1)} %get-tuple-element.29), channel_id=1, source_target_pairs={{0,7},{1,2},{2,1},{3,4},{4,3},{5,6},{6,5},{7,0},{8,15},{9,10},{10,... | collective-permute-start | bytes 221192 | tf_op jit(solution)/shard_map/ppermute | solution.py:563
  42.1 5.1 %collective-permute-start.5 = (f32[144,128]{1,0:T(8,128)S(1)}, f32[144,128]{1,0:T(8,128)S(1)}, u32[]{:S(2)}, u32[]{:S(2)}) collective-permute-start(f32[144,128]{1,0:T(8,128)S(1)} %get-tuple-element.30), channel_id=1, source_target_pairs={{0,1},{1,0},{2,3},{3,2},{4,5},{5,4},{6,7},{7,6},{8,9},{9,8},{10,11... | collective-permute-start | bytes 221192 | tf_op jit(solution)/shard_map/ppermute | solution.py:564
  49.9 25.2 %all-to-all-start = ((f32[64,4,128]{2,1,0:T(4,128)}), f32[64,4,128]{2,1,0:T(4,128)S(1)}, u32[]{:S(2)}, u32[]{:S(2)}) async-start(f32[64,4,128]{2,1,0:T(4,128)} %get-tuple-element.33), calls=%async_computation | async-start | bytes 262144 | tf_op jit(solution)/shard_map/all_to_all | solution.py:608
  62.3 10.1 %collective-permute-start.9 = (f32[2,16,128]{2,1,0:T(8,128)S(1)}, f32[2,16,128]{2,1,0:T(8,128)S(1)}, u32[]{:S(2)}, u32[]{:S(2)}) collective-permute-start(f32[2,16,128]{2,1,0:T(8,128)S(1)} %get-tuple-element.34.refs_2_), channel_id=1, source_target_pairs={{0,504},{8,16},{16,8},{24,32},{32,24},{40,48},{48,40},{56,64},{64,... | collective-permute-start | bytes 49160 | tf_op jit(solution)/shard_map/ppermute | solution.py:563
  65.8 7.4 %collective-permute-start.8 = (f32[2,16,128]{2,1,0:T(8,128)S(1)}, f32[2,16,128]{2,1,0:T(8,128)S(1)}, u32[]{:S(2)}, u32[]{:S(2)}) collective-permute-start(f32[2,16,128]{2,1,0:T(8,128)S(1)} %get-tuple-element.34.refs_2_), channel_id=1, source_target_pairs={{0,8},{8,0},{16,24},{24,16},{32,40},{40,32},{48,56},{56,48},{64,72... | collective-permute-start | bytes 49160 | tf_op jit(solution)/shard_map/ppermute | solution.py:564
  75.7 10.0 %copy-start.3 = (bf16[384,384]{1,0:T(8,128)(2,1)S(1)}, bf16[384,384]{1,0:T(8,128)(2,1)}, u32[]{:S(2)}) copy-start(bf16[384,384]{1,0:T(8,128)(2,1)} %constant.14.clone.third) | copy-start | bytes 884740
  75.7 10.0 %copy-start.4 = (bf16[384,384]{1,0:T(8,128)(2,1)S(1)}, bf16[384,384]{1,0:T(8,128)(2,1)}, u32[]{:S(2)}) copy-start(bf16[384,384]{1,0:T(8,128)(2,1)} %constant.13.clone.second) | copy-start | bytes 884740
